TPU v7x, 256 devices: a whole 4x4x8 slice. The times are simulated.
256 devices in a mesh: row: 8 (over z_hi, x), col: 32 (over z_lo, y, core).
Axes of the slice: x: 4, y: 4, z: 8 (z_hi: 2, z_lo: 4; z = z_hi * 4 + z_lo), core: 2. Of those that a mesh axis runs over, the one named last changes fastest.
Arguments:
- features: bfloat16 [384, 512], P('col'), may hold values from -6 to 6
- weights: bfloat16 [1507328, 512], P(('row', 'col')), may hold values from -0.25 to 0.25
- label_bias: float32 [1507328], P(('row', 'col')), may hold values from -11 to -7
- pos_ids: int32 [384, 32], P('col'), may hold values from 0 to 1507327, as said below
- pos_count: int32 [384], P('col'), may hold values from 1 to 32
Outputs:
- weight_grad: bfloat16 [1507328, 512], P(('row', 'col'))
- bias_grad: float32 [1507328], P(('row', 'col'))
- feature_grad: bfloat16 [384, 512], P('col', 'row')
Inputs may be any that keep to these rules, and one draw needn't show every extreme that they name: `pos_ids`: slots at or beyond an example's count are ignored; an id may repeat within one list.
All inputs are finite; a program needn't handle non-finite values.
Results may differ from a plain program's by a relative error of at most 0.0046.
Values may be sent and summed in bfloat16 or wider, within the bound.
No kernel may reach another device: no remote copies, remote signals or barrier semaphores. Data moves between devices by JAX's collectives and lax.ppermute only.
A program may use at most 128 MiB of HBM per device.

v0:
```python
import jax
import jax.numpy as jnp
from jax import lax
from jax.sharding import PartitionSpec as P


def block_grad(feat_rows, w_block, b_block, label_ids, live_slot, row_index, offset):
    logits = lax.dot_general(
        feat_rows, w_block, (((1,), (1,)), ((), ())), preferred_element_type=jnp.float32
    )
    logits = logits + b_block[None, :]
    lab_width = w_block.shape[0]
    local_ids = label_ids - offset
    inside = live_slot & (local_ids >= 0) & (local_ids < lab_width)
    target = jnp.where(inside, local_ids, lab_width)
    hit_table = (
        jnp.zeros((feat_rows.shape[0], lab_width), jnp.float32)
        .at[row_index, target]
        .max(1.0, mode="drop")
    )
    return (jax.nn.sigmoid(logits) - hit_table).astype(jnp.bfloat16)


def local(features, weights, label_bias, pos_ids, pos_count):
    lab_width = weights.shape[0]
    offset = (lax.axis_index("row") * lax.axis_size("col") + lax.axis_index("col")) * lab_width
    ids_all, count_all = (
        lax.all_gather(pos_ids, "col", axis=0, tiled=True),
        lax.all_gather(pos_count, "col", axis=0, tiled=True),
    )
    ex_total = ids_all.shape[0]
    pos_slots = ids_all.shape[1]
    slot_index = jnp.arange(pos_slots, dtype=jnp.int32)
    live_all = slot_index[None, :] < count_all[:, None]
    gathered = lax.all_gather(features, "col", axis=0, tiled=True)
    row_index = jnp.broadcast_to(
        jnp.arange(ex_total, dtype=jnp.int32)[:, None], (ex_total, pos_slots)
    )
    label_grad = block_grad(gathered, weights, label_bias, ids_all, live_all, row_index, offset)
    weight_grad = lax.dot_general(
        label_grad, gathered, (((0,), (0,)), ((), ())), preferred_element_type=jnp.float32
    ).astype(jnp.bfloat16)
    bias_grad = jnp.sum(label_grad, axis=0, dtype=jnp.float32)
    dx_full = jnp.dot(label_grad, weights, preferred_element_type=jnp.float32)
    dx_part = lax.psum_scatter(dx_full, "col", scatter_dimension=0, tiled=True)
    summed = lax.psum_scatter(dx_part, "row", scatter_dimension=1, tiled=True)
    return (weight_grad, bias_grad, summed.astype(jnp.bfloat16))


def solution(mesh):
    return jax.shard_map(
        local,
        mesh=mesh,
        in_specs=(
            P("col", None),
            P(("row", "col"), None),
            P(("row", "col")),
            P("col", None),
            P("col"),
        ),
        out_specs=(P(("row", "col"), None), P(("row", "col")), P("col", "row")),
        check_vma=False,
    )
```

profile of v0, /device:TPU:8, one launch (start us, length us, event | category | flops | bytes accessed | tf_op | source)
XLA Modules:
  0.0 396.5 jit_solution(15127961683875132051)
XLA Ops:
  7.2 40.8 %all-gather.1 = s32[32,12,32]{2,1,0:T(8,128)S(1)} all-gather(s32[1,12,32]{2,1,0:T(8,128)} %bitcast.19), channel_id=1, replica_groups=mesh['row'=8,'col'=32] {'col'}, dimensions={0}, use_global_device_ids=true | all-gather | bytes 50688 | tf_op jit(solution)/shard_map/all_gather | solution.py:28
  48.1 1.3 fusion.6
  50.9 13.6 %all-reduce = s32[384]{0:T(512)S(1)} all-reduce(s32[384]{0:T(512)S(1)} %dynamic-update-slice), channel_id=1, replica_groups=mesh['row'=8,'col'=32] {'col'}, use_global_device_ids=true, to_apply=%add | all-reduce | flops 384 | bytes 3072
  66.6 68.5 %scatter_custom_fusion = f32[2260992]{0:T(1024)} fusion(s32[12288]{0:T(1024)S(1)} %reshape.24, f32[12288]{0:T(1024)S(1)} %broadcast.43, f32[]{:T(128)} %constant.9.clone.1), kind=kCustom, calls=%fused_computation.4 | custom fusion | flops 12288 | bytes 9043972
  135.1 9.9 %reshape.23 = f32[384,5888]{1,0:T(8,128)} reshape(f32[2260992]{0:T(1024)} %scatter_custom_fusion) | data formatting | bytes 18087936 | tf_op jit(solution)/shard_map/scatter-max | solution.py:19
  145.0 41.6 %all-gather = bf16[32,12,512]{2,1,0:T(8,128)(2,1)S(1)} all-gather(bf16[1,12,512]{2,1,0:T(8,128)(2,1)S(1)} %bitcast.18), channel_id=1, replica_groups=mesh['row'=8,'col'=32] {'col'}, dimensions={0}, use_global_device_ids=true | all-gather | bytes 405504 | tf_op jit(solution)/shard_map/all_gather | solution.py:35
  186.7 9.2 %convert_reduce_fusion = (f32[5888]{0:T(1024)}, bf16[384,5888]{1,0:T(8,128)(2,1)S(1)}) fusion(f32[384,5888]{1,0:T(8,128)} %reshape.23, f32[5888]{0:T(1024)S(1)} %copy-done.1, bf16[384,512]{1,0:T(8,128)(2,1)S(1)} %reshape.34, bf16[5888,512]{1,0:T(8,128)(2,1)} %param.6), kind=kOutput, calls=%fused_computation.1 | convolution fusion | flops 2333337856 | bytes 20035584 | tf_op jit(solution)/shard_map/dot_general | solution.py:8
  195.9 2.0 copy-done.2
  197.9 5.2 %fusion.7 = f32[384,512]{1,0:T(8,128)S(1)} fusion(bf16[384,5888]{1,0:T(8,128)(2,1)S(1)} %get-tuple-element.6, bf16[5888,512]{1,0:T(8,128)(2,1)} %param.6), kind=kOutput, calls=%fused_computation.18 | convolution fusion | flops 2315255808 | bytes 11337728 | tf_op jit(solution)/shard_map/dot_general | solution.py:44
  203.1 72.3 %fusion = f32[16,512]{1,0:T(8,128)S(1)} fusion(f32[384,512]{1,0:T(8,128)S(1)} %fusion.7), kind=kCustom, calls=%all-reduce-scatter | all-reduce-scatter fusion | flops 262145 | bytes 820224
  275.4 1.9 collective-permute-start
  277.4 1.9 collective-permute-start.1
  279.3 1.3 collective-permute-start.7
  280.6 1.3 collective-permute-start.2
  281.9 1.3 collective-permute-start.3
  283.2 1.3 collective-permute-start.4
  284.5 15.6 %collective-permute-start.5 = (f32[16,512]{1,0:T(8,128)S(1)}, f32[16,512]{1,0:T(8,128)S(1)}, u32[]{:S(2)}, u32[]{:S(2)}) collective-permute-start(f32[16,512]{1,0:T(8,128)S(1)} %fusion), channel_id=1, source_target_pairs={{0,6},{1,7},{2,8},{3,9},{4,10},{5,11},{6,12},{7,13},{8,14},{9,15},... | collective-permute-start | bytes 98312
  300.2 1.3 collective-permute-start.6
  302.1 0.9 collective-permute-done.6
  303.0 0.9 concatenate.4
  304.0 0.9 copy.11
  304.9 7.5 %convolution_convert_fusion = bf16[5888,512]{1,0:T(8,128)(2,1)} fusion(bf16[384,5888]{1,0:T(8,128)(2,1)} %copy-done.2, bf16[384,512]{1,0:T(8,128)(2,1)S(1)} %reshape.34), kind=kOutput, calls=%fused_computation.3 | convolution fusion | flops 2318270464 | bytes 10944512 | tf_op jit(solution)/shard_map/dot_general | solution.py:40
  312.4 75.9 %reduce-scatter.6.cloned.1.call-done = f32[64,12]{1,0:T(8,128)} async-done(((f32[512,12]{1,0:T(8,128)}), f32[64,12]{1,0:T(8,128)}) %reduce-scatter.6.cloned.1.call-update) | async-done | bytes 3088
  388.2 1.4 copy.12
  (30 shorter events, 3.0 us)
Async XLA Ops:
  7.2 381.1 %reduce-scatter.6.cloned.1.call-start = ((), (), s32[]{:S(2)}) async-start(), calls=%async_computation.1 | async-start | bytes 294912
  135.1 9.9 %copy-start = (bf16[12,512]{1,0:T(8,128)(2,1)S(1)}, bf16[12,512]{1,0:T(8,128)(2,1)}, u32[]{:S(2)}) copy-start(bf16[12,512]{1,0:T(8,128)(2,1)} %param.5) | copy-start | bytes 36868
  135.1 51.6 %copy-start.1 = (f32[5888]{0:T(1024)S(1)}, f32[5888]{0:T(1024)}, u32[]{:S(2)}) copy-start(f32[5888]{0:T(1024)} %param.7) | copy-start | bytes 70660
  195.9 2.1 copy-start.2
  275.4 9.1 %collective-permute-start = (f32[16,512]{1,0:T(8,128)S(1)}, f32[16,512]{1,0:T(8,128)S(1)}, u32[]{:S(2)}, u32[]{:S(2)}) collective-permute-start(f32[16,512]{1,0:T(8,128)S(1)} %fusion), channel_id=1, source_target_pairs={{0,1},{1,2},{2,3},{3,4},{4,5},{5,6},{6,7},{7,8},{8,9},{9,10},{10,1... | collective-permute-start | bytes 98312
  277.4 22.8 %collective-permute-start.1 = (f32[16,512]{1,0:T(8,128)S(1)}, f32[16,512]{1,0:T(8,128)S(1)}, u32[]{:S(2)}, u32[]{:S(2)}) collective-permute-start(f32[16,512]{1,0:T(8,128)S(1)} %fusion), channel_id=1, source_target_pairs={{0,2},{1,3},{2,4},{3,5},{4,6},{5,7},{6,8},{7,9},{8,10},{9,11},{10,... | collective-permute-start | bytes 98312
  279.3 3.9 collective-permute-start.7
  280.6 21.5 %collective-permute-start.2 = (f32[16,512]{1,0:T(8,128)S(1)}, f32[16,512]{1,0:T(8,128)S(1)}, u32[]{:S(2)}, u32[]{:S(2)}) collective-permute-start(f32[16,512]{1,0:T(8,128)S(1)} %fusion), channel_id=1, source_target_pairs={{0,3},{1,4},{2,5},{3,6},{4,7},{5,8},{6,9},{7,10},{8,11},{9,12},{10... | collective-permute-start | bytes 98312
  281.9 20.2 %collective-permute-start.3 = (f32[16,512]{1,0:T(8,128)S(1)}, f32[16,512]{1,0:T(8,128)S(1)}, u32[]{:S(2)}, u32[]{:S(2)}) collective-permute-start(f32[16,512]{1,0:T(8,128)S(1)} %fusion), channel_id=1, source_target_pairs={{0,4},{1,5},{2,6},{3,7},{4,8},{5,9},{6,10},{7,11},{8,12},{9,13},{1... | collective-permute-start | bytes 98312
  283.2 18.9 %collective-permute-start.4 = (f32[16,512]{1,0:T(8,128)S(1)}, f32[16,512]{1,0:T(8,128)S(1)}, u32[]{:S(2)}, u32[]{:S(2)}) collective-permute-start(f32[16,512]{1,0:T(8,128)S(1)} %fusion), channel_id=1, source_target_pairs={{0,5},{1,6},{2,7},{3,8},{4,9},{5,10},{6,11},{7,12},{8,13},{9,14},{... | collective-permute-start | bytes 98312
  284.5 17.6 %collective-permute-start.5 = (f32[16,512]{1,0:T(8,128)S(1)}, f32[16,512]{1,0:T(8,128)S(1)}, u32[]{:S(2)}, u32[]{:S(2)}) collective-permute-start(f32[16,512]{1,0:T(8,128)S(1)} %fusion), channel_id=1, source_target_pairs={{0,6},{1,7},{2,8},{3,9},{4,10},{5,11},{6,12},{7,13},{8,14},{9,15},... | collective-permute-start | bytes 98312
  300.2 2.9 collective-permute-start.6
Sparse Core Ops, SparseCore 0:
  305.0 83.1 reduce-scatter.5
where the time goes:
time: 397 us
  blocking collectives  168 us (42%)
  waiting for transfers between devices  76.8 us (19%)
  other arithmetic  70.1 us (18%)
  starting transfers between devices  26 us (7%)
  matrix products  21.9 us (6%)
  local copies, waits for them, and re-layouts  17.9 us (5%)
  between operations  15.6 us (4%)
    unnamed x2, blocking collectives  85.9 us
    unnamed x10, waiting for transfers between devices  76.8 us
    unnamed x4, other arithmetic  70 us
    all_gather x1, blocking collectives, local(): gathered = lax.all_gather(features, 'col', axis=0, tiled=True)  41.6 us
    all_gather x1, blocking collectives, local(): lax.all_gather(pos_ids, 'col', axis=0, tiled=True)  40.8 us
    unnamed x9, starting transfers between devices  26 us
    another operation x1, local copies, waits for them, and re-layouts, block_grad(): hit_table = jnp.zeros((feat_rows.shape[0], lab_width), jnp.float32).at[ro...  9.9 us
    dot_general x1, matrix products, block_grad(): lax.dot_general(feat_rows, w_block, (((1,), (1,)), ((), ())), preferred_e...  9.23 us
  transfers between devices with their start and end apart: 9, of which 2 were waited for; matrix products, arithmetic and copies ran while one was open for 2% of the time, Pallas kernels for 0%

commit v1 on v0

v1 whole, which is shorter than its diff:
```python
import functools

import jax
import jax.numpy as jnp
from jax import lax
from jax.experimental import pallas as pl
from jax.experimental.pallas import tpu as pltpu
from jax.sharding import Mesh, PartitionSpec as P

BF = jnp.bfloat16
F32 = jnp.float32
TILE = 256
KEY = 8192.0


def xor_permute(x, axis, size, bit):
    return lax.ppermute(x, axis, [(i, i ^ bit) for i in range(size)])


def grad_kernel(where_ref, own_ref, other_ref, w_hbm, bias_ref, g_ref, mine_ref, theirs_ref,
                f_scr, w_scr, first_scr, key_scr, dx_scr, sems):
    labels = w_scr.shape[0]
    tiles = labels // TILE
    half = own_ref.shape[0]
    rows = 2 * half
    width = f_scr.shape[1]

    def w_copy(t):
        at = pl.ds(t * TILE, TILE)
        return pltpu.make_async_copy(w_hbm.at[at], w_scr.at[at], sems.at[t])

    for t in range(tiles):
        w_copy(t).start()
    f_scr[0:half] = own_ref[:, 0:width]
    f_scr[half:rows] = other_ref[:, 0:width]

    digit = lax.broadcasted_iota(jnp.int32, (128, 128), 0)
    lane = lax.broadcasted_iota(jnp.int32, (128, 128), 1)
    same = (digit % 32) == (lane % 32)
    power = jnp.where(digit < 32, 1.0, jnp.where(digit < 64, 256.0, jnp.where(digit < 96, 65536.0, 0.0)))
    decode = jnp.where(same, power, 0.0).astype(BF)
    offset = where_ref[1].astype(F32)
    row = lax.broadcasted_iota(jnp.int32, (half, 128), 0).astype(F32)
    for h, ref in enumerate((own_ref, other_ref)):
        at = pl.ds(h * half, half)
        local = jnp.dot(ref[:, width:width + 128], decode, preferred_element_type=F32) - offset
        local = jnp.where((local >= 0.0) & (local < float(labels)), local, -1.0)
        first = jnp.max(local, axis=1, keepdims=True)
        first_scr[at] = jnp.broadcast_to(first, (half, 128))
        more = (local >= 0.0) & (local < first)
        key_scr[at] = jnp.where(more, (row + float(h * half)) * KEY + local, -1.0)
    dx_scr[...] = jnp.zeros_like(dx_scr)

    lanes = lax.broadcasted_iota(jnp.int32, (rows, 128), 1).astype(F32)

    def step(t, carry):
        w_copy(t).wait()
        at = pl.ds(pl.multiple_of(t * TILE, TILE), TILE)
        w = w_scr[at]
        logits = lax.dot_general(f_scr[...], w, (((1,), (1,)), ((), ())), preferred_element_type=F32)
        x = logits + bias_ref[:, at]
        s = 1.0 / (1.0 + jnp.exp(-x))
        base = (t * TILE).astype(F32)
        first = first_scr[...] - base
        hit = jnp.concatenate([lanes == first - 128.0 * k for k in range(TILE // 128)], axis=1)
        g = jnp.where(hit, s - 1.0, s).astype(BF)
        g_ref[:, at] = g
        dx_scr[...] += jnp.dot(g, w, preferred_element_type=F32)
        return carry

    lax.fori_loop(0, tiles, step, 0)

    def more_hits(top):
        return top >= 0.0

    def one_hit(top):
        k = top.astype(jnp.int32)
        b = k // int(KEY)
        l = k - b * int(KEY)
        b16 = pl.ds(pl.multiple_of((b // 16) * 16, 16), 16)
        l128 = pl.ds(pl.multiple_of((l // 128) * 128, 128), 128)
        r = lax.broadcasted_iota(jnp.int32, (16, 128), 0)
        c = lax.broadcasted_iota(jnp.int32, (16, 128), 1)
        spot = (r == b % 16) & (c == l % 128)
        old = g_ref[b16, l128].astype(F32)
        g_ref[b16, l128] = jnp.where(spot, old - 1.0, old).astype(BF)
        l16 = pl.ds(pl.multiple_of((l // 16) * 16, 16), 16)
        r = lax.broadcasted_iota(jnp.int32, (16, width), 0)
        w_row = jnp.sum(jnp.where(r == l % 16, w_scr[l16].astype(F32), 0.0), axis=0, keepdims=True)
        dx_scr[b16] -= jnp.where(r == b % 16, w_row, 0.0)
        keys = key_scr[...]
        keys = jnp.where(keys == top, -1.0, keys)
        key_scr[...] = keys
        return jnp.max(keys)

    lax.while_loop(more_hits, one_hit, jnp.max(key_scr[...]))

    me = where_ref[0]
    low = lax.broadcasted_iota(jnp.int32, (half, 128), 1) < 64
    per = mine_ref.shape[1]
    for h, ref in enumerate((mine_ref, theirs_ref)):
        at = pl.ds(h * half, half)
        for x in range(4):
            k = (x // 2) * 128
            left = dx_scr[at, k:k + 128]
            right = dx_scr[at, 256 + k:256 + k + 128]
            if x % 2 == 0:
                both = jnp.where(low, left, pltpu.roll(right, 64, 1))
            else:
                both = jnp.where(low, pltpu.roll(left, 64, 1), right)
            for j in range(16):
                ref[x * 16 + (me ^ j)] = both[j * per:(j + 1) * per].astype(ref.dtype)


def weight_kernel(g_ref, own_ref, other_ref, wg_ref, bg_ref):
    half = own_ref.shape[0]
    width = wg_ref.shape[1]
    g = g_ref[...]
    tn = (((0,), (0,)), ((), ()))
    acc = lax.dot_general(g[:half], own_ref[:, 0:width], tn, preferred_element_type=F32)
    acc += lax.dot_general(g[half:], other_ref[:, 0:width], tn, preferred_element_type=F32)
    wg_ref[...] = acc.astype(BF)
    bg_ref[...] = jnp.sum(g.astype(F32), axis=0, keepdims=True)


def local(features, weights, label_bias, pos_ids, pos_count):
    labels, width = weights.shape
    per, slots = pos_ids.shape
    half = per * 16
    rows = 2 * half
    slot = jnp.arange(slots, dtype=jnp.int32)
    ids = jnp.where(slot[None, :] < pos_count[:, None], pos_ids, 0xFFFFFF)
    pay = jnp.concatenate(
        [features, (ids & 255).astype(BF), ((ids >> 8) & 255).astype(BF), (ids >> 16).astype(BF),
         jnp.zeros((per, 32), BF)], axis=1)
    pay = jnp.concatenate([pay] + [xor_permute(pay, "y", 4, d) for d in (1, 2, 3)], axis=0)
    own = jnp.concatenate([pay] + [xor_permute(pay, "zl", 4, d) for d in (1, 2, 3)], axis=0)
    other = xor_permute(own, "c", 2, 1)

    zh, x, zl, y, c = (lax.axis_index(a) for a in ("zh", "x", "zl", "y", "c"))
    dev = (((zh * 4 + x) * 4 + zl) * 4 + y) * 2 + c
    where = jnp.stack([zl * 4 + y, dev * labels]).astype(jnp.int32)

    vmem = pl.BlockSpec(memory_space=pltpu.VMEM)
    g, mine, theirs = pl.pallas_call(
        grad_kernel,
        out_shape=(
            jax.ShapeDtypeStruct((rows, labels), BF),
            jax.ShapeDtypeStruct((64, per, 128), F32),
            jax.ShapeDtypeStruct((64, per, 128), BF),
        ),
        in_specs=[pl.BlockSpec(memory_space=pltpu.SMEM), vmem, vmem, pl.BlockSpec(memory_space=pl.ANY), vmem],
        out_specs=(vmem, vmem, vmem),
        scratch_shapes=[
            pltpu.VMEM((rows, width), BF),
            pltpu.VMEM((labels, width), BF),
            pltpu.VMEM((rows, 128), F32),
            pltpu.VMEM((rows, 128), F32),
            pltpu.VMEM((rows, width), F32),
            pltpu.SemaphoreType.DMA((labels // TILE,)),
        ],
        compiler_params=pltpu.CompilerParams(vmem_limit_bytes=40 * 1024 * 1024),
        cost_estimate=pl.CostEstimate(
            flops=4 * rows * labels * width, bytes_accessed=2 * labels * width, transcendentals=2 * rows * labels),
        name="label_grad",
    )(where, own, other, weights, label_bias.reshape(1, labels))

    weight_grad, bias_grad = pl.pallas_call(
        weight_kernel,
        grid=(labels // TILE,),
        out_shape=(
            jax.ShapeDtypeStruct((labels, width), BF),
            jax.ShapeDtypeStruct((1, labels), F32),
        ),
        in_specs=[
            pl.BlockSpec((rows, TILE), lambda t: (0, t)),
            pl.BlockSpec((half, 640), lambda t: (0, 0)),
            pl.BlockSpec((half, 640), lambda t: (0, 0)),
        ],
        out_specs=(pl.BlockSpec((TILE, width), lambda t: (t, 0)), pl.BlockSpec((1, TILE), lambda t: (0, t))),
        cost_estimate=pl.CostEstimate(
            flops=2 * rows * labels * width, bytes_accessed=2 * labels * (width + rows), transcendentals=0),
        name="weight_grad",
    )(g, own, other)

    summed = (mine + xor_permute(theirs, "c", 2, 1).astype(F32)).astype(BF)
    parts = lax.all_to_all(summed, ("x", "zl", "y"), 0, 0)
    total = jnp.sum(parts.astype(F32), axis=0)
    keep = jnp.where(zh == 0, total[:, :64], total[:, 64:])
    send = jnp.where(zh == 0, total[:, 64:], total[:, :64])
    feature_grad = keep + xor_permute(send, "zh", 2, 1)
    return weight_grad, bias_grad.reshape(labels), feature_grad.astype(BF)


def solution(mesh):
    fine = Mesh(mesh.devices.reshape(2, 4, 4, 4, 2), ("zh", "x", "zl", "y", "c"))
    row, col = ("zh", "x"), ("zl", "y", "c")
    return jax.shard_map(
        local,
        mesh=fine,
        in_specs=(P(col, None), P(row + col, None), P(row + col), P(col, None), P(col)),
        out_specs=(P(row + col, None), P(row + col), P(col, row)),
        check_vma=False,
    )
```

time: 397 us -> 92.2 us (0.23)
  blocking collectives: 168 us -> 0 us
  other arithmetic: 70.1 us -> 3.87 us
  waiting for transfers between devices: 76.8 us -> 22.1 us
  Pallas kernels: 0 us -> 34.5 us
  matrix products: 21.9 us -> 0 us
  between operations: 15.6 us -> 0.74 us
  local copies, waits for them, and re-layouts: 17.9 us -> 6.73 us
    unnamed x2 -> x0, blocking collectives: 85.9 us -> none
    all_gather x2 -> x0, blocking collectives: 82.4 us -> none  [the longest x1 41.6 us: local(): gathered = lax.all_gather(features, 'col', axis=0, tiled=True)]
    unnamed x10 -> x0, waiting for transfers between devices: 76.8 us -> none
    unnamed x4 -> x0, other arithmetic: 70 us -> none
    pallas_call x0 -> x2, Pallas kernels: none -> 34.5 us  [the longest x1 17.5 us: local(): pl.pallas_call(weight_kernel, grid=(labels // TILE,), out_shape=(jax.Shap...]
    unnamed x9 -> x0, starting transfers between devices: 26 us -> none
    dot_general x3 -> x0, matrix products: 21.9 us -> none  [the longest x1 9.23 us: block_grad(): lax.dot_general(feat_rows, w_block, (((1,), (1,)), ((), ())), preferred_e...]
    ppermute x0 -> x9, starting transfers between devices: none -> 13.6 us  [xor_permute(): return lax.ppermute(x, axis, [(i, i ^ bit) for i in range(size)])]
  transfers between devices with their start and end apart: 9 -> 10, of which waited for: 2 -> 7; matrix products, arithmetic and copies ran while one was open for 2% -> 2% of each run, Pallas kernels for 0% -> 19%
where the time goes in v1:
time: 92.2 us; the launch traced here: 91.4 us
  Pallas kernels  34.5 us (37%)
  starting transfers between devices  23.4 us (25%)
  waiting for transfers between devices  22.1 us (24%)
  local copies, waits for them, and re-layouts  6.73 us (7%)
  other arithmetic  3.87 us (4%)
    pallas_call x1, Pallas kernels, local(): pl.pallas_call(weight_kernel, grid=(labels // TILE,), out_shape=(jax.Shap...  17.5 us
    pallas_call x1, Pallas kernels, local(): pl.pallas_call(grad_kernel, out_shape=(jax.ShapeDtypeStruct((rows, labels...  17 us
    ppermute x9, starting transfers between devices, xor_permute(): return lax.ppermute(x, axis, [(i, i ^ bit) for i in range(size)])  13.6 us
    all_to_all x1, waiting for transfers between devices, local(): parts = lax.all_to_all(summed, ('x', 'zl', 'y'), 0, 0)  12.1 us
    ppermute x9, waiting for transfers between devices, xor_permute(): return lax.ppermute(x, axis, [(i, i ^ bit) for i in range(size)])  10 us
    all_to_all x1, starting transfers between devices, local(): parts = lax.all_to_all(summed, ('x', 'zl', 'y'), 0, 0)  9.83 us
    unnamed x8, local copies, waits for them, and re-layouts  4.77 us
  transfers between devices with their start and end apart: 10, of which 7 were waited for; matrix products, arithmetic and copies ran while one was open for 2% of the time, Pallas kernels for 19%

profile of v1, /device:TPU:8, one launch (start us, length us, event | category | flops | bytes accessed | tf_op | source)
XLA Modules:
  0.0 91.4 jit_solution(3233988695398360038)
XLA Ops:
  0.6 0.8 shift-right-arithmetic_convert_fusion
  1.4 0.8 concatenate.10
  2.2 1.6 %collective-permute-start.2 = (bf16[12,640]{1,0:T(8,128)(2,1)S(1)}, bf16[12,640]{1,0:T(8,128)(2,1)S(1)}, u32[]{:S(2)}, u32[]{:S(2)}) collective-permute-start(bf16[12,640]{1,0:T(8,128)(2,1)S(1)} %concatenate.10), channel_id=1, source_target_pairs={{0,6},{2,4},{4,2},{6,0},{1,7},{3,5},{5,3},{7,1},{8,14},{10,12},{12... | collective-permute-start | bytes 46088 | tf_op jit(solution)/shard_map/ppermute | solution.py:17
  3.8 2.7 %collective-permute-start.1 = (bf16[12,640]{1,0:T(8,128)(2,1)S(1)}, bf16[12,640]{1,0:T(8,128)(2,1)S(1)}, u32[]{:S(2)}, u32[]{:S(2)}) collective-permute-start(bf16[12,640]{1,0:T(8,128)(2,1)S(1)} %concatenate.10), channel_id=1, source_target_pairs={{0,4},{2,6},{4,0},{6,2},{1,5},{3,7},{5,1},{7,3},{8,12},{10,14},{12... | collective-permute-start | bytes 46088 | tf_op jit(solution)/shard_map/ppermute | solution.py:17
  6.5 2.6 %collective-permute-done.1 = bf16[12,640]{1,0:T(8,128)(2,1)S(1)} collective-permute-done((bf16[12,640]{1,0:T(8,128)(2,1)S(1)}, bf16[12,640]{1,0:T(8,128)(2,1)S(1)}, u32[]{:S(2)}, u32[]{:S(2)}) %collective-permute-start.1) | collective-permute-done | bytes 15392 | tf_op jit(solution)/shard_map/ppermute | solution.py:17
  9.1 1.2 %collective-permute-done = bf16[12,640]{1,0:T(8,128)(2,1)S(1)} collective-permute-done((bf16[12,640]{1,0:T(8,128)(2,1)S(1)}, bf16[12,640]{1,0:T(8,128)(2,1)S(1)}, u32[]{:S(2)}, u32[]{:S(2)}) %collective-permute-start) | collective-permute-done | bytes 15392 | tf_op jit(solution)/shard_map/ppermute | solution.py:17
  10.3 3.5 %collective-permute-start.5 = (bf16[48,640]{1,0:T(8,128)(2,1)S(1)}, bf16[48,640]{1,0:T(8,128)(2,1)S(1)}, u32[]{:S(2)}, u32[]{:S(2)}) collective-permute-start(bf16[48,640]{1,0:T(8,128)(2,1)S(1)} %pad_maximum_fusion), channel_id=1, source_target_pairs={{0,24},{8,16},{16,8},{24,0},{1,25},{9,17},{17,9},{25,1},{2,26},{10... | collective-permute-start | bytes 184328 | tf_op jit(solution)/shard_map/ppermute | solution.py:17
  13.9 0.9 %collective-permute-start.3 = (bf16[48,640]{1,0:T(8,128)(2,1)S(1)}, bf16[48,640]{1,0:T(8,128)(2,1)S(1)}, u32[]{:S(2)}, u32[]{:S(2)}) collective-permute-start(bf16[48,640]{1,0:T(8,128)(2,1)S(1)} %pad_maximum_fusion), channel_id=1, source_target_pairs={{0,8},{8,0},{16,24},{24,16},{1,9},{9,1},{17,25},{25,17},{2,10},{10... | collective-permute-start | bytes 184328 | tf_op jit(solution)/shard_map/ppermute | solution.py:17
  14.8 1.7 %collective-permute-done.5 = bf16[48,640]{1,0:T(8,128)(2,1)S(1)} collective-permute-done((bf16[48,640]{1,0:T(8,128)(2,1)S(1)}, bf16[48,640]{1,0:T(8,128)(2,1)S(1)}, u32[]{:S(2)}, u32[]{:S(2)}) %collective-permute-start.5) | collective-permute-done | bytes 61472 | tf_op jit(solution)/shard_map/ppermute | solution.py:17
  16.5 2.5 %collective-permute-done.4 = bf16[48,640]{1,0:T(8,128)(2,1)S(1)} collective-permute-done((bf16[48,640]{1,0:T(8,128)(2,1)S(1)}, bf16[48,640]{1,0:T(8,128)(2,1)S(1)}, u32[]{:S(2)}, u32[]{:S(2)}) %collective-permute-start.4) | collective-permute-done | bytes 61472 | tf_op jit(solution)/shard_map/ppermute | solution.py:17
  19.0 0.4 concatenate.12.own_ref
  19.5 0.8 reshape.13.bias_ref
  20.3 0.6 collective-permute-done.6.other_ref
  21.0 2.7 %copy-done.1 = bf16[5888,512]{1,0:T(8,128)(2,1)S(1)} copy-done((bf16[5888,512]{1,0:T(8,128)(2,1)S(1)}, bf16[5888,512]{1,0:T(8,128)(2,1)}, u32[]{:S(2)}) %copy-start.1) | copy-done | bytes 6029336
  23.7 17.0 %label_grad.1 = (bf16[384,5888]{1,0:T(8,128)(2,1)S(1)}, f32[64,12,128]{2,1,0:T(8,128)S(1)}, bf16[64,12,128]{2,1,0:T(8,128)(2,1)S(1)}) custom-call(s32[2]{0:T(128)S(1)} %pad_add_fusion.where_ref, bf16[192,640]{1,0:T(8,128)(2,1)S(1)} %concatenate.12.own_ref, bf16[192,640]{1,0:T(8,128)(2,1)S(1)} %collective-permute-done.6.other_ref, ...), custom_call_target="tpu_custom_call" | custom-call | flops 4630511616 | bytes 6029312 | tf_op jit(solution)/shard_map/label_grad/pallas_call | solution.py:145
  40.7 2.1 %copy-done.3 = bf16[384,5888]{1,0:T(8,128)(2,1)} copy-done((bf16[384,5888]{1,0:T(8,128)(2,1)}, bf16[384,5888]{1,0:T(8,128)(2,1)S(1)}, u32[]{:S(2)}) %copy-start.3) | copy-done | bytes 4522008
  42.9 1.4 %collective-permute-done.7 = bf16[64,12,128]{2,1,0:T(8,128)(2,1)S(1)} collective-permute-done((bf16[64,12,128]{2,1,0:T(8,128)(2,1)S(1)}, bf16[64,12,128]{2,1,0:T(8,128)(2,1)S(1)}, u32[]{:S(2)}, u32[]{:S(2)}) %collective-permute-start.7) | collective-permute-done | bytes 196640 | tf_op jit(solution)/shard_map/ppermute | solution.py:17
  44.3 0.8 add_convert_fusion
  45.1 9.8 %all-to-all-start = ((bf16[64,12,128]{2,1,0:T(8,128)(2,1)}), bf16[64,12,128]{2,1,0:T(8,128)(2,1)S(1)}, u32[]{:S(2)}, u32[]{:S(2)}) async-start(bf16[64,12,128]{2,1,0:T(8,128)(2,1)} %add_convert_fusion), calls=%async_computation | async-start | bytes 524288 | tf_op jit(solution)/shard_map/all_to_all | solution.py:187
  54.9 12.1 %all-to-all-done = bf16[64,12,128]{2,1,0:T(8,128)(2,1)S(1)} async-done(((bf16[64,12,128]{2,1,0:T(8,128)(2,1)}), bf16[64,12,128]{2,1,0:T(8,128)(2,1)S(1)}, u32[]{:S(2)}, u32[]{:S(2)}) %all-to-all-start) | async-done | bytes 196640 | tf_op jit(solution)/shard_map/all_to_all | solution.py:187
  67.1 4.6 %collective-permute-start.8 = (f32[12,64]{1,0:T(8,128)S(1)}, f32[12,64]{1,0:T(8,128)S(1)}, u32[]{:S(2)}, u32[]{:S(2)}) collective-permute-start(f32[12,64]{1,0:T(8,128)S(1)} %slice_select_fusion), channel_id=1, source_target_pairs={{0,128},{128,0},{1,129},{129,1},{2,130},{130,2},{3,131},{131,3},{4... | collective-permute-start | bytes 9224 | tf_op jit(solution)/shard_map/ppermute | solution.py:17
  71.7 17.5 %weight_grad.1 = (bf16[5888,512]{1,0:T(8,128)(2,1)}, f32[1,5888]{1,0:T(1,128)}) custom-call(bf16[384,5888]{1,0:T(8,128)(2,1)} %copy-done.3, bf16[192,640]{1,0:T(8,128)(2,1)} %copy-done, bf16[192,640]{1,0:T(8,128)(2,1)} %copy-done.2), custom_call_target="tpu_custom_call" | custom-call | flops 2315255808 | bytes 10551296 | tf_op jit(solution)/shard_map/weight_grad/pallas_call | solution.py:168
  89.3 1.4 %reduce = f32[5888]{0:T(1024)} reduce(f32[1,5888]{1,0:T(1,128)} %get-tuple-element.10, f32[]{:T(128)} %constant.42), dimensions={0}, to_apply=%get-tuple-element.10.reduce_sub_computation | reduce | bytes 47108 | tf_op jit(solution)/shard_map/weight_grad/pallas_call | solution.py:168
  90.7 0.7 add_convert_fusion.1
  (18 shorter events, 0.5 us)
Async XLA Ops:
  2.2 4.3 %collective-permute-start.2 = (bf16[12,640]{1,0:T(8,128)(2,1)S(1)}, bf16[12,640]{1,0:T(8,128)(2,1)S(1)}, u32[]{:S(2)}, u32[]{:S(2)}) collective-permute-start(bf16[12,640]{1,0:T(8,128)(2,1)S(1)} %concatenate.10), channel_id=1, source_target_pairs={{0,6},{2,4},{4,2},{6,0},{1,7},{3,5},{5,3},{7,1},{8,14},{10,12},{12... | collective-permute-start | bytes 46088 | tf_op jit(solution)/shard_map/ppermute | solution.py:17
  3.8 5.3 %collective-permute-start.1 = (bf16[12,640]{1,0:T(8,128)(2,1)S(1)}, bf16[12,640]{1,0:T(8,128)(2,1)S(1)}, u32[]{:S(2)}, u32[]{:S(2)}) collective-permute-start(bf16[12,640]{1,0:T(8,128)(2,1)S(1)} %concatenate.10), channel_id=1, source_target_pairs={{0,4},{2,6},{4,0},{6,2},{1,5},{3,7},{5,1},{7,3},{8,12},{10,14},{12... | collective-permute-start | bytes 46088 | tf_op jit(solution)/shard_map/ppermute | solution.py:17
  6.5 3.8 %collective-permute-start = (bf16[12,640]{1,0:T(8,128)(2,1)S(1)}, bf16[12,640]{1,0:T(8,128)(2,1)S(1)}, u32[]{:S(2)}, u32[]{:S(2)}) collective-permute-start(bf16[12,640]{1,0:T(8,128)(2,1)S(1)} %concatenate.10), channel_id=1, source_target_pairs={{0,2},{2,0},{4,6},{6,4},{1,3},{3,1},{5,7},{7,5},{8,10},{10,8},{12,... | collective-permute-start | bytes 46088 | tf_op jit(solution)/shard_map/ppermute | solution.py:17
  10.3 6.2 %collective-permute-start.5 = (bf16[48,640]{1,0:T(8,128)(2,1)S(1)}, bf16[48,640]{1,0:T(8,128)(2,1)S(1)}, u32[]{:S(2)}, u32[]{:S(2)}) collective-permute-start(bf16[48,640]{1,0:T(8,128)(2,1)S(1)} %pad_maximum_fusion), channel_id=1, source_target_pairs={{0,24},{8,16},{16,8},{24,0},{1,25},{9,17},{17,9},{25,1},{2,26},{10... | collective-permute-start | bytes 184328 | tf_op jit(solution)/shard_map/ppermute | solution.py:17
  13.9 5.1 %collective-permute-start.4 = (bf16[48,640]{1,0:T(8,128)(2,1)S(1)}, bf16[48,640]{1,0:T(8,128)(2,1)S(1)}, u32[]{:S(2)}, u32[]{:S(2)}) collective-permute-start(bf16[48,640]{1,0:T(8,128)(2,1)S(1)} %pad_maximum_fusion), channel_id=1, source_target_pairs={{0,16},{8,24},{16,0},{24,8},{1,17},{9,25},{17,1},{25,9},{2,18},{10... | collective-permute-start | bytes 184328 | tf_op jit(solution)/shard_map/ppermute | solution.py:17
  13.9 5.1 %collective-permute-start.3 = (bf16[48,640]{1,0:T(8,128)(2,1)S(1)}, bf16[48,640]{1,0:T(8,128)(2,1)S(1)}, u32[]{:S(2)}, u32[]{:S(2)}) collective-permute-start(bf16[48,640]{1,0:T(8,128)(2,1)S(1)} %pad_maximum_fusion), channel_id=1, source_target_pairs={{0,8},{8,0},{16,24},{24,16},{1,9},{9,1},{17,25},{25,17},{2,10},{10... | collective-permute-start | bytes 184328 | tf_op jit(solution)/shard_map/ppermute | solution.py:17
  19.4 21.3 %copy-start = (bf16[192,640]{1,0:T(8,128)(2,1)}, bf16[192,640]{1,0:T(8,128)(2,1)S(1)}, u32[]{:S(2)}) copy-start(bf16[192,640]{1,0:T(8,128)(2,1)S(1)} %concatenate.12.own_ref) | copy-start | bytes 737284
  19.4 1.6 %collective-permute-start.6 = (bf16[192,640]{1,0:T(8,128)(2,1)S(1)}, bf16[192,640]{1,0:T(8,128)(2,1)S(1)}, u32[]{:S(2)}, u32[]{:S(2)}) collective-permute-start(bf16[192,640]{1,0:T(8,128)(2,1)S(1)} %concatenate.12.own_ref), channel_id=1, source_target_pairs={{0,1},{1,0},{2,3},{3,2},{4,5},{5,4},{6,7},{7,6},{8,9},{9,8},{10,11... | collective-permute-start | bytes 737288 | tf_op jit(solution)/shard_map/ppermute | solution.py:17
  21.0 2.7 %copy-start.1 = (bf16[5888,512]{1,0:T(8,128)(2,1)S(1)}, bf16[5888,512]{1,0:T(8,128)(2,1)}, u32[]{:S(2)}) copy-start(bf16[5888,512]{1,0:T(8,128)(2,1)} %w_hbm.1) | copy-start | bytes 18087940
  23.7 17.0 %copy-start.2 = (bf16[192,640]{1,0:T(8,128)(2,1)}, bf16[192,640]{1,0:T(8,128)(2,1)S(1)}, u32[]{:S(2)}) copy-start(bf16[192,640]{1,0:T(8,128)(2,1)S(1)} %collective-permute-done.6.other_ref) | copy-start | bytes 737284
  40.7 2.1 %copy-start.3 = (bf16[384,5888]{1,0:T(8,128)(2,1)}, bf16[384,5888]{1,0:T(8,128)(2,1)S(1)}, u32[]{:S(2)}) copy-start(bf16[384,5888]{1,0:T(8,128)(2,1)S(1)} %get-tuple-element.8.g_ref) | copy-start | bytes 13565956
  42.8 1.5 %collective-permute-start.7 = (bf16[64,12,128]{2,1,0:T(8,128)(2,1)S(1)}, bf16[64,12,128]{2,1,0:T(8,128)(2,1)S(1)}, u32[]{:S(2)}, u32[]{:S(2)}) collective-permute-start(bf16[64,12,128]{2,1,0:T(8,128)(2,1)S(1)} %get-tuple-element.12), channel_id=1, source_target_pairs={{0,1},{1,0},{2,3},{3,2},{4,5},{5,4},{6,7},{7,6},{8,9},{9,8},{10,11... | collective-permute-start | bytes 589832 | tf_op jit(solution)/shard_map/ppermute | solution.py:17
  45.1 21.9 %all-to-all-start = ((bf16[64,12,128]{2,1,0:T(8,128)(2,1)}), bf16[64,12,128]{2,1,0:T(8,128)(2,1)S(1)}, u32[]{:S(2)}, u32[]{:S(2)}) async-start(bf16[64,12,128]{2,1,0:T(8,128)(2,1)} %add_convert_fusion), calls=%async_computation | async-start | bytes 524288 | tf_op jit(solution)/shard_map/all_to_all | solution.py:187
  67.1 23.6 %collective-permute-start.8 = (f32[12,64]{1,0:T(8,128)S(1)}, f32[12,64]{1,0:T(8,128)S(1)}, u32[]{:S(2)}, u32[]{:S(2)}) collective-permute-start(f32[12,64]{1,0:T(8,128)S(1)} %slice_select_fusion), channel_id=1, source_target_pairs={{0,128},{128,0},{1,129},{129,1},{2,130},{130,2},{3,131},{131,3},{4... | collective-permute-start | bytes 9224 | tf_op jit(solution)/shard_map/ppermute | solution.py:17

commit v2 on v1

v2 whole, which is shorter than its diff:
```python
import functools

import jax
import jax.numpy as jnp
from jax import lax
from jax.experimental import pallas as pl
from jax.experimental.pallas import tpu as pltpu
from jax.sharding import Mesh, PartitionSpec as P

BF = jnp.bfloat16
F32 = jnp.float32
KEY = 8192
BITS = (0, 3, 2, 1)
CHUNK = 1024
DX_CHUNK = 2048
ROWS_AT_ONCE = 64
SPLIT = 3072
WEIGHT_VMEM = 59 * 1024 * 1024
MIB = 1024 * 1024


def cuts(total, size):
    return [(a, min(size, total - a)) for a in range(0, total, size)]


def xor_permute(x, axis, size, bit):
    return lax.ppermute(x, axis, [(i, i ^ bit) for i in range(size)])


def pack_kernel(*refs):
    *parts, out_ref = refs
    n = parts[0].shape[0]
    for i, part in enumerate(parts):
        out_ref[i * n:(i + 1) * n] = part[...]


def stage_kernel(w_hbm, w_ref, sem):
    copy = pltpu.make_async_copy(w_hbm, w_ref, sem)
    copy.start()
    copy.wait()


def grad_kernel(own_ref, other_ref, w_scr, bias_ref, g_hbm, bg_ref, mine_ref, theirs_ref,
                g_scr, f_scr, first_scr, key_scr, dx_scr, even_scr, odd_scr, sems):
    labels, width = w_scr.shape
    zh, x, zl, y, c = (lax.axis_index(a) for a in ("zh", "x", "zl", "y", "c"))
    dev = (((zh * 4 + x) * 4 + zl) * 4 + y) * 2 + c
    half = own_ref.shape[0]
    rows = 2 * half
    chunks = cuts(labels, CHUNK)
    f_scr[0:half] = own_ref[:, 0:width]
    f_scr[half:rows] = other_ref[:, 0:width]
    f_copy = pltpu.make_async_copy(f_scr, g_hbm.at[:, pl.ds(labels, width)], sems.at[len(chunks)])
    f_copy.start()

    digit = lax.broadcasted_iota(jnp.int32, (128, 128), 0)
    lane = lax.broadcasted_iota(jnp.int32, (128, 128), 1)
    same = (digit % 32) == (lane % 32)
    power = jnp.where(digit < 32, 1.0, jnp.where(digit < 64, 256.0, jnp.where(digit < 96, 65536.0, 0.0)))
    decode = jnp.where(same, power, 0.0).astype(BF)
    offset = (dev * labels).astype(F32)
    row = lax.broadcasted_iota(jnp.int32, (half, 128), 0).astype(F32)
    for h, ref in enumerate((own_ref, other_ref)):
        at = pl.ds(h * half, half)
        local = jnp.dot(ref[:, width:width + 128], decode, preferred_element_type=F32) - offset
        local = jnp.where((local >= 0.0) & (local < float(labels)), local, -1.0)
        first = jnp.max(local, axis=1, keepdims=True)
        first_scr[at] = jnp.broadcast_to(first, (half, 128))
        more = (local >= 0.0) & (local < first)
        key_scr[at] = jnp.where(more, (row + float(h * half)) * float(KEY) + local, -1.0)

    buffers = (even_scr, odd_scr)
    lanes = lax.broadcasted_iota(jnp.int32, (ROWS_AT_ONCE, 128), 1).astype(F32)

    def logits(i):
        a, n = chunks[i]
        buffers[i % 2][:, 0:n] = lax.dot_general(
            f_scr[...], w_scr[a:a + n], (((1,), (1,)), ((), ())), preferred_element_type=F32)

    logits(0)
    for i, (a, n) in enumerate(chunks):
        if i + 1 < len(chunks):
            logits(i + 1)
        for k in range(0, n, 128):
            bias = bias_ref[a + k:a + k + 128].reshape(1, 128)
            for r in range(0, rows, ROWS_AT_ONCE):
                x = buffers[i % 2][r:r + ROWS_AT_ONCE, k:k + 128] + bias
                s = pltpu.reciprocal(1.0 + jnp.exp(-x), approx=True)
                hit = (first_scr[r:r + ROWS_AT_ONCE] - float(a + k)) == lanes
                g_scr[r:r + ROWS_AT_ONCE, a + k:a + k + 128] = jnp.where(hit, s - 1.0, s).astype(BF)

    def one_hit(top):
        key = top.astype(jnp.int32)
        b = key // KEY
        l = key - b * KEY
        b16 = pl.ds(pl.multiple_of((b // 16) * 16, 16), 16)
        l128 = pl.ds(pl.multiple_of((l // 128) * 128, 128), 128)
        r = lax.broadcasted_iota(jnp.int32, (16, 128), 0)
        c = lax.broadcasted_iota(jnp.int32, (16, 128), 1)
        old = g_scr[b16, l128].astype(F32)
        g_scr[b16, l128] = jnp.where((r == b % 16) & (c == l % 128), old - 1.0, old).astype(BF)
        keys = key_scr[...]
        keys = jnp.where(keys == top, -1.0, keys)
        key_scr[...] = keys
        return jnp.max(keys)

    lax.while_loop(lambda top: top >= 0.0, one_hit, jnp.max(key_scr[...]))
    g_copies = [
        pltpu.make_async_copy(g_scr.at[:, pl.ds(a, n)], g_hbm.at[:, pl.ds(a, n)], sems.at[i])
        for i, (a, n) in enumerate(chunks)
    ]
    for copy in g_copies:
        copy.start()
    for a, n in chunks:
        bg_ref[a:a + n] = jnp.sum(g_scr[:, a:a + n].astype(F32), axis=0)

    for j, (a, n) in enumerate(cuts(labels, DX_CHUNK)):
        term = jnp.dot(g_scr[:, a:a + n], w_scr[a:a + n], preferred_element_type=F32)
        if j == 0:
            dx_scr[0:rows] = term
        else:
            dx_scr[0:rows] += term
    dx_scr[rows:rows + 16] = jnp.zeros((16, width), F32)

    low = lax.broadcasted_iota(jnp.int32, (half + 16, 128), 1) < 64
    per, block = half // 16, mine_ref.shape[2]
    for jc, ref in enumerate((mine_ref, theirs_ref)):
        at = pl.ds(jc * half, half + 16)
        for to_x in range(4):
            k = (to_x // 2) * 128
            left = dx_scr[at, k:k + 128]
            right = dx_scr[at, 256 + k:256 + k + 128]
            if to_x % 2 == 0:
                both = jnp.where(low, left, pltpu.roll(right, 64, 1))
            else:
                both = jnp.where(low, pltpu.roll(left, 64, 1), right)
            for pz, jz in enumerate(BITS):
                for py, jy in enumerate(BITS):
                    j = (pz * 4 + py) * per
                    ref[to_x * 4 + (y ^ jy), zl ^ jz] = both[j:j + block].astype(ref.dtype)
    for copy in g_copies:
        copy.wait()
    f_copy.wait()


def weight_kernel(begin, end, g_hbm, *refs):
    wg_hbm, g_scr, f_scr, out_scr, g_sems, out_sems, f_sem = refs[-7:]
    chunks = cuts(end - begin, CHUNK)
    labels, width = wg_hbm.shape
    f_copy = pltpu.make_async_copy(g_hbm.at[:, pl.ds(labels, width)], f_scr, f_sem)
    f_copy.start()
    g_copies = [
        pltpu.make_async_copy(g_hbm.at[:, pl.ds(begin + a, n)], g_scr.at[:, pl.ds(a, n)], g_sems.at[i])
        for i, (a, n) in enumerate(chunks)
    ]
    out_copies = [
        pltpu.make_async_copy(out_scr.at[pl.ds(a, n)], wg_hbm.at[pl.ds(begin + a, n)], out_sems.at[i])
        for i, (a, n) in enumerate(chunks)
    ]
    for copy in g_copies:
        copy.start()
    f_copy.wait()
    for i, (a, n) in enumerate(chunks):
        g_copies[i].wait()
        g = g_scr[:, a:a + n]
        out_scr[a:a + n] = lax.dot_general(
            g, f_scr[...], (((0,), (0,)), ((), ())), preferred_element_type=F32).astype(BF)
        out_copies[i].start()
    for copy in out_copies:
        copy.wait()


def local(features, weights, label_bias, pos_ids, pos_count):
    labels, width = weights.shape
    per, slots = pos_ids.shape
    half = per * 16
    rows = 2 * half
    wide = width + 4 * slots
    vmem = pl.BlockSpec(memory_space=pltpu.VMEM)
    hbm = pl.BlockSpec(memory_space=pltpu.HBM)
    n_chunks = len(cuts(labels, CHUNK))

    slot = jnp.arange(slots, dtype=jnp.int32)
    ids = jnp.where(slot[None, :] < pos_count[:, None], pos_ids, 0xFFFFFF)
    pay = jnp.pad(features, ((0, 0), (0, wide - width)))
    for k in range(3):
        at = width + k * slots
        pay = pay + jnp.pad(((ids >> (8 * k)) & 255).astype(BF), ((0, 0), (at, wide - at - slots)))
    pay = jnp.concatenate([pay] + [xor_permute(pay, "y", 4, d) for d in BITS[1:]], axis=0)
    pay, weights_then = lax.optimization_barrier((pay, weights))
    staged = pl.pallas_call(
        stage_kernel,
        out_shape=jax.ShapeDtypeStruct((labels, width), BF),
        in_specs=[hbm],
        out_specs=vmem,
        scratch_shapes=[pltpu.SemaphoreType.DMA],
        compiler_params=pltpu.CompilerParams(vmem_limit_bytes=46 * MIB),
        cost_estimate=pl.CostEstimate(flops=0, bytes_accessed=4 * labels * width, transcendentals=0),
        name="stage_weights",
    )(weights_then)
    zs = [xor_permute(pay, "zl", 4, d) for d in BITS[1:]]
    staged, *zs = lax.optimization_barrier((staged, *zs))
    own = pl.pallas_call(
        pack_kernel,
        out_shape=jax.ShapeDtypeStruct((half, wide), BF),
        in_specs=[vmem] * 4,
        out_specs=vmem,
        compiler_params=pltpu.CompilerParams(vmem_limit_bytes=4 * MIB),
        name="pack",
    )(pay, *zs)
    other = xor_permute(own, "c", 2, 1)

    g, bias_grad, mine, theirs = pl.pallas_call(
        grad_kernel,
        out_shape=(
            jax.ShapeDtypeStruct((rows, 2 * labels), BF),
            jax.ShapeDtypeStruct((labels,), F32),
            jax.ShapeDtypeStruct((16, 4, 16, 128), F32),
            jax.ShapeDtypeStruct((16, 4, 16, 128), BF),
        ),
        in_specs=[vmem] * 4,
        out_specs=(hbm, vmem, vmem, vmem),
        scratch_shapes=[
            pltpu.VMEM((rows, labels), BF),
            pltpu.VMEM((rows, width), BF),
            pltpu.VMEM((rows, 128), F32),
            pltpu.VMEM((rows, 128), F32),
            pltpu.VMEM((rows + 16, width), F32),
            pltpu.VMEM((rows, CHUNK), F32),
            pltpu.VMEM((rows, CHUNK), F32),
            pltpu.SemaphoreType.DMA((n_chunks + 1,)),
        ],
        compiler_params=pltpu.CompilerParams(vmem_limit_bytes=44 * MIB),
        cost_estimate=pl.CostEstimate(
            flops=4 * rows * labels * width, bytes_accessed=2 * labels * (width + rows),
            transcendentals=2 * rows * labels),
        name="label_grad",
    )(own, other, staged, label_bias)

    send = (mine + xor_permute(theirs, "c", 2, 1).astype(F32)).astype(BF)
    parts = lax.all_to_all(send, ("x", "y"), 0, 0)

    def weight_part(begin, end, *before):
        n = len(cuts(end - begin, CHUNK))
        return pl.pallas_call(
            functools.partial(weight_kernel, begin, end),
            out_shape=jax.ShapeDtypeStruct((labels, width), BF),
            in_specs=[hbm] * (1 + len(before)),
            out_specs=hbm,
            input_output_aliases={1: 0} if before else {},
            scratch_shapes=[
                pltpu.VMEM((rows, end - begin), BF),
                pltpu.VMEM((rows, width), BF),
                pltpu.VMEM((end - begin, width), BF),
                pltpu.SemaphoreType.DMA((n,)),
                pltpu.SemaphoreType.DMA((n,)),
                pltpu.SemaphoreType.DMA,
            ],
            compiler_params=pltpu.CompilerParams(vmem_limit_bytes=WEIGHT_VMEM),
            cost_estimate=pl.CostEstimate(
                flops=2 * rows * (end - begin) * width, bytes_accessed=2 * (end - begin) * (width + rows),
                transcendentals=0),
            name="weight_grad",
        )(g, *before)

    weight_grad = weight_part(0, SPLIT)
    total = jnp.sum(parts.astype(F32), axis=0)
    total, weight_grad = lax.optimization_barrier((total, weight_grad))
    weight_grad = weight_part(SPLIT, labels, weight_grad)
    blocks = lax.all_to_all(jnp.concatenate([total, total]), ("zh", "zl"), 0, 0)
    total = jnp.sum(blocks, axis=0)[:per]
    feature_grad = jnp.where(lax.axis_index("zh") == 0, total[:, :64], total[:, 64:]).astype(BF)
    return weight_grad, bias_grad, feature_grad


def solution(mesh):
    fine = Mesh(mesh.devices.reshape(2, 4, 4, 4, 2), ("zh", "x", "zl", "y", "c"))
    row, col = ("zh", "x"), ("zl", "y", "c")
    return jax.shard_map(
        local,
        mesh=fine,
        in_specs=(P(col, None), P(row + col, None), P(row + col), P(col, None), P(col)),
        out_specs=(P(row + col, None), P(row + col), P(col, row)),
        check_vma=False,
    )
```

time: 92.2 us -> 64.5 us (0.70)
  Pallas kernels: 34.5 us -> 21.9 us
  waiting for transfers between devices: 22.1 us -> 14.6 us
  local copies, waits for them, and re-layouts: 6.73 us -> 0.01 us
    pallas_call x2 -> x5, Pallas kernels: 34.5 us -> 21.9 us  [the longest x1 9.88 us: local(): pl.pallas_call(grad_kernel, out_shape=(jax.ShapeDtypeStruct((rows, 2 * la...]
    all_to_all x1 -> x2, waiting for transfers between devices: 12.1 us -> 6.47 us  [the longest x1 3.87 us: local(): blocks = lax.all_to_all(jnp.concatenate([total, total]), ('zh', 'zl'), 0, 0)]
    unnamed x8 -> x2, local copies, waits for them, and re-layouts: 4.77 us -> 0.01 us
    ppermute x9 -> x8, starting transfers between devices: 13.6 us -> 9.07 us  [xor_permute(): return lax.ppermute(x, axis, [(i, i ^ bit) for i in range(size)])]
    all_to_all x1 -> x2, starting transfers between devices: 9.83 us -> 13.9 us  [the longest x1 8 us: local(): parts = lax.all_to_all(send, ('x', 'y'), 0, 0)]
    ppermute x9 -> x8, waiting for transfers between devices: 10 us -> 8.13 us  [xor_permute(): return lax.ppermute(x, axis, [(i, i ^ bit) for i in range(size)])]
    pallas_call x1 -> x0, other arithmetic: 1.4 us -> none  [local(): pl.pallas_call(weight_kernel, grid=(labels // TILE,), out_shape=(jax.Shap...]
    concatenate x2 -> x0, local copies, waits for them, and re-layouts: 1.2 us -> none  [the longest x1 0.81 us: local(): jnp.concatenate([features, (ids & 255).astype(BF), (ids >> 8 & 255).astyp...]
  transfers between devices with their start and end apart: 10 -> 10, of which waited for: 7 -> 7; matrix products, arithmetic and copies ran while one was open for 2% -> 0% of each run, Pallas kernels for 19% -> 19%
where the time goes in v2:
time: 64.5 us; the launch traced here: 63.9 us
  starting transfers between devices  23 us (36%)
  Pallas kernels  21.9 us (34%)
  waiting for transfers between devices  14.6 us (23%)
  other arithmetic  3.74 us (6%)
  between operations  0.71 us (1%)
    pallas_call x1, Pallas kernels, local(): pl.pallas_call(grad_kernel, out_shape=(jax.ShapeDtypeStruct((rows, 2 * la...  9.88 us
    pallas_call x2, Pallas kernels, weight_part(): pl.pallas_call(functools.partial(weight_kernel, begin, end), out_shape=ja...  9.24 us
    ppermute x8, starting transfers between devices, xor_permute(): return lax.ppermute(x, axis, [(i, i ^ bit) for i in range(size)])  9.07 us
    ppermute x8, waiting for transfers between devices, xor_permute(): return lax.ppermute(x, axis, [(i, i ^ bit) for i in range(size)])  8.13 us
    all_to_all x1, starting transfers between devices, local(): parts = lax.all_to_all(send, ('x', 'y'), 0, 0)  8 us
    all_to_all x1, starting transfers between devices, local(): blocks = lax.all_to_all(jnp.concatenate([total, total]), ('zh', 'zl'), 0, 0)  5.88 us
    all_to_all x1, waiting for transfers between devices, local(): blocks = lax.all_to_all(jnp.concatenate([total, total]), ('zh', 'zl'), 0, 0)  3.87 us
    pallas_call x1, Pallas kernels, local(): pl.pallas_call(stage_kernel, out_shape=jax.ShapeDtypeStruct((labels, widt...  2.72 us
  transfers between devices with their start and end apart: 10, of which 7 were waited for; matrix products, arithmetic and copies ran while one was open for 0% of the time, Pallas kernels for 19%

profile of v2, /device:TPU:8, one launch (start us, length us, event | category | flops | bytes accessed | tf_op | source)
XLA Modules:
  0.0 63.9 jit_solution(13613537171762150463)
XLA Ops:
  0.6 0.8 %and_convert_fusion.2 = (bf16[12,32]{1,0:T(8,128)(2,1)S(1)}, bf16[12,32]{1,0:T(8,128)(2,1)S(1)}, bf16[12,32]{1,0:T(8,128)(2,1)S(1)}) fusion(s32[12,32]{1,0:T(8,128)} %param.8, s32[12]{0:T(128)} %param.9), kind=kLoop, calls=%fused_computation.9 | loop fusion | flops 4224 | bytes 3888 | tf_op jit(solution)/shard_map/convert_element_type | solution.py:188
  1.4 0.8 %pad_add_fusion = bf16[12,640]{1,0:T(8,128)(2,1)S(1)} fusion(bf16[12,32]{1,0:T(8,128)(2,1)S(1)} %get-tuple-element.29, bf16[12,32]{1,0:T(8,128)(2,1)S(1)} %get-tuple-element.28, bf16[12,32]{1,0:T(8,128)(2,1)S(1)} %get-tuple-element.27, bf16[12,512]{1,0:T(8,128)(2,1)} %param.5), kind=kLoop, calls=%fused_computation.4 | loop fusion | flops 61440 | bytes 29952 | tf_op jit(solution)/shard_map/add | solution.py:188
  2.2 1.6 %collective-permute-start = (bf16[12,640]{1,0:T(8,128)(2,1)S(1)}, bf16[12,640]{1,0:T(8,128)(2,1)S(1)}, u32[]{:S(2)}, u32[]{:S(2)}) collective-permute-start(bf16[12,640]{1,0:T(8,128)(2,1)S(1)} %pad_add_fusion), channel_id=1, source_target_pairs={{0,6},{2,4},{4,2},{6,0},{1,7},{3,5},{5,3},{7,1},{8,14},{10,12},{12... | collective-permute-start | bytes 46088 | tf_op jit(solution)/shard_map/ppermute | solution.py:27
  3.8 2.7 %collective-permute-start.1 = (bf16[12,640]{1,0:T(8,128)(2,1)S(1)}, bf16[12,640]{1,0:T(8,128)(2,1)S(1)}, u32[]{:S(2)}, u32[]{:S(2)}) collective-permute-start(bf16[12,640]{1,0:T(8,128)(2,1)S(1)} %pad_add_fusion), channel_id=1, source_target_pairs={{0,4},{2,6},{4,0},{6,2},{1,5},{3,7},{5,1},{7,3},{8,12},{10,14},{12... | collective-permute-start | bytes 46088 | tf_op jit(solution)/shard_map/ppermute | solution.py:27
  6.5 2.6 %collective-permute-done.1 = bf16[12,640]{1,0:T(8,128)(2,1)S(1)} collective-permute-done((bf16[12,640]{1,0:T(8,128)(2,1)S(1)}, bf16[12,640]{1,0:T(8,128)(2,1)S(1)}, u32[]{:S(2)}, u32[]{:S(2)}) %collective-permute-start.1) | collective-permute-done | bytes 15392 | tf_op jit(solution)/shard_map/ppermute | solution.py:27
  9.1 1.2 %collective-permute-done.2 = bf16[12,640]{1,0:T(8,128)(2,1)S(1)} collective-permute-done((bf16[12,640]{1,0:T(8,128)(2,1)S(1)}, bf16[12,640]{1,0:T(8,128)(2,1)S(1)}, u32[]{:S(2)}, u32[]{:S(2)}) %collective-permute-start.2) | collective-permute-done | bytes 15392 | tf_op jit(solution)/shard_map/ppermute | solution.py:27
  10.3 3.5 %collective-permute-start.3 = (bf16[48,640]{1,0:T(8,128)(2,1)S(1)}, bf16[48,640]{1,0:T(8,128)(2,1)S(1)}, u32[]{:S(2)}, u32[]{:S(2)}) collective-permute-start(bf16[48,640]{1,0:T(8,128)(2,1)S(1)} %pad_maximum_fusion.1.refs_0_), channel_id=1, source_target_pairs={{0,24},{8,16},{16,8},{24,0},{1,25},{9,17},{17,9},{25,1},{2,26},{10... | collective-permute-start | bytes 184328 | tf_op jit(solution)/shard_map/ppermute | solution.py:27
  13.8 0.9 %collective-permute-start.5 = (bf16[48,640]{1,0:T(8,128)(2,1)S(1)}, bf16[48,640]{1,0:T(8,128)(2,1)S(1)}, u32[]{:S(2)}, u32[]{:S(2)}) collective-permute-start(bf16[48,640]{1,0:T(8,128)(2,1)S(1)} %pad_maximum_fusion.1.refs_0_), channel_id=1, source_target_pairs={{0,8},{8,0},{16,24},{24,16},{1,9},{9,1},{17,25},{25,17},{2,10},{10... | collective-permute-start | bytes 184328 | tf_op jit(solution)/shard_map/ppermute | solution.py:27
  14.8 2.7 %stage_weights.1.w_scr = bf16[5888,512]{1,0:T(8,128)(2,1)S(1)} custom-call(bf16[5888,512]{1,0:T(8,128)(2,1)} %w_hbm), custom_call_target="tpu_custom_call" | custom-call | bytes 12058624 | tf_op jit(solution)/shard_map/stage_weights/pallas_call | solution.py:191
  17.5 1.5 %collective-permute-done.4.refs_2_ = bf16[48,640]{1,0:T(8,128)(2,1)S(1)} collective-permute-done((bf16[48,640]{1,0:T(8,128)(2,1)S(1)}, bf16[48,640]{1,0:T(8,128)(2,1)S(1)}, u32[]{:S(2)}, u32[]{:S(2)}) %collective-permute-start.4) | collective-permute-done | bytes 61472 | tf_op jit(solution)/shard_map/ppermute | solution.py:27
  19.0 0.1 collective-permute-start.6
  19.1 1.5 %collective-permute-done.6.other_ref = bf16[192,640]{1,0:T(8,128)(2,1)S(1)} collective-permute-done((bf16[192,640]{1,0:T(8,128)(2,1)S(1)}, bf16[192,640]{1,0:T(8,128)(2,1)S(1)}, u32[]{:S(2)}, u32[]{:S(2)}) %collective-permute-start.6) | collective-permute-done | bytes 245792 | tf_op jit(solution)/shard_map/ppermute | solution.py:27
  20.6 9.9 %label_grad.1 = (bf16[384,11776]{1,0:T(8,128)(2,1)}, f32[5888]{0:T(1024)}, f32[16,4,16,128]{3,2,1,0:T(8,128)S(1)}, bf16[16,4,16,128]{3,2,1,0:T(8,128)(2,1)S(1)}) custom-call(bf16[192,640]{1,0:T(8,128)(2,1)S(1)} %pack.1.own_ref, bf16[192,640]{1,0:T(8,128)(2,1)S(1)} %collective-permute-done.6.other_ref, bf16[5888,512]{1,0:T(8,128)(2,1)S(1)} %stage_weights.1.w_scr, ...), custom_call_target="tpu_custom_call" | custom-call | flops 4630511616 | bytes 10551296 | tf_op jit(solution)/shard_map/label_grad/pallas_call | solution.py:213
  30.5 0.2 collective-permute-start.7
  30.7 1.4 %collective-permute-done.7 = bf16[16,4,16,128]{3,2,1,0:T(8,128)(2,1)S(1)} collective-permute-done((bf16[16,4,16,128]{3,2,1,0:T(8,128)(2,1)S(1)}, bf16[16,4,16,128]{3,2,1,0:T(8,128)(2,1)S(1)}, u32[]{:S(2)}, u32[]{:S(2)}) %collective-permute-start.7) | collective-permute-done | bytes 262176 | tf_op jit(solution)/shard_map/ppermute | solution.py:27
  32.1 0.8 %add_convert_fusion = bf16[16,4,16,128]{3,2,1,0:T(8,128)(2,1)} fusion(f32[16,4,16,128]{3,2,1,0:T(8,128)S(1)} %get-tuple-element.22, bf16[16,4,16,128]{3,2,1,0:T(8,128)(2,1)S(1)} %collective-permute-done.7), kind=kLoop, calls=%fused_computation.1 | loop fusion | flops 393216 | bytes 1048576 | tf_op jit(solution)/shard_map/convert_element_type | solution.py:240
  32.9 8.0 %all-to-all-start = ((bf16[16,4,16,128]{3,2,1,0:T(8,128)(2,1)}), bf16[16,4,16,128]{3,2,1,0:T(8,128)(2,1)S(1)}, u32[]{:S(2)}, u32[]{:S(2)}) async-start(bf16[16,4,16,128]{3,2,1,0:T(8,128)(2,1)} %add_convert_fusion), calls=%async_computation | async-start | bytes 524288 | tf_op jit(solution)/shard_map/all_to_all | solution.py:241
  40.9 4.7 %weight_grad.2.refs_0_ = bf16[5888,512]{1,0:T(8,128)(2,1)} custom-call(bf16[384,11776]{1,0:T(8,128)(2,1)} %get-tuple-element.21.g_hbm), custom_call_target="tpu_custom_call" | custom-call | flops 1207959552 | bytes 5505024 | tf_op jit(solution)/shard_map/weight_grad/pallas_call | solution.py:245
  45.7 2.6 %all-to-all-done = bf16[16,4,16,128]{3,2,1,0:T(8,128)(2,1)S(1)} async-done(((bf16[16,4,16,128]{3,2,1,0:T(8,128)(2,1)}), bf16[16,4,16,128]{3,2,1,0:T(8,128)(2,1)S(1)}, u32[]{:S(2)}, u32[]{:S(2)}) %all-to-all-start) | async-done | bytes 262176 | tf_op jit(solution)/shard_map/all_to_all | solution.py:241
  48.3 0.6 pad_maximum_fusion
  48.9 5.9 %all-to-all-start.1 = ((f32[8,16,128]{2,1,0:T(8,128)}), f32[8,16,128]{2,1,0:T(8,128)S(1)}, u32[]{:S(2)}, u32[]{:S(2)}) async-start(f32[8,16,128]{2,1,0:T(8,128)} %pad_maximum_fusion), calls=%async_computation.1 | async-start | bytes 131072 | tf_op jit(solution)/shard_map/all_to_all | solution.py:270
  54.8 4.5 %weight_grad.3 = bf16[5888,512]{1,0:T(8,128)(2,1)} custom-call(bf16[384,11776]{1,0:T(8,128)(2,1)} %get-tuple-element.21.g_hbm, bf16[5888,512]{1,0:T(8,128)(2,1)} %weight_grad.2.refs_0_), custom_call_target="tpu_custom_call", output_to_operand_aliasing={{}: (1, {})} | custom-call | flops 1107296256 | bytes 5046272 | tf_op jit(solution)/shard_map/weight_grad/pallas_call | solution.py:245
  59.3 3.9 %all-to-all-done.1 = f32[8,16,128]{2,1,0:T(8,128)S(1)} async-done(((f32[8,16,128]{2,1,0:T(8,128)}), f32[8,16,128]{2,1,0:T(8,128)S(1)}, u32[]{:S(2)}, u32[]{:S(2)}) %all-to-all-start.1) | async-done | bytes 65568 | tf_op jit(solution)/shard_map/all_to_all | solution.py:270
  63.2 0.7 %fusion = bf16[12,64]{1,0:T(8,128)(2,1)} fusion(bf16[16,128]{1,0:T(8,128)(2,1)S(1)} %reduce_sum.19, pred[]{:T(512)S(6)} %eq.3), kind=kLoop, calls=%fused_computation.6 | loop fusion | flops 768 | bytes 4609 | tf_op jit(solution)/shard_map/convert_element_type | solution.py:272
  (11 shorter events, 0.1 us)
Async XLA Ops:
  2.2 4.3 %collective-permute-start = (bf16[12,640]{1,0:T(8,128)(2,1)S(1)}, bf16[12,640]{1,0:T(8,128)(2,1)S(1)}, u32[]{:S(2)}, u32[]{:S(2)}) collective-permute-start(bf16[12,640]{1,0:T(8,128)(2,1)S(1)} %pad_add_fusion), channel_id=1, source_target_pairs={{0,6},{2,4},{4,2},{6,0},{1,7},{3,5},{5,3},{7,1},{8,14},{10,12},{12... | collective-permute-start | bytes 46088 | tf_op jit(solution)/shard_map/ppermute | solution.py:27
  3.8 5.3 %collective-permute-start.1 = (bf16[12,640]{1,0:T(8,128)(2,1)S(1)}, bf16[12,640]{1,0:T(8,128)(2,1)S(1)}, u32[]{:S(2)}, u32[]{:S(2)}) collective-permute-start(bf16[12,640]{1,0:T(8,128)(2,1)S(1)} %pad_add_fusion), channel_id=1, source_target_pairs={{0,4},{2,6},{4,0},{6,2},{1,5},{3,7},{5,1},{7,3},{8,12},{10,14},{12... | collective-permute-start | bytes 46088 | tf_op jit(solution)/shard_map/ppermute | solution.py:27
  6.5 3.8 %collective-permute-start.2 = (bf16[12,640]{1,0:T(8,128)(2,1)S(1)}, bf16[12,640]{1,0:T(8,128)(2,1)S(1)}, u32[]{:S(2)}, u32[]{:S(2)}) collective-permute-start(bf16[12,640]{1,0:T(8,128)(2,1)S(1)} %pad_add_fusion), channel_id=1, source_target_pairs={{0,2},{2,0},{4,6},{6,4},{1,3},{3,1},{5,7},{7,5},{8,10},{10,8},{12,... | collective-permute-start | bytes 46088 | tf_op jit(solution)/shard_map/ppermute | solution.py:27
  10.3 10.3 %copy-start = (f32[5888]{0:T(1024)S(1)}, f32[5888]{0:T(1024)}, u32[]{:S(2)}) copy-start(f32[5888]{0:T(1024)} %bias_ref.1) | copy-start | bytes 70660
  10.3 7.2 %collective-permute-start.3 = (bf16[48,640]{1,0:T(8,128)(2,1)S(1)}, bf16[48,640]{1,0:T(8,128)(2,1)S(1)}, u32[]{:S(2)}, u32[]{:S(2)}) collective-permute-start(bf16[48,640]{1,0:T(8,128)(2,1)S(1)} %pad_maximum_fusion.1.refs_0_), channel_id=1, source_target_pairs={{0,24},{8,16},{16,8},{24,0},{1,25},{9,17},{17,9},{25,1},{2,26},{10... | collective-permute-start | bytes 184328 | tf_op jit(solution)/shard_map/ppermute | solution.py:27
  13.8 5.1 %collective-permute-start.4 = (bf16[48,640]{1,0:T(8,128)(2,1)S(1)}, bf16[48,640]{1,0:T(8,128)(2,1)S(1)}, u32[]{:S(2)}, u32[]{:S(2)}) collective-permute-start(bf16[48,640]{1,0:T(8,128)(2,1)S(1)} %pad_maximum_fusion.1.refs_0_), channel_id=1, source_target_pairs={{0,16},{8,24},{16,0},{24,8},{1,17},{9,25},{17,1},{25,9},{2,18},{10... | collective-permute-start | bytes 184328 | tf_op jit(solution)/shard_map/ppermute | solution.py:27
  13.8 5.1 %collective-permute-start.5 = (bf16[48,640]{1,0:T(8,128)(2,1)S(1)}, bf16[48,640]{1,0:T(8,128)(2,1)S(1)}, u32[]{:S(2)}, u32[]{:S(2)}) collective-permute-start(bf16[48,640]{1,0:T(8,128)(2,1)S(1)} %pad_maximum_fusion.1.refs_0_), channel_id=1, source_target_pairs={{0,8},{8,0},{16,24},{24,16},{1,9},{9,1},{17,25},{25,17},{2,10},{10... | collective-permute-start | bytes 184328 | tf_op jit(solution)/shard_map/ppermute | solution.py:27
  19.0 1.6 %collective-permute-start.6 = (bf16[192,640]{1,0:T(8,128)(2,1)S(1)}, bf16[192,640]{1,0:T(8,128)(2,1)S(1)}, u32[]{:S(2)}, u32[]{:S(2)}) collective-permute-start(bf16[192,640]{1,0:T(8,128)(2,1)S(1)} %pack.1.own_ref), channel_id=1, source_target_pairs={{0,1},{1,0},{2,3},{3,2},{4,5},{5,4},{6,7},{7,6},{8,9},{9,8},{10,11... | collective-permute-start | bytes 737288 | tf_op jit(solution)/shard_map/ppermute | solution.py:27
  30.5 1.6 %collective-permute-start.7 = (bf16[16,4,16,128]{3,2,1,0:T(8,128)(2,1)S(1)}, bf16[16,4,16,128]{3,2,1,0:T(8,128)(2,1)S(1)}, u32[]{:S(2)}, u32[]{:S(2)}) collective-permute-start(bf16[16,4,16,128]{3,2,1,0:T(8,128)(2,1)S(1)} %get-tuple-element.23), channel_id=1, source_target_pairs={{0,1},{1,0},{2,3},{3,2},{4,5},{5,4},{6,7},{7,6},{8,9},{9,8},{10,11... | collective-permute-start | bytes 786440 | tf_op jit(solution)/shard_map/ppermute | solution.py:27
  32.9 15.4 %all-to-all-start = ((bf16[16,4,16,128]{3,2,1,0:T(8,128)(2,1)}), bf16[16,4,16,128]{3,2,1,0:T(8,128)(2,1)S(1)}, u32[]{:S(2)}, u32[]{:S(2)}) async-start(bf16[16,4,16,128]{3,2,1,0:T(8,128)(2,1)} %add_convert_fusion), calls=%async_computation | async-start | bytes 524288 | tf_op jit(solution)/shard_map/all_to_all | solution.py:241
  48.9 14.3 %all-to-all-start.1 = ((f32[8,16,128]{2,1,0:T(8,128)}), f32[8,16,128]{2,1,0:T(8,128)S(1)}, u32[]{:S(2)}, u32[]{:S(2)}) async-start(f32[8,16,128]{2,1,0:T(8,128)} %pad_maximum_fusion), calls=%async_computation.1 | async-start | bytes 131072 | tf_op jit(solution)/shard_map/all_to_all | solution.py:270

commit v3 on v2

v3 whole, which is shorter than its diff:
```python
import functools

import jax
import jax.numpy as jnp
from jax import lax
from jax.experimental import pallas as pl
from jax.experimental.pallas import tpu as pltpu
from jax.sharding import Mesh, PartitionSpec as P

BF = jnp.bfloat16
F32 = jnp.float32
KEY = 8192
BITS = (0, 3, 2, 1)
CHUNK = 1024
DX_CHUNK = 2048
ROWS_AT_ONCE = 64
SPLIT = 3072
MIB = 1024 * 1024
WEIGHT_VMEM = 50 * MIB
OTHER_VMEM = 43 * MIB


def cuts(total, size):
    return [(a, min(size, total - a)) for a in range(0, total, size)]


def xor_permute(x, axis, size, bit):
    return lax.ppermute(x, axis, [(i, i ^ bit) for i in range(size)])


def pack_kernel(*refs):
    *parts, out_ref = refs
    n = parts[0].shape[0]
    for i, part in enumerate(parts):
        out_ref[i * n:(i + 1) * n] = part[...]


def stage_kernel(w_hbm, w_ref, sem):
    copy = pltpu.make_async_copy(w_hbm, w_ref, sem)
    copy.start()
    copy.wait()


def half_grad(first_row, rows_ref, w_ref, bias_ref, g_ref, first_scr, key_scr, even_scr, odd_scr):
    labels, width = w_ref.shape
    half = rows_ref.shape[0]
    chunks = cuts(labels, CHUNK)
    zh, x, zl, y, c = (lax.axis_index(a) for a in ("zh", "x", "zl", "y", "c"))
    offset = ((((zh * 4 + x) * 4 + zl) * 4 + y) * 2 + c) * labels

    digit = lax.broadcasted_iota(jnp.int32, (128, 128), 0)
    lane = lax.broadcasted_iota(jnp.int32, (128, 128), 1)
    same = (digit % 32) == (lane % 32)
    power = jnp.where(digit < 32, 1.0, jnp.where(digit < 64, 256.0, jnp.where(digit < 96, 65536.0, 0.0)))
    decode = jnp.where(same, power, 0.0).astype(BF)
    row = lax.broadcasted_iota(jnp.int32, (half, 128), 0).astype(F32)
    local = jnp.dot(rows_ref[:, width:width + 128], decode, preferred_element_type=F32) - offset.astype(F32)
    local = jnp.where((local >= 0.0) & (local < float(labels)), local, -1.0)
    first = jnp.max(local, axis=1, keepdims=True)
    first_scr[...] = jnp.broadcast_to(first, (half, 128))
    more = (local >= 0.0) & (local < first)
    key_scr[...] = jnp.where(more, row * float(KEY) + local, -1.0)

    buffers = (even_scr, odd_scr)
    lanes = lax.broadcasted_iota(jnp.int32, (ROWS_AT_ONCE, 128), 1).astype(F32)

    def logits(i):
        a, n = chunks[i]
        buffers[i % 2][:, 0:n] = lax.dot_general(
            rows_ref[:, 0:width], w_ref[a:a + n], (((1,), (1,)), ((), ())), preferred_element_type=F32)

    logits(0)
    for i, (a, n) in enumerate(chunks):
        if i + 1 < len(chunks):
            logits(i + 1)
        for k in range(0, n, 128):
            bias = bias_ref[a + k:a + k + 128].reshape(1, 128)
            for r in range(0, half, ROWS_AT_ONCE):
                x = buffers[i % 2][r:r + ROWS_AT_ONCE, k:k + 128] + bias
                s = pltpu.reciprocal(1.0 + jnp.exp(-x), approx=True)
                hit = (first_scr[r:r + ROWS_AT_ONCE] - float(a + k)) == lanes
                g_ref[r:r + ROWS_AT_ONCE, a + k:a + k + 128] = jnp.where(hit, s - 1.0, s).astype(BF)

    def one_hit(top):
        key = top.astype(jnp.int32)
        b = key // KEY
        l = key - b * KEY
        b16 = pl.ds(pl.multiple_of((b // 16) * 16, 16), 16)
        l128 = pl.ds(pl.multiple_of((l // 128) * 128, 128), 128)
        r = lax.broadcasted_iota(jnp.int32, (16, 128), 0)
        c = lax.broadcasted_iota(jnp.int32, (16, 128), 1)
        old = g_ref[b16, l128].astype(F32)
        g_ref[b16, l128] = jnp.where((r == b % 16) & (c == l % 128), old - 1.0, old).astype(BF)
        keys = key_scr[...]
        keys = jnp.where(keys == top, -1.0, keys)
        key_scr[...] = keys
        return jnp.max(keys)

    lax.while_loop(lambda top: top >= 0.0, one_hit, jnp.max(key_scr[...]))


def half_dx(g_ref, w_ref, dx_scr, out_ref):
    labels, width = w_ref.shape
    half = g_ref.shape[0]
    for j, (a, n) in enumerate(cuts(labels, DX_CHUNK)):
        term = jnp.dot(g_ref[:, a:a + n], w_ref[a:a + n], preferred_element_type=F32)
        if j == 0:
            dx_scr[0:half] = term
        else:
            dx_scr[0:half] += term
    dx_scr[half:half + 16] = jnp.zeros((16, width), F32)
    zl, y = lax.axis_index("zl"), lax.axis_index("y")
    low = lax.broadcasted_iota(jnp.int32, (half + 16, 128), 1) < 64
    per, block = half // 16, out_ref.shape[2]
    for to_x in range(4):
        k = (to_x // 2) * 128
        left = dx_scr[:, k:k + 128]
        right = dx_scr[:, 256 + k:256 + k + 128]
        if to_x % 2 == 0:
            both = jnp.where(low, left, pltpu.roll(right, 64, 1))
        else:
            both = jnp.where(low, pltpu.roll(left, 64, 1), right)
        for pz, jz in enumerate(BITS):
            for py, jy in enumerate(BITS):
                j = (pz * 4 + py) * per
                out_ref[to_x * 4 + (y ^ jy), zl ^ jz] = both[j:j + block].astype(out_ref.dtype)


def own_kernel(own_ref, w_ref, bias_ref, g_ref, *scratch):
    half_grad(0, own_ref, w_ref, bias_ref, g_ref, *scratch)


def other_kernel(own_ref, other_ref, g_own_ref, w_ref, bias_ref, g_hbm, theirs_ref,
                 g_scr, dx_scr, first_scr, key_scr, even_scr, odd_scr, sems):
    labels, width = w_ref.shape
    half = own_ref.shape[0]
    low, high = pl.ds(0, half), pl.ds(half, half)
    body, tail = pl.ds(0, labels), pl.ds(labels, width)
    early = [
        pltpu.make_async_copy(g_own_ref, g_hbm.at[low, body], sems.at[0]),
        pltpu.make_async_copy(own_ref.at[:, pl.ds(0, width)], g_hbm.at[low, tail], sems.at[1]),
        pltpu.make_async_copy(other_ref.at[:, pl.ds(0, width)], g_hbm.at[high, tail], sems.at[2]),
    ]
    for copy in early:
        copy.start()
    half_grad(half, other_ref, w_ref, bias_ref, g_scr, first_scr, key_scr, even_scr, odd_scr)
    late = pltpu.make_async_copy(g_scr, g_hbm.at[high, body], sems.at[3])
    late.start()
    half_dx(g_scr, w_ref, dx_scr, theirs_ref)
    for copy in early + [late]:
        copy.wait()


def own_dx_kernel(g_ref, w_ref, mine_ref, dx_scr):
    half_dx(g_ref, w_ref, dx_scr, mine_ref)


def join_kernel(mine_ref, received_ref, out_ref):
    out_ref[...] = (mine_ref[...] + received_ref[...].astype(F32)).astype(BF)


def plane_sum_kernel(parts_ref, out_ref):
    total = jnp.sum(parts_ref[...].astype(F32), axis=0)
    out_ref[0:4] = total
    out_ref[4:8] = total


def weight_kernel(begin, end, g_hbm, *refs):
    wg_hbm, bg_hbm, g_scr, f_scr, out_scr, bias_scr, g_sems, out_sems, f_sem, bias_sem = refs[-10:]
    chunks = cuts(end - begin, CHUNK)
    labels, width = wg_hbm.shape
    f_copy = pltpu.make_async_copy(g_hbm.at[:, pl.ds(labels, width)], f_scr, f_sem)
    f_copy.start()
    g_copies = [
        pltpu.make_async_copy(g_hbm.at[:, pl.ds(begin + a, n)], g_scr.at[:, pl.ds(a, n)], g_sems.at[i])
        for i, (a, n) in enumerate(chunks)
    ]
    out_copies = [
        pltpu.make_async_copy(out_scr.at[pl.ds(a, n)], wg_hbm.at[pl.ds(begin + a, n)], out_sems.at[i])
        for i, (a, n) in enumerate(chunks)
    ]
    for copy in g_copies:
        copy.start()
    f_copy.wait()
    for i, (a, n) in enumerate(chunks):
        g_copies[i].wait()
        g = g_scr[:, a:a + n]
        out_scr[a:a + n] = lax.dot_general(
            g, f_scr[...], (((0,), (0,)), ((), ())), preferred_element_type=F32).astype(BF)
        out_copies[i].start()
        bias_scr[a:a + n] = jnp.sum(g.astype(F32), axis=0)
    bias_copy = pltpu.make_async_copy(bias_scr, bg_hbm.at[pl.ds(begin, end - begin)], bias_sem)
    bias_copy.start()
    for copy in out_copies + [bias_copy]:
        copy.wait()


def local(features, weights, label_bias, pos_ids, pos_count):
    labels, width = weights.shape
    per, slots = pos_ids.shape
    half = per * 16
    rows = 2 * half
    wide = width + 4 * slots
    vmem = pl.BlockSpec(memory_space=pltpu.VMEM)
    hbm = pl.BlockSpec(memory_space=pltpu.HBM)
    n_chunks = len(cuts(labels, CHUNK))

    slot = jnp.arange(slots, dtype=jnp.int32)
    ids = jnp.where(slot[None, :] < pos_count[:, None], pos_ids, 0xFFFFFF)
    pay = jnp.pad(features, ((0, 0), (0, wide - width)))
    for k in range(3):
        at = width + k * slots
        pay = pay + jnp.pad(((ids >> (8 * k)) & 255).astype(BF), ((0, 0), (at, wide - at - slots)))
    pay = jnp.concatenate([pay] + [xor_permute(pay, "y", 4, d) for d in BITS[1:]], axis=0)
    pay, weights_then = lax.optimization_barrier((pay, weights))
    staged = pl.pallas_call(
        stage_kernel,
        out_shape=jax.ShapeDtypeStruct((labels, width), BF),
        in_specs=[hbm],
        out_specs=vmem,
        scratch_shapes=[pltpu.SemaphoreType.DMA],
        compiler_params=pltpu.CompilerParams(vmem_limit_bytes=46 * MIB),
        cost_estimate=pl.CostEstimate(flops=0, bytes_accessed=4 * labels * width, transcendentals=0),
        name="stage_weights",
    )(weights_then)
    zs = [xor_permute(pay, "zl", 4, d) for d in BITS[1:]]
    staged, *zs = lax.optimization_barrier((staged, *zs))
    own = pl.pallas_call(
        pack_kernel,
        out_shape=jax.ShapeDtypeStruct((half, wide), BF),
        in_specs=[vmem] * 4,
        out_specs=vmem,
        compiler_params=pltpu.CompilerParams(vmem_limit_bytes=4 * MIB),
        name="pack",
    )(pay, *zs)
    other = xor_permute(own, "c", 2, 1)

    half_scratch = [
        pltpu.VMEM((half, 128), F32),
        pltpu.VMEM((half, 128), F32),
        pltpu.VMEM((half, CHUNK), F32),
        pltpu.VMEM((half, CHUNK), F32),
    ]
    dx_scratch = pltpu.VMEM((half + 16, width), F32)
    blocks_of = functools.partial(jax.ShapeDtypeStruct, (16, 4, 16, 128))
    product = 2 * half * labels * width
    g_own = pl.pallas_call(
        own_kernel,
        out_shape=jax.ShapeDtypeStruct((half, labels), BF),
        in_specs=[vmem] * 3,
        out_specs=vmem,
        scratch_shapes=half_scratch,
        compiler_params=pltpu.CompilerParams(vmem_limit_bytes=16 * MIB),
        cost_estimate=pl.CostEstimate(
            flops=product, bytes_accessed=2 * labels * width, transcendentals=2 * half * labels),
        name="own_label_grad",
    )(own, staged, label_bias)
    g, theirs = pl.pallas_call(
        other_kernel,
        out_shape=(
            jax.ShapeDtypeStruct((rows, 3 * labels), BF),
            blocks_of(BF),
        ),
        in_specs=[vmem] * 5,
        out_specs=(hbm, vmem),
        scratch_shapes=[pltpu.VMEM((half, labels), BF), dx_scratch] + half_scratch + [pltpu.SemaphoreType.DMA((4,))],
        compiler_params=pltpu.CompilerParams(vmem_limit_bytes=OTHER_VMEM),
        cost_estimate=pl.CostEstimate(
            flops=2 * product, bytes_accessed=2 * labels * width, transcendentals=2 * half * labels),
        name="other_label_grad",
    )(own, other, g_own, staged, label_bias)
    received = xor_permute(theirs, "c", 2, 1)
    mine = pl.pallas_call(
        own_dx_kernel,
        out_shape=blocks_of(F32),
        in_specs=[vmem] * 2,
        out_specs=vmem,
        scratch_shapes=[dx_scratch],
        compiler_params=pltpu.CompilerParams(vmem_limit_bytes=16 * MIB),
        cost_estimate=pl.CostEstimate(flops=product, bytes_accessed=2 * labels * width, transcendentals=0),
        name="own_dx",
    )(g_own, staged)
    send = pl.pallas_call(
        join_kernel,
        out_shape=blocks_of(BF),
        in_specs=[vmem] * 2,
        out_specs=vmem,
        compiler_params=pltpu.CompilerParams(vmem_limit_bytes=16 * MIB),
        name="join",
    )(mine, received)
    send, g = lax.optimization_barrier((send, g))
    parts = lax.all_to_all(send, ("x", "y"), 0, 0)

    def weight_part(begin, end, *before):
        n = len(cuts(end - begin, CHUNK))
        return pl.pallas_call(
            functools.partial(weight_kernel, begin, end),
            out_shape=(jax.ShapeDtypeStruct((labels, width), BF), jax.ShapeDtypeStruct((labels,), F32)),
            in_specs=[hbm] * (1 + len(before)),
            out_specs=(hbm, hbm),
            input_output_aliases={1: 0, 2: 1} if before else {},
            scratch_shapes=[
                pltpu.VMEM((rows, end - begin), BF),
                pltpu.VMEM((rows, width), BF),
                pltpu.VMEM((end - begin, width), BF),
                pltpu.VMEM((end - begin,), F32),
                pltpu.SemaphoreType.DMA((n,)),
                pltpu.SemaphoreType.DMA((n,)),
                pltpu.SemaphoreType.DMA,
                pltpu.SemaphoreType.DMA,
            ],
            compiler_params=pltpu.CompilerParams(vmem_limit_bytes=WEIGHT_VMEM),
            cost_estimate=pl.CostEstimate(
                flops=2 * rows * (end - begin) * width, bytes_accessed=2 * (end - begin) * (width + rows),
                transcendentals=0),
            name="weight_grad",
        )(g, *before)

    weight_grad, bias_grad = weight_part(0, SPLIT)
    blocks = pl.pallas_call(
        plane_sum_kernel,
        out_shape=jax.ShapeDtypeStruct((8, 16, 128), F32),
        in_specs=[vmem],
        out_specs=vmem,
        compiler_params=pltpu.CompilerParams(vmem_limit_bytes=16 * MIB),
        name="plane_sum",
    )(parts)
    blocks, weight_grad, bias_grad = lax.optimization_barrier((blocks, weight_grad, bias_grad))
    weight_grad, bias_grad = weight_part(SPLIT, labels, weight_grad, bias_grad)
    blocks = lax.all_to_all(blocks, ("zh", "zl"), 0, 0)
    total = jnp.sum(blocks, axis=0)[:per]
    feature_grad = jnp.where(lax.axis_index("zh") == 0, total[:, :64], total[:, 64:]).astype(BF)
    return weight_grad, bias_grad, feature_grad


def solution(mesh):
    fine = Mesh(mesh.devices.reshape(2, 4, 4, 4, 2), ("zh", "x", "zl", "y", "c"))
    row, col = ("zh", "x"), ("zl", "y", "c")
    return jax.shard_map(
        local,
        mesh=fine,
        in_specs=(P(col, None), P(row + col, None), P(row + col), P(col, None), P(col)),
        out_specs=(P(row + col, None), P(row + col), P(col, row)),
        check_vma=False,
    )
```

time: 64.5 us -> 60.3 us (0.935)
  waiting for transfers between devices: 14.6 us -> 11.7 us
  other arithmetic: 3.74 us -> 2.28 us
    ppermute x8, waiting for transfers between devices: 8.13 us -> 5.24 us  [xor_permute(): return lax.ppermute(x, axis, [(i, i ^ bit) for i in range(size)])]
    convert_element_type x1 -> x0, other arithmetic: 0.79 us -> none  [local(): send = (mine + xor_permute(theirs, 'c', 2, 1).astype(F32)).astype(BF)]
    pallas_call x3 -> x7, Pallas kernels: 19.1 us -> 19.3 us  [the longest x2 9.24 us: weight_part(): pl.pallas_call(functools.partial(weight_kernel, begin, end), out_shape=(j...]
  transfers between devices with their start and end apart: 10 -> 10, of which waited for: 7 -> 5; matrix products, arithmetic and copies ran while one was open for 0% -> 0% of each run, Pallas kernels for 19% -> 26%
where the time goes in v3:
time: 60.3 us; the launch traced here: 59.7 us
  starting transfers between devices  23 us (38%)
  Pallas kernels  22.1 us (37%)
  waiting for transfers between devices  11.7 us (19%)
  other arithmetic  2.28 us (4%)
  between operations  0.75 us (1%)
    pallas_call x2, Pallas kernels, weight_part(): pl.pallas_call(functools.partial(weight_kernel, begin, end), out_shape=(j...  9.24 us
    ppermute x8, starting transfers between devices, xor_permute(): return lax.ppermute(x, axis, [(i, i ^ bit) for i in range(size)])  9.15 us
    all_to_all x1, starting transfers between devices, local(): parts = lax.all_to_all(send, ('x', 'y'), 0, 0)  7.66 us
    all_to_all x1, starting transfers between devices, local(): blocks = lax.all_to_all(blocks, ('zh', 'zl'), 0, 0)  6.14 us
    ppermute x8, waiting for transfers between devices, xor_permute(): return lax.ppermute(x, axis, [(i, i ^ bit) for i in range(size)])  5.24 us
    pallas_call x1, Pallas kernels, local(): pl.pallas_call(other_kernel, out_shape=(jax.ShapeDtypeStruct((rows, 3 * l...  4.99 us
    all_to_all x1, waiting for transfers between devices, local(): blocks = lax.all_to_all(blocks, ('zh', 'zl'), 0, 0)  3.87 us
    pallas_call x1, Pallas kernels, local(): pl.pallas_call(stage_kernel, out_shape=jax.ShapeDtypeStruct((labels, widt...  2.72 us
  transfers between devices with their start and end apart: 10, of which 5 were waited for; matrix products, arithmetic and copies ran while one was open for 0% of the time, Pallas kernels for 26%

profile of v3, /device:TPU:8, one launch (start us, length us, event | category | flops | bytes accessed | tf_op | source)
XLA Modules:
  0.0 59.7 jit_solution(3884209395132426634)
XLA Ops:
  0.6 0.8 %and_convert_fusion.2 = (bf16[12,32]{1,0:T(8,128)(2,1)S(1)}, bf16[12,32]{1,0:T(8,128)(2,1)S(1)}, bf16[12,32]{1,0:T(8,128)(2,1)S(1)}) fusion(s32[12,32]{1,0:T(8,128)} %param.8, s32[12]{0:T(128)} %param.9), kind=kLoop, calls=%fused_computation.6 | loop fusion | flops 4224 | bytes 3888 | tf_op jit(solution)/shard_map/convert_element_type | solution.py:213
  1.4 0.8 %pad_add_fusion = bf16[12,640]{1,0:T(8,128)(2,1)S(1)} fusion(bf16[12,32]{1,0:T(8,128)(2,1)S(1)} %get-tuple-element.39, bf16[12,32]{1,0:T(8,128)(2,1)S(1)} %get-tuple-element.38, bf16[12,32]{1,0:T(8,128)(2,1)S(1)} %get-tuple-element.37, bf16[12,512]{1,0:T(8,128)(2,1)} %param.5), kind=kLoop, calls=%fused_computation.1 | loop fusion | flops 61440 | bytes 29952 | tf_op jit(solution)/shard_map/add | solution.py:213
  2.2 1.6 %collective-permute-start = (bf16[12,640]{1,0:T(8,128)(2,1)S(1)}, bf16[12,640]{1,0:T(8,128)(2,1)S(1)}, u32[]{:S(2)}, u32[]{:S(2)}) collective-permute-start(bf16[12,640]{1,0:T(8,128)(2,1)S(1)} %pad_add_fusion), channel_id=1, source_target_pairs={{0,6},{2,4},{4,2},{6,0},{1,7},{3,5},{5,3},{7,1},{8,14},{10,12},{12... | collective-permute-start | bytes 46088 | tf_op jit(solution)/shard_map/ppermute | solution.py:28
  3.8 2.7 %collective-permute-start.1 = (bf16[12,640]{1,0:T(8,128)(2,1)S(1)}, bf16[12,640]{1,0:T(8,128)(2,1)S(1)}, u32[]{:S(2)}, u32[]{:S(2)}) collective-permute-start(bf16[12,640]{1,0:T(8,128)(2,1)S(1)} %pad_add_fusion), channel_id=1, source_target_pairs={{0,4},{2,6},{4,0},{6,2},{1,5},{3,7},{5,1},{7,3},{8,12},{10,14},{12... | collective-permute-start | bytes 46088 | tf_op jit(solution)/shard_map/ppermute | solution.py:28
  6.5 2.6 %collective-permute-done.1 = bf16[12,640]{1,0:T(8,128)(2,1)S(1)} collective-permute-done((bf16[12,640]{1,0:T(8,128)(2,1)S(1)}, bf16[12,640]{1,0:T(8,128)(2,1)S(1)}, u32[]{:S(2)}, u32[]{:S(2)}) %collective-permute-start.1) | collective-permute-done | bytes 15392 | tf_op jit(solution)/shard_map/ppermute | solution.py:28
  9.1 1.2 %collective-permute-done.2 = bf16[12,640]{1,0:T(8,128)(2,1)S(1)} collective-permute-done((bf16[12,640]{1,0:T(8,128)(2,1)S(1)}, bf16[12,640]{1,0:T(8,128)(2,1)S(1)}, u32[]{:S(2)}, u32[]{:S(2)}) %collective-permute-start.2) | collective-permute-done | bytes 15392 | tf_op jit(solution)/shard_map/ppermute | solution.py:28
  10.3 3.5 %collective-permute-start.3 = (bf16[48,640]{1,0:T(8,128)(2,1)S(1)}, bf16[48,640]{1,0:T(8,128)(2,1)S(1)}, u32[]{:S(2)}, u32[]{:S(2)}) collective-permute-start(bf16[48,640]{1,0:T(8,128)(2,1)S(1)} %pad_maximum_fusion.refs_0_), channel_id=1, source_target_pairs={{0,24},{8,16},{16,8},{24,0},{1,25},{9,17},{17,9},{25,1},{2,26},{10... | collective-permute-start | bytes 184328 | tf_op jit(solution)/shard_map/ppermute | solution.py:28
  13.8 0.9 %collective-permute-start.5 = (bf16[48,640]{1,0:T(8,128)(2,1)S(1)}, bf16[48,640]{1,0:T(8,128)(2,1)S(1)}, u32[]{:S(2)}, u32[]{:S(2)}) collective-permute-start(bf16[48,640]{1,0:T(8,128)(2,1)S(1)} %pad_maximum_fusion.refs_0_), channel_id=1, source_target_pairs={{0,8},{8,0},{16,24},{24,16},{1,9},{9,1},{17,25},{25,17},{2,10},{10... | collective-permute-start | bytes 184328 | tf_op jit(solution)/shard_map/ppermute | solution.py:28
  14.8 2.7 %stage_weights.1.w_ref = bf16[5888,512]{1,0:T(8,128)(2,1)S(1)} custom-call(bf16[5888,512]{1,0:T(8,128)(2,1)} %w_hbm), custom_call_target="tpu_custom_call" | custom-call | bytes 12058624 | tf_op jit(solution)/shard_map/stage_weights/pallas_call | solution.py:216
  17.5 1.5 %collective-permute-done.4.refs_2_ = bf16[48,640]{1,0:T(8,128)(2,1)S(1)} collective-permute-done((bf16[48,640]{1,0:T(8,128)(2,1)S(1)}, bf16[48,640]{1,0:T(8,128)(2,1)S(1)}, u32[]{:S(2)}, u32[]{:S(2)}) %collective-permute-start.4) | collective-permute-done | bytes 61472 | tf_op jit(solution)/shard_map/ppermute | solution.py:28
  19.0 0.1 collective-permute-start.6
  19.1 2.2 %own_label_grad.1.g_ref.g_own_ref = bf16[192,5888]{1,0:T(8,128)(2,1)S(1)} custom-call(bf16[192,640]{1,0:T(8,128)(2,1)S(1)} %pack.1.own_ref, bf16[5888,512]{1,0:T(8,128)(2,1)S(1)} %stage_weights.1.w_ref, f32[5888]{0:T(1024)S(1)} %copy-done), custom_call_target="tpu_custom_call" | custom-call | flops 1157627904 | bytes 6029312 | tf_op jit(solution)/shard_map/own_label_grad/pallas_call | solution.py:247
  21.3 5.0 %other_label_grad.1 = (bf16[384,17664]{1,0:T(8,128)(2,1)}, bf16[16,4,16,128]{3,2,1,0:T(8,128)(2,1)S(1)}) custom-call(bf16[192,640]{1,0:T(8,128)(2,1)S(1)} %pack.1.own_ref, bf16[192,640]{1,0:T(8,128)(2,1)S(1)} %collective-permute-done.6.other_ref, bf16[192,5888]{1,0:T(8,128)(2,1)S(1)} %own_label_grad.1.g_ref.g_own_ref, ...), custom_call_target="tpu_custom_call" | custom-call | flops 2315255808 | bytes 6029312 | tf_op jit(solution)/shard_map/other_label_grad/pallas_call | solution.py:258
  26.3 0.3 collective-permute-start.7
  26.6 1.5 %own_dx.1.mine_ref = f32[16,4,16,128]{3,2,1,0:T(8,128)S(1)} custom-call(bf16[192,5888]{1,0:T(8,128)(2,1)S(1)} %own_label_grad.1.g_ref.g_own_ref, bf16[5888,512]{1,0:T(8,128)(2,1)S(1)} %stage_weights.1.w_ref), custom_call_target="tpu_custom_call" | custom-call | flops 1157627904 | bytes 6029312 | tf_op jit(solution)/shard_map/own_dx/pallas_call | solution.py:273
  28.1 0.8 %join.1 = bf16[16,4,16,128]{3,2,1,0:T(8,128)(2,1)} custom-call(f32[16,4,16,128]{3,2,1,0:T(8,128)S(1)} %own_dx.1.mine_ref, bf16[16,4,16,128]{3,2,1,0:T(8,128)(2,1)S(1)} %collective-permute-done.7.received_ref), custom_call_target="tpu_custom_call" | custom-call | tf_op jit(solution)/shard_map/join/pallas_call | solution.py:283
  28.9 7.7 %all-to-all-start = ((bf16[16,4,16,128]{3,2,1,0:T(8,128)(2,1)}), bf16[16,4,16,128]{3,2,1,0:T(8,128)(2,1)S(1)}, u32[]{:S(2)}, u32[]{:S(2)}) async-start(bf16[16,4,16,128]{3,2,1,0:T(8,128)(2,1)} %join.1), calls=%async_computation | async-start | bytes 524288 | tf_op jit(solution)/shard_map/all_to_all | solution.py:292
  36.5 4.7 %weight_grad.2 = (bf16[5888,512]{1,0:T(8,128)(2,1)}, f32[5888]{0:T(1024)}) custom-call(bf16[384,17664]{1,0:T(8,128)(2,1)} %get-tuple-element.28.g_hbm), custom_call_target="tpu_custom_call" | custom-call | flops 1207959552 | bytes 5505024 | tf_op jit(solution)/shard_map/weight_grad/pallas_call | solution.py:296
  41.3 2.5 %all-to-all-done.parts_ref = bf16[16,4,16,128]{3,2,1,0:T(8,128)(2,1)S(1)} async-done(((bf16[16,4,16,128]{3,2,1,0:T(8,128)(2,1)}), bf16[16,4,16,128]{3,2,1,0:T(8,128)(2,1)S(1)}, u32[]{:S(2)}, u32[]{:S(2)}) %all-to-all-start) | async-done | bytes 262176 | tf_op jit(solution)/shard_map/all_to_all | solution.py:292
  43.8 0.7 %plane_sum.1 = f32[8,16,128]{2,1,0:T(8,128)} custom-call(bf16[16,4,16,128]{3,2,1,0:T(8,128)(2,1)S(1)} %all-to-all-done.parts_ref), custom_call_target="tpu_custom_call" | custom-call | tf_op jit(solution)/shard_map/plane_sum/pallas_call | solution.py:320
  44.5 6.1 %all-to-all-start.1 = ((f32[8,16,128]{2,1,0:T(8,128)}), f32[8,16,128]{2,1,0:T(8,128)S(1)}, u32[]{:S(2)}, u32[]{:S(2)}) async-start(f32[8,16,128]{2,1,0:T(8,128)} %plane_sum.1), calls=%async_computation.1 | async-start | bytes 131072 | tf_op jit(solution)/shard_map/all_to_all | solution.py:330
  50.7 4.5 %weight_grad.3 = (bf16[5888,512]{1,0:T(8,128)(2,1)}, f32[5888]{0:T(1024)}) custom-call(bf16[384,17664]{1,0:T(8,128)(2,1)} %get-tuple-element.28.g_hbm, bf16[5888,512]{1,0:T(8,128)(2,1)} %get-tuple-element.32.refs_0_, f32[5888]{0:T(1024)} %get-tuple-element.33.refs_1_), custom_call_target="tpu_custom_call", output_to_operand_aliasing={{0}: (1, {}), {1}: (2, {})} | custom-call | flops 1107296256 | bytes 5046272 | tf_op jit(solution)/shard_map/weight_grad/pallas_call | solution.py:296
  55.2 3.9 %all-to-all-done.1 = f32[8,16,128]{2,1,0:T(8,128)S(1)} async-done(((f32[8,16,128]{2,1,0:T(8,128)}), f32[8,16,128]{2,1,0:T(8,128)S(1)}, u32[]{:S(2)}, u32[]{:S(2)}) %all-to-all-start.1) | async-done | bytes 65568 | tf_op jit(solution)/shard_map/all_to_all | solution.py:330
  59.1 0.7 %fusion = bf16[12,64]{1,0:T(8,128)(2,1)} fusion(bf16[16,128]{1,0:T(8,128)(2,1)S(1)} %reduce_sum.9, pred[]{:T(512)S(6)} %eq.3), kind=kLoop, calls=%fused_computation.3 | loop fusion | flops 768 | bytes 4609 | tf_op jit(solution)/shard_map/convert_element_type | solution.py:332
  (12 shorter events, 0.1 us)
Async XLA Ops:
  2.2 4.3 %collective-permute-start = (bf16[12,640]{1,0:T(8,128)(2,1)S(1)}, bf16[12,640]{1,0:T(8,128)(2,1)S(1)}, u32[]{:S(2)}, u32[]{:S(2)}) collective-permute-start(bf16[12,640]{1,0:T(8,128)(2,1)S(1)} %pad_add_fusion), channel_id=1, source_target_pairs={{0,6},{2,4},{4,2},{6,0},{1,7},{3,5},{5,3},{7,1},{8,14},{10,12},{12... | collective-permute-start | bytes 46088 | tf_op jit(solution)/shard_map/ppermute | solution.py:28
  3.8 5.3 %collective-permute-start.1 = (bf16[12,640]{1,0:T(8,128)(2,1)S(1)}, bf16[12,640]{1,0:T(8,128)(2,1)S(1)}, u32[]{:S(2)}, u32[]{:S(2)}) collective-permute-start(bf16[12,640]{1,0:T(8,128)(2,1)S(1)} %pad_add_fusion), channel_id=1, source_target_pairs={{0,4},{2,6},{4,0},{6,2},{1,5},{3,7},{5,1},{7,3},{8,12},{10,14},{12... | collective-permute-start | bytes 46088 | tf_op jit(solution)/shard_map/ppermute | solution.py:28
  6.5 3.8 %collective-permute-start.2 = (bf16[12,640]{1,0:T(8,128)(2,1)S(1)}, bf16[12,640]{1,0:T(8,128)(2,1)S(1)}, u32[]{:S(2)}, u32[]{:S(2)}) collective-permute-start(bf16[12,640]{1,0:T(8,128)(2,1)S(1)} %pad_add_fusion), channel_id=1, source_target_pairs={{0,2},{2,0},{4,6},{6,4},{1,3},{3,1},{5,7},{7,5},{8,10},{10,8},{12,... | collective-permute-start | bytes 46088 | tf_op jit(solution)/shard_map/ppermute | solution.py:28
  10.3 8.8 %copy-start = (f32[5888]{0:T(1024)S(1)}, f32[5888]{0:T(1024)}, u32[]{:S(2)}) copy-start(f32[5888]{0:T(1024)} %bias_ref.3) | copy-start | bytes 70660
  10.3 7.2 %collective-permute-start.3 = (bf16[48,640]{1,0:T(8,128)(2,1)S(1)}, bf16[48,640]{1,0:T(8,128)(2,1)S(1)}, u32[]{:S(2)}, u32[]{:S(2)}) collective-permute-start(bf16[48,640]{1,0:T(8,128)(2,1)S(1)} %pad_maximum_fusion.refs_0_), channel_id=1, source_target_pairs={{0,24},{8,16},{16,8},{24,0},{1,25},{9,17},{17,9},{25,1},{2,26},{10... | collective-permute-start | bytes 184328 | tf_op jit(solution)/shard_map/ppermute | solution.py:28
  13.8 5.1 %collective-permute-start.4 = (bf16[48,640]{1,0:T(8,128)(2,1)S(1)}, bf16[48,640]{1,0:T(8,128)(2,1)S(1)}, u32[]{:S(2)}, u32[]{:S(2)}) collective-permute-start(bf16[48,640]{1,0:T(8,128)(2,1)S(1)} %pad_maximum_fusion.refs_0_), channel_id=1, source_target_pairs={{0,16},{8,24},{16,0},{24,8},{1,17},{9,25},{17,1},{25,9},{2,18},{10... | collective-permute-start | bytes 184328 | tf_op jit(solution)/shard_map/ppermute | solution.py:28
  13.8 5.1 %collective-permute-start.5 = (bf16[48,640]{1,0:T(8,128)(2,1)S(1)}, bf16[48,640]{1,0:T(8,128)(2,1)S(1)}, u32[]{:S(2)}, u32[]{:S(2)}) collective-permute-start(bf16[48,640]{1,0:T(8,128)(2,1)S(1)} %pad_maximum_fusion.refs_0_), channel_id=1, source_target_pairs={{0,8},{8,0},{16,24},{24,16},{1,9},{9,1},{17,25},{25,17},{2,10},{10... | collective-permute-start | bytes 184328 | tf_op jit(solution)/shard_map/ppermute | solution.py:28
  19.0 2.3 %collective-permute-start.6 = (bf16[192,640]{1,0:T(8,128)(2,1)S(1)}, bf16[192,640]{1,0:T(8,128)(2,1)S(1)}, u32[]{:S(2)}, u32[]{:S(2)}) collective-permute-start(bf16[192,640]{1,0:T(8,128)(2,1)S(1)} %pack.1.own_ref), channel_id=1, source_target_pairs={{0,1},{1,0},{2,3},{3,2},{4,5},{5,4},{6,7},{7,6},{8,9},{9,8},{10,11... | collective-permute-start | bytes 737288 | tf_op jit(solution)/shard_map/ppermute | solution.py:28
  26.3 1.8 %collective-permute-start.7 = (bf16[16,4,16,128]{3,2,1,0:T(8,128)(2,1)S(1)}, bf16[16,4,16,128]{3,2,1,0:T(8,128)(2,1)S(1)}, u32[]{:S(2)}, u32[]{:S(2)}) collective-permute-start(bf16[16,4,16,128]{3,2,1,0:T(8,128)(2,1)S(1)} %get-tuple-element.26), channel_id=1, source_target_pairs={{0,1},{1,0},{2,3},{3,2},{4,5},{5,4},{6,7},{7,6},{8,9},{9,8},{10,11... | collective-permute-start | bytes 786440 | tf_op jit(solution)/shard_map/ppermute | solution.py:28
  28.9 15.0 %all-to-all-start = ((bf16[16,4,16,128]{3,2,1,0:T(8,128)(2,1)}), bf16[16,4,16,128]{3,2,1,0:T(8,128)(2,1)S(1)}, u32[]{:S(2)}, u32[]{:S(2)}) async-start(bf16[16,4,16,128]{3,2,1,0:T(8,128)(2,1)} %join.1), calls=%async_computation | async-start | bytes 524288 | tf_op jit(solution)/shard_map/all_to_all | solution.py:292
  44.5 14.5 %all-to-all-start.1 = ((f32[8,16,128]{2,1,0:T(8,128)}), f32[8,16,128]{2,1,0:T(8,128)S(1)}, u32[]{:S(2)}, u32[]{:S(2)}) async-start(f32[8,16,128]{2,1,0:T(8,128)} %plane_sum.1), calls=%async_computation.1 | async-start | bytes 131072 | tf_op jit(solution)/shard_map/all_to_all | solution.py:330

commit v4 on v3

v4 whole, which is shorter than its diff:
```python
import functools

import jax
import jax.numpy as jnp
import numpy as np
from jax import lax
from jax.experimental import pallas as pl
from jax.experimental.pallas import tpu as pltpu
from jax.sharding import Mesh, PartitionSpec as P

BF = jnp.bfloat16
F32 = jnp.float32
KEY = 8192
BITS = (0, 3, 2, 1)
CHUNK = 1024
DX_CHUNK = 2048
ROWS_AT_ONCE = 64
MIB = 1024 * 1024
WEIGHT_VMEM = 50 * MIB
OTHER_VMEM = 38 * MIB


def cuts(total, size):
    return [(a, min(size, total - a)) for a in range(0, total, size)]


def xor_permute(x, axis, size, bit):
    return lax.ppermute(x, axis, [(i, i ^ bit) for i in range(size)])


def pack_kernel(*refs):
    *parts, out_ref = refs
    n = parts[0].shape[0]
    for i, part in enumerate(parts):
        out_ref[i * n:(i + 1) * n] = part[...]


def stage_kernel(w_hbm, w_ref, sem):
    copy = pltpu.make_async_copy(w_hbm, w_ref, sem)
    copy.start()
    copy.wait()


def half_grad(rows_ref, w_ref, bias_ref, g_ref, first_scr, key_scr, even_scr, odd_scr):
    labels, width = w_ref.shape
    half = rows_ref.shape[0]
    chunks = cuts(labels, CHUNK)
    zh, x, zl, y, c = (lax.axis_index(a) for a in ("zh", "x", "zl", "y", "c"))
    offset = ((((zh * 4 + x) * 4 + zl) * 4 + y) * 2 + c) * labels

    digit = lax.broadcasted_iota(jnp.int32, (128, 128), 0)
    lane = lax.broadcasted_iota(jnp.int32, (128, 128), 1)
    same = (digit % 32) == (lane % 32)
    power = jnp.where(digit < 32, 1.0, jnp.where(digit < 64, 256.0, jnp.where(digit < 96, 65536.0, 0.0)))
    decode = jnp.where(same, power, 0.0).astype(BF)
    row = lax.broadcasted_iota(jnp.int32, (half, 128), 0).astype(F32)
    local = jnp.dot(rows_ref[:, width:width + 128], decode, preferred_element_type=F32) - offset.astype(F32)
    local = jnp.where((local >= 0.0) & (local < float(labels)), local, -1.0)
    first = jnp.max(local, axis=1, keepdims=True)
    first_scr[...] = jnp.broadcast_to(first, (half, 128))
    more = (local >= 0.0) & (local < first)
    key_scr[...] = jnp.where(more, row * float(KEY) + local, -1.0)

    buffers = (even_scr, odd_scr)
    lanes = lax.broadcasted_iota(jnp.int32, (ROWS_AT_ONCE, 128), 1).astype(F32)

    def logits(i):
        a, n = chunks[i]
        buffers[i % 2][:, 0:n] = lax.dot_general(
            rows_ref[:, 0:width], w_ref[a:a + n], (((1,), (1,)), ((), ())), preferred_element_type=F32)

    logits(0)
    for i, (a, n) in enumerate(chunks):
        if i + 1 < len(chunks):
            logits(i + 1)
        for k in range(0, n, 128):
            bias = bias_ref[a + k:a + k + 128].reshape(1, 128)
            for r in range(0, half, ROWS_AT_ONCE):
                x = buffers[i % 2][r:r + ROWS_AT_ONCE, k:k + 128] + bias
                s = pltpu.reciprocal(1.0 + jnp.exp(-x), approx=True)
                hit = (first_scr[r:r + ROWS_AT_ONCE] - float(a + k)) == lanes
                g_ref[r:r + ROWS_AT_ONCE, a + k:a + k + 128] = jnp.where(hit, s - 1.0, s).astype(BF)

    def one_hit(top):
        key = top.astype(jnp.int32)
        b = key // KEY
        l = key - b * KEY
        b16 = pl.ds(pl.multiple_of((b // 16) * 16, 16), 16)
        l128 = pl.ds(pl.multiple_of((l // 128) * 128, 128), 128)
        r = lax.broadcasted_iota(jnp.int32, (16, 128), 0)
        c = lax.broadcasted_iota(jnp.int32, (16, 128), 1)
        old = g_ref[b16, l128].astype(F32)
        g_ref[b16, l128] = jnp.where((r == b % 16) & (c == l % 128), old - 1.0, old).astype(BF)
        keys = key_scr[...]
        keys = jnp.where(keys == top, -1.0, keys)
        key_scr[...] = keys
        return jnp.max(keys)

    lax.while_loop(lambda top: top >= 0.0, one_hit, jnp.max(key_scr[...]))


def half_dx(g_ref, w_ref, dx_scr, out_ref):
    labels, width = w_ref.shape
    half = g_ref.shape[0]
    for j, (a, n) in enumerate(cuts(labels, DX_CHUNK)):
        term = jnp.dot(g_ref[:, a:a + n], w_ref[a:a + n], preferred_element_type=F32)
        if j == 0:
            dx_scr[0:half] = term
        else:
            dx_scr[0:half] += term
    dx_scr[half:half + 16] = jnp.zeros((16, width), F32)
    zl, y = lax.axis_index("zl"), lax.axis_index("y")
    low = lax.broadcasted_iota(jnp.int32, (8, 128), 1) < 64
    per = half // 16
    for k in range(width // 128):
        here = dx_scr[:, k * 128:(k + 1) * 128]
        turned = pltpu.roll(here, 64, 1)
        for pz, jz in enumerate(BITS):
            for py, jy in enumerate(BITS):
                j = (pz * 4 + py) * per
                to_chip = (zl ^ jz) * 4 + (y ^ jy)
                m = j + per // 2
                even = jnp.where(low, here[j:j + 8], turned[m:m + 8])
                odd = jnp.where(low, turned[j:j + 8], here[m:m + 8])
                out_ref[32 * k + to_chip] = even.astype(out_ref.dtype)
                out_ref[32 * k + 16 + to_chip] = odd.astype(out_ref.dtype)


def own_kernel(own_ref, w_ref, bias_ref, g_ref, *scratch):
    half_grad(own_ref, w_ref, bias_ref, g_ref, *scratch)


def other_kernel(own_ref, other_ref, g_own_ref, w_ref, bias_ref, g_hbm, g_ref, theirs_ref, dx_scr, first_scr, key_scr, even_scr, odd_scr, sems):
    width = w_ref.shape[1]
    cols = pl.ds(0, width)
    early = [
        pltpu.make_async_copy(g_own_ref, g_hbm.at[0], sems.at[0]),
        pltpu.make_async_copy(own_ref.at[:, cols], g_hbm.at[2, :, cols], sems.at[1]),
        pltpu.make_async_copy(other_ref.at[:, cols], g_hbm.at[3, :, cols], sems.at[2]),
    ]
    for copy in early:
        copy.start()
    half_grad(other_ref, w_ref, bias_ref, g_ref, first_scr, key_scr, even_scr, odd_scr)
    half_dx(g_ref, w_ref, dx_scr, theirs_ref)
    for copy in early:
        copy.wait()


def own_dx_kernel(g_ref, w_ref, g_other_ref, _, mine_ref, g_hbm, dx_scr, sem):
    copy = pltpu.make_async_copy(g_other_ref, g_hbm.at[1], sem)
    copy.start()
    half_dx(g_ref, w_ref, dx_scr, mine_ref)
    copy.wait()


def join_kernel(mine_ref, received_ref, out_ref):
    out_ref[...] = (mine_ref[...] + received_ref[...].astype(F32)).astype(BF)


def total_kernel(parts_ref, out_ref):
    total = jnp.sum(parts_ref[...].astype(F32), axis=0)
    per, cols = out_ref.shape
    out_ref[0:per // 2] = total[0:per // 2, 0:cols].astype(BF)
    out_ref[per // 2:per] = total[0:per // 2, cols:2 * cols].astype(BF)


def weight_kernel(g_hbm, wg_hbm, bg_hbm, g_scr, f_scr, out_scr, bias_scr, g_sems, out_sems, f_sems, bias_sem):
    labels, width = wg_hbm.shape
    chunks = cuts(labels, CHUNK)
    half = g_hbm.shape[1]
    halves = [pl.ds(0, half), pl.ds(half, half)]
    f_copies = [
        pltpu.make_async_copy(g_hbm.at[2 + h, :, pl.ds(0, width)], f_scr.at[at], f_sems.at[h])
        for h, at in enumerate(halves)
    ]
    g_copies = [
        pltpu.make_async_copy(g_hbm.at[h, :, pl.ds(a, n)], g_scr.at[at, pl.ds(a, n)], g_sems.at[2 * i + h])
        for i, (a, n) in enumerate(chunks) for h, at in enumerate(halves)
    ]
    out_copies = [
        pltpu.make_async_copy(out_scr.at[pl.ds(a, n)], wg_hbm.at[pl.ds(a, n)], out_sems.at[i])
        for i, (a, n) in enumerate(chunks)
    ]
    for copy in f_copies + g_copies:
        copy.start()
    for copy in f_copies:
        copy.wait()
    for i, (a, n) in enumerate(chunks):
        g_copies[2 * i].wait()
        g_copies[2 * i + 1].wait()
        g = g_scr[:, a:a + n]
        out_scr[a:a + n] = lax.dot_general(
            g, f_scr[...], (((0,), (0,)), ((), ())), preferred_element_type=F32).astype(BF)
        out_copies[i].start()
        bias_scr[a:a + n] = jnp.sum(g.astype(F32), axis=0)
    bias_copy = pltpu.make_async_copy(bias_scr, bg_hbm, bias_sem)
    bias_copy.start()
    for copy in out_copies + [bias_copy]:
        copy.wait()


def local(features, weights, label_bias, pos_ids, pos_count):
    labels, width = weights.shape
    per, slots = pos_ids.shape
    half = per * 16
    rows = 2 * half
    wide = width + 4 * slots
    vmem = pl.BlockSpec(memory_space=pltpu.VMEM)
    hbm = pl.BlockSpec(memory_space=pltpu.HBM)
    n_chunks = len(cuts(labels, CHUNK))

    lane = np.arange(wide) - width
    slot = np.where(lane < 0, 0, lane % slots).astype(np.int32)
    shift = (8 * np.clip(lane // slots, 0, 2)).astype(np.int32)
    ids = sum(
        jnp.pad(pos_ids, ((0, 0), (width + k * slots, (3 - k) * slots))) for k in range(3))
    ids = jnp.where(slot[None, :] < pos_count[:, None], ids, 0xFFFFFF)
    digits = lax.shift_right_logical(ids, jnp.broadcast_to(shift[None, :], ids.shape)) & 255
    pay = jnp.where(
        (lane < 0)[None, :], jnp.pad(features, ((0, 0), (0, wide - width))), digits.astype(BF))
    pay = jnp.concatenate([pay] + [xor_permute(pay, "y", 4, d) for d in BITS[1:]], axis=0)
    pay, weights_then = lax.optimization_barrier((pay, weights))
    staged = pl.pallas_call(
        stage_kernel,
        out_shape=jax.ShapeDtypeStruct((labels, width), BF),
        in_specs=[hbm],
        out_specs=vmem,
        scratch_shapes=[pltpu.SemaphoreType.DMA],
        compiler_params=pltpu.CompilerParams(vmem_limit_bytes=46 * MIB),
        cost_estimate=pl.CostEstimate(flops=0, bytes_accessed=4 * labels * width, transcendentals=0),
        name="stage_weights",
    )(weights_then)
    zs = [xor_permute(pay, "zl", 4, d) for d in BITS[1:]]
    staged, *zs = lax.optimization_barrier((staged, *zs))
    own = pl.pallas_call(
        pack_kernel,
        out_shape=jax.ShapeDtypeStruct((half, wide), BF),
        in_specs=[vmem] * 4,
        out_specs=vmem,
        compiler_params=pltpu.CompilerParams(vmem_limit_bytes=4 * MIB),
        name="pack",
    )(pay, *zs)
    other = xor_permute(own, "c", 2, 1)

    half_scratch = [
        pltpu.VMEM((half, 128), F32),
        pltpu.VMEM((half, 128), F32),
        pltpu.VMEM((half, CHUNK), F32),
        pltpu.VMEM((half, CHUNK), F32),
    ]
    dx_scratch = pltpu.VMEM((half + 16, width), F32)
    blocks_of = functools.partial(jax.ShapeDtypeStruct, (128, 8, 128))
    product = 2 * half * labels * width
    g_own = pl.pallas_call(
        own_kernel,
        out_shape=jax.ShapeDtypeStruct((half, labels), BF),
        in_specs=[vmem] * 3,
        out_specs=vmem,
        scratch_shapes=half_scratch,
        compiler_params=pltpu.CompilerParams(vmem_limit_bytes=16 * MIB),
        cost_estimate=pl.CostEstimate(
            flops=product, bytes_accessed=2 * labels * width, transcendentals=2 * half * labels),
        name="own_label_grad",
    )(own, staged, label_bias)
    g, g_other, theirs = pl.pallas_call(
        other_kernel,
        out_shape=(
            jax.ShapeDtypeStruct((8, half, labels), BF),
            jax.ShapeDtypeStruct((half, labels), BF),
            blocks_of(BF),
        ),
        in_specs=[vmem] * 5,
        out_specs=(hbm, vmem, vmem),
        scratch_shapes=[dx_scratch] + half_scratch + [pltpu.SemaphoreType.DMA((3,))],
        compiler_params=pltpu.CompilerParams(vmem_limit_bytes=OTHER_VMEM),
        cost_estimate=pl.CostEstimate(
            flops=2 * product, bytes_accessed=2 * labels * width, transcendentals=2 * half * labels),
        name="other_label_grad",
    )(own, other, g_own, staged, label_bias)
    received = xor_permute(theirs, "c", 2, 1)
    mine, g = pl.pallas_call(
        own_dx_kernel,
        out_shape=(blocks_of(F32), jax.ShapeDtypeStruct(g.shape, BF)),
        in_specs=[vmem] * 3 + [hbm],
        out_specs=(vmem, hbm),
        input_output_aliases={3: 1},
        scratch_shapes=[dx_scratch, pltpu.SemaphoreType.DMA],
        compiler_params=pltpu.CompilerParams(vmem_limit_bytes=OTHER_VMEM),
        cost_estimate=pl.CostEstimate(flops=product, bytes_accessed=2 * labels * width, transcendentals=0),
        name="own_dx",
    )(g_own, staged, g_other, g)
    send = pl.pallas_call(
        join_kernel,
        out_shape=blocks_of(BF),
        in_specs=[vmem] * 2,
        out_specs=vmem,
        compiler_params=pltpu.CompilerParams(vmem_limit_bytes=16 * MIB),
        name="join",
    )(mine, received)
    send, g = lax.optimization_barrier((send, g))
    parts = lax.all_to_all(send, ("zh", "x", "zl", "y"), 0, 0)

    weight_grad, bias_grad = pl.pallas_call(
        weight_kernel,
        out_shape=(jax.ShapeDtypeStruct((labels, width), BF), jax.ShapeDtypeStruct((labels,), F32)),
        in_specs=[hbm],
        out_specs=(hbm, hbm),
        scratch_shapes=[
            pltpu.VMEM((rows, labels), BF),
            pltpu.VMEM((rows, width), BF),
            pltpu.VMEM((labels, width), BF),
            pltpu.VMEM((labels,), F32),
            pltpu.SemaphoreType.DMA((2 * n_chunks,)),
            pltpu.SemaphoreType.DMA((n_chunks,)),
            pltpu.SemaphoreType.DMA((2,)),
            pltpu.SemaphoreType.DMA,
        ],
        compiler_params=pltpu.CompilerParams(vmem_limit_bytes=WEIGHT_VMEM),
        cost_estimate=pl.CostEstimate(
            flops=2 * rows * labels * width, bytes_accessed=2 * labels * (width + rows), transcendentals=0),
        name="weight_grad",
    )(g)
    feature_grad = pl.pallas_call(
        total_kernel,
        out_shape=jax.ShapeDtypeStruct((per, 64), BF),
        in_specs=[vmem],
        out_specs=vmem,
        compiler_params=pltpu.CompilerParams(vmem_limit_bytes=16 * MIB),
        name="total",
    )(parts)
    return weight_grad, bias_grad, feature_grad


def solution(mesh):
    fine = Mesh(mesh.devices.reshape(2, 4, 4, 4, 2), ("zh", "x", "zl", "y", "c"))
    row, col = ("zh", "x"), ("zl", "y", "c")
    return jax.shard_map(
        local,
        mesh=fine,
        in_specs=(P(col, None), P(row + col, None), P(row + col), P(col, None), P(col)),
        out_specs=(P(row + col, None), P(row + col), P(col, row)),
        check_vma=False,
    )
```

time: 60.3 us -> 58.7 us (0.973)
  waiting for transfers between devices: 11.7 us -> 14.1 us
  Pallas kernels: 22.1 us -> 20.4 us
  starting transfers between devices: 23 us -> 21.5 us
  other arithmetic: 2.28 us -> 0.93 us
    ppermute x8, waiting for transfers between devices: 5.24 us -> 7.01 us  [xor_permute(): return lax.ppermute(x, axis, [(i, i ^ bit) for i in range(size)])]
    pallas_call x5 -> x4, Pallas kernels: 16.4 us -> 14.7 us  [the longest x1 7.65 us: local(): pl.pallas_call(weight_kernel, out_shape=(jax.ShapeDtypeStruct((labels, wi...]
    convert_element_type x2 -> x0, other arithmetic: 1.45 us -> none  [the longest x1 0.78 us: local(): (ids >> 8 * k & 255).astype(BF)]
    all_to_all x2 -> x1, starting transfers between devices: 13.8 us -> 12.5 us  [local(): parts = lax.all_to_all(send, ('zh', 'x', 'zl', 'y'), 0, 0)]
    select_n x0 -> x1, other arithmetic: none -> 0.91 us  [local(): jnp.where((lane < 0)[None, :], jnp.pad(features, ((0, 0), (0, wide - widt...]
    add x1 -> x0, other arithmetic: 0.8 us -> none  [local(): pay + jnp.pad((ids >> 8 * k & 255).astype(BF), ((0, 0), (at, wide - at -...]
    all_to_all x2 -> x1, waiting for transfers between devices: 6.42 us -> 7.05 us  [local(): parts = lax.all_to_all(send, ('zh', 'x', 'zl', 'y'), 0, 0)]
  transfers between devices with their start and end apart: 10 -> 9, of which waited for: 5 -> 5; matrix products, arithmetic and copies ran while one was open for 0% -> 0% of each run, Pallas kernels for 26% -> 26%
where the time goes in v4:
time: 58.7 us; the launch traced here: 57.7 us
  starting transfers between devices  21.5 us (37%)
  Pallas kernels  20.4 us (35%)
  waiting for transfers between devices  14.1 us (24%)
  other arithmetic  0.93 us (2%)
  between operations  0.75 us (1%)
    all_to_all x1, starting transfers between devices, local(): parts = lax.all_to_all(send, ('zh', 'x', 'zl', 'y'), 0, 0)  12.5 us
    ppermute x8, starting transfers between devices, xor_permute(): return lax.ppermute(x, axis, [(i, i ^ bit) for i in range(size)])  8.99 us
    pallas_call x1, Pallas kernels, local(): pl.pallas_call(weight_kernel, out_shape=(jax.ShapeDtypeStruct((labels, wi...  7.65 us
    all_to_all x1, waiting for transfers between devices, local(): parts = lax.all_to_all(send, ('zh', 'x', 'zl', 'y'), 0, 0)  7.05 us
    ppermute x8, waiting for transfers between devices, xor_permute(): return lax.ppermute(x, axis, [(i, i ^ bit) for i in range(size)])  7.01 us
    pallas_call x1, Pallas kernels, local(): pl.pallas_call(other_kernel, out_shape=(jax.ShapeDtypeStruct((8, half, la...  3.72 us
    pallas_call x1, Pallas kernels, local(): pl.pallas_call(stage_kernel, out_shape=jax.ShapeDtypeStruct((labels, widt...  2.72 us
    pallas_call x1, Pallas kernels, local(): pl.pallas_call(own_dx_kernel, out_shape=(blocks_of(F32), jax.ShapeDtypeSt...  2.54 us
  transfers between devices with their start and end apart: 9, of which 5 were waited for; matrix products, arithmetic and copies ran while one was open for 0% of the time, Pallas kernels for 26%

profile of v4, /device:TPU:8, one launch (start us, length us, event | category | flops | bytes accessed | tf_op | source)
XLA Modules:
  0.0 57.7 jit_solution(17187297008049350400)
XLA Ops:
  0.6 0.9 %fusion = bf16[12,640]{1,0:T(8,128)(2,1)S(1)} fusion(s32[12,32]{1,0:T(8,128)} %param.11, s32[640]{0:T(1024)} %constant.30, s32[640]{0:T(1024)} %constant.29, bf16[12,512]{1,0:T(8,128)(2,1)} %param.8, s32[12]{0:T(128)} %param.12, pred[640]{0:T(1024)(128)(4,1)} %constant.28), kind=kLoop, calls=%fused_computation.2 | loop fusion | flops 61440 | bytes 34992 | tf_op jit(solution)/shard_map/jit(_where)/select_n | solution.py:219
  1.5 2.3 %collective-permute-start.2 = (bf16[12,640]{1,0:T(8,128)(2,1)S(1)}, bf16[12,640]{1,0:T(8,128)(2,1)S(1)}, u32[]{:S(2)}, u32[]{:S(2)}) collective-permute-start(bf16[12,640]{1,0:T(8,128)(2,1)S(1)} %fusion), channel_id=1, source_target_pairs={{0,2},{2,0},{4,6},{6,4},{1,3},{3,1},{5,7},{7,5},{8,10},{10,8},{12,... | collective-permute-start | bytes 46088 | tf_op jit(solution)/shard_map/ppermute | solution.py:28
  3.8 0.9 %collective-permute-start.1 = (bf16[12,640]{1,0:T(8,128)(2,1)S(1)}, bf16[12,640]{1,0:T(8,128)(2,1)S(1)}, u32[]{:S(2)}, u32[]{:S(2)}) collective-permute-start(bf16[12,640]{1,0:T(8,128)(2,1)S(1)} %fusion), channel_id=1, source_target_pairs={{0,4},{2,6},{4,0},{6,2},{1,5},{3,7},{5,1},{7,3},{8,12},{10,14},{12... | collective-permute-start | bytes 46088 | tf_op jit(solution)/shard_map/ppermute | solution.py:28
  4.7 0.7 %collective-permute-start = (bf16[12,640]{1,0:T(8,128)(2,1)S(1)}, bf16[12,640]{1,0:T(8,128)(2,1)S(1)}, u32[]{:S(2)}, u32[]{:S(2)}) collective-permute-start(bf16[12,640]{1,0:T(8,128)(2,1)S(1)} %fusion), channel_id=1, source_target_pairs={{0,6},{2,4},{4,2},{6,0},{1,7},{3,5},{5,3},{7,1},{8,14},{10,12},{12... | collective-permute-start | bytes 46088 | tf_op jit(solution)/shard_map/ppermute | solution.py:28
  5.4 0.2 collective-permute-done.2
  5.6 3.5 %collective-permute-done.1 = bf16[12,640]{1,0:T(8,128)(2,1)S(1)} collective-permute-done((bf16[12,640]{1,0:T(8,128)(2,1)S(1)}, bf16[12,640]{1,0:T(8,128)(2,1)S(1)}, u32[]{:S(2)}, u32[]{:S(2)}) %collective-permute-start.1) | collective-permute-done | bytes 15392 | tf_op jit(solution)/shard_map/ppermute | solution.py:28
  9.1 0.0 collective-permute-done
  9.1 0.0 copy-start
  9.1 1.3 %collective-permute-start.5 = (bf16[48,640]{1,0:T(8,128)(2,1)S(1)}, bf16[48,640]{1,0:T(8,128)(2,1)S(1)}, u32[]{:S(2)}, u32[]{:S(2)}) collective-permute-start(bf16[48,640]{1,0:T(8,128)(2,1)S(1)} %pad_maximum_fusion.refs_0_), channel_id=1, source_target_pairs={{0,8},{8,0},{16,24},{24,16},{1,9},{9,1},{17,25},{25,17},{2,10},{10... | collective-permute-start | bytes 184328 | tf_op jit(solution)/shard_map/ppermute | solution.py:28
  10.5 3.3 %collective-permute-start.4 = (bf16[48,640]{1,0:T(8,128)(2,1)S(1)}, bf16[48,640]{1,0:T(8,128)(2,1)S(1)}, u32[]{:S(2)}, u32[]{:S(2)}) collective-permute-start(bf16[48,640]{1,0:T(8,128)(2,1)S(1)} %pad_maximum_fusion.refs_0_), channel_id=1, source_target_pairs={{0,16},{8,24},{16,0},{24,8},{1,17},{9,25},{17,1},{25,9},{2,18},{10... | collective-permute-start | bytes 184328 | tf_op jit(solution)/shard_map/ppermute | solution.py:28
  13.8 2.7 %stage_weights.1.w_ref = bf16[5888,512]{1,0:T(8,128)(2,1)S(1)} custom-call(bf16[5888,512]{1,0:T(8,128)(2,1)} %w_hbm), custom_call_target="tpu_custom_call" | custom-call | bytes 12058624 | tf_op jit(solution)/shard_map/stage_weights/pallas_call | solution.py:223
  16.5 0.8 %collective-permute-done.4.refs_2_ = bf16[48,640]{1,0:T(8,128)(2,1)S(1)} collective-permute-done((bf16[48,640]{1,0:T(8,128)(2,1)S(1)}, bf16[48,640]{1,0:T(8,128)(2,1)S(1)}, u32[]{:S(2)}, u32[]{:S(2)}) %collective-permute-start.4) | collective-permute-done | bytes 61472 | tf_op jit(solution)/shard_map/ppermute | solution.py:28
  17.3 2.5 %collective-permute-done.3.refs_1_ = bf16[48,640]{1,0:T(8,128)(2,1)S(1)} collective-permute-done((bf16[48,640]{1,0:T(8,128)(2,1)S(1)}, bf16[48,640]{1,0:T(8,128)(2,1)S(1)}, u32[]{:S(2)}, u32[]{:S(2)}) %collective-permute-start.3) | collective-permute-done | bytes 61472 | tf_op jit(solution)/shard_map/ppermute | solution.py:28
  19.8 0.1 collective-permute-start.6
  19.9 2.2 %own_label_grad.1.g_own_ref.g_ref = bf16[192,5888]{1,0:T(8,128)(2,1)S(1)} custom-call(bf16[192,640]{1,0:T(8,128)(2,1)S(1)} %pack.1.own_ref, bf16[5888,512]{1,0:T(8,128)(2,1)S(1)} %stage_weights.1.w_ref, f32[5888]{0:T(1024)S(1)} %copy-done), custom_call_target="tpu_custom_call" | custom-call | flops 1157627904 | bytes 6029312 | tf_op jit(solution)/shard_map/own_label_grad/pallas_call | solution.py:254
  22.1 3.7 %other_label_grad.1 = (bf16[8,192,5888]{2,1,0:T(8,128)(2,1)}, bf16[192,5888]{1,0:T(8,128)(2,1)S(1)}, bf16[128,8,128]{2,1,0:T(8,128)(2,1)S(1)}) custom-call(bf16[192,640]{1,0:T(8,128)(2,1)S(1)} %pack.1.own_ref, bf16[192,640]{1,0:T(8,128)(2,1)S(1)} %collective-permute-done.6.other_ref, bf16[192,5888]{1,0:T(8,128)(2,1)S(1)} %own_label_grad.1.g_own_ref.g_ref, ...), custom_call_target="tpu_custom_call" | custom-call | flops 2315255808 | bytes 6029312 | tf_op jit(solution)/shard_map/other_label_grad/pallas_call | solution.py:265
  25.9 0.4 collective-permute-start.7
  26.3 2.5 %own_dx.1 = (f32[128,8,128]{2,1,0:T(8,128)S(1)}, bf16[8,192,5888]{2,1,0:T(8,128)(2,1)}) custom-call(bf16[192,5888]{1,0:T(8,128)(2,1)S(1)} %own_label_grad.1.g_own_ref.g_ref, bf16[5888,512]{1,0:T(8,128)(2,1)S(1)} %stage_weights.1.w_ref, bf16[192,5888]{1,0:T(8,128)(2,1)S(1)} %get-tuple-element.24.g_other_ref, ...), custom_call_target="tpu_custom_call", output_to_operand_aliasing={{1}: (3, {})} | custom-call | flops 1157627904 | bytes 6029312 | tf_op jit(solution)/shard_map/own_dx/pallas_call | solution.py:281
  28.9 0.0 collective-permute-done.7.received_ref
  28.9 0.8 %join.1 = bf16[128,8,128]{2,1,0:T(8,128)(2,1)} custom-call(f32[128,8,128]{2,1,0:T(8,128)S(1)} %get-tuple-element.26.mine_ref, bf16[128,8,128]{2,1,0:T(8,128)(2,1)S(1)} %collective-permute-done.7.received_ref), custom_call_target="tpu_custom_call" | custom-call | tf_op jit(solution)/shard_map/join/pallas_call | solution.py:292
  29.6 12.5 %all-to-all-start = ((bf16[128,8,128]{2,1,0:T(8,128)(2,1)}), bf16[128,8,128]{2,1,0:T(8,128)(2,1)S(1)}, u32[]{:S(2)}, u32[]{:S(2)}) async-start(bf16[128,8,128]{2,1,0:T(8,128)(2,1)} %join.1), calls=%async_computation | async-start | bytes 524288 | tf_op jit(solution)/shard_map/all_to_all | solution.py:301
  42.2 7.6 %weight_grad.1 = (bf16[5888,512]{1,0:T(8,128)(2,1)}, f32[5888]{0:T(1024)}) custom-call(bf16[8,192,5888]{2,1,0:T(8,128)(2,1)} %get-tuple-element.29.g_hbm), custom_call_target="tpu_custom_call" | custom-call | flops 2315255808 | bytes 10551296 | tf_op jit(solution)/shard_map/weight_grad/pallas_call | solution.py:303
  49.8 7.1 %all-to-all-done.parts_ref = bf16[128,8,128]{2,1,0:T(8,128)(2,1)S(1)} async-done(((bf16[128,8,128]{2,1,0:T(8,128)(2,1)}), bf16[128,8,128]{2,1,0:T(8,128)(2,1)S(1)}, u32[]{:S(2)}, u32[]{:S(2)}) %all-to-all-start) | async-done | bytes 262176 | tf_op jit(solution)/shard_map/all_to_all | solution.py:301
  56.9 0.8 %total.1 = bf16[12,64]{1,0:T(8,128)(2,1)} custom-call(bf16[128,8,128]{2,1,0:T(8,128)(2,1)S(1)} %all-to-all-done.parts_ref), custom_call_target="tpu_custom_call" | custom-call | tf_op jit(solution)/shard_map/total/pallas_call | solution.py:323
  (6 shorter events, 0.1 us)
Async XLA Ops:
  1.5 4.0 %collective-permute-start.2 = (bf16[12,640]{1,0:T(8,128)(2,1)S(1)}, bf16[12,640]{1,0:T(8,128)(2,1)S(1)}, u32[]{:S(2)}, u32[]{:S(2)}) collective-permute-start(bf16[12,640]{1,0:T(8,128)(2,1)S(1)} %fusion), channel_id=1, source_target_pairs={{0,2},{2,0},{4,6},{6,4},{1,3},{3,1},{5,7},{7,5},{8,10},{10,8},{12,... | collective-permute-start | bytes 46088 | tf_op jit(solution)/shard_map/ppermute | solution.py:28
  3.8 5.3 %collective-permute-start.1 = (bf16[12,640]{1,0:T(8,128)(2,1)S(1)}, bf16[12,640]{1,0:T(8,128)(2,1)S(1)}, u32[]{:S(2)}, u32[]{:S(2)}) collective-permute-start(bf16[12,640]{1,0:T(8,128)(2,1)S(1)} %fusion), channel_id=1, source_target_pairs={{0,4},{2,6},{4,0},{6,2},{1,5},{3,7},{5,1},{7,3},{8,12},{10,14},{12... | collective-permute-start | bytes 46088 | tf_op jit(solution)/shard_map/ppermute | solution.py:28
  4.7 4.4 %collective-permute-start = (bf16[12,640]{1,0:T(8,128)(2,1)S(1)}, bf16[12,640]{1,0:T(8,128)(2,1)S(1)}, u32[]{:S(2)}, u32[]{:S(2)}) collective-permute-start(bf16[12,640]{1,0:T(8,128)(2,1)S(1)} %fusion), channel_id=1, source_target_pairs={{0,6},{2,4},{4,2},{6,0},{1,7},{3,5},{5,3},{7,1},{8,14},{10,12},{12... | collective-permute-start | bytes 46088 | tf_op jit(solution)/shard_map/ppermute | solution.py:28
  9.1 10.8 %copy-start = (f32[5888]{0:T(1024)S(1)}, f32[5888]{0:T(1024)}, u32[]{:S(2)}) copy-start(f32[5888]{0:T(1024)} %bias_ref.3) | copy-start | bytes 70660
  9.1 7.4 %collective-permute-start.5 = (bf16[48,640]{1,0:T(8,128)(2,1)S(1)}, bf16[48,640]{1,0:T(8,128)(2,1)S(1)}, u32[]{:S(2)}, u32[]{:S(2)}) collective-permute-start(bf16[48,640]{1,0:T(8,128)(2,1)S(1)} %pad_maximum_fusion.refs_0_), channel_id=1, source_target_pairs={{0,8},{8,0},{16,24},{24,16},{1,9},{9,1},{17,25},{25,17},{2,10},{10... | collective-permute-start | bytes 184328 | tf_op jit(solution)/shard_map/ppermute | solution.py:28
  10.5 6.8 %collective-permute-start.4 = (bf16[48,640]{1,0:T(8,128)(2,1)S(1)}, bf16[48,640]{1,0:T(8,128)(2,1)S(1)}, u32[]{:S(2)}, u32[]{:S(2)}) collective-permute-start(bf16[48,640]{1,0:T(8,128)(2,1)S(1)} %pad_maximum_fusion.refs_0_), channel_id=1, source_target_pairs={{0,16},{8,24},{16,0},{24,8},{1,17},{9,25},{17,1},{25,9},{2,18},{10... | collective-permute-start | bytes 184328 | tf_op jit(solution)/shard_map/ppermute | solution.py:28
  13.8 6.0 %collective-permute-start.3 = (bf16[48,640]{1,0:T(8,128)(2,1)S(1)}, bf16[48,640]{1,0:T(8,128)(2,1)S(1)}, u32[]{:S(2)}, u32[]{:S(2)}) collective-permute-start(bf16[48,640]{1,0:T(8,128)(2,1)S(1)} %pad_maximum_fusion.refs_0_), channel_id=1, source_target_pairs={{0,24},{8,16},{16,8},{24,0},{1,25},{9,17},{17,9},{25,1},{2,26},{10... | collective-permute-start | bytes 184328 | tf_op jit(solution)/shard_map/ppermute | solution.py:28
  19.8 2.3 %collective-permute-start.6 = (bf16[192,640]{1,0:T(8,128)(2,1)S(1)}, bf16[192,640]{1,0:T(8,128)(2,1)S(1)}, u32[]{:S(2)}, u32[]{:S(2)}) collective-permute-start(bf16[192,640]{1,0:T(8,128)(2,1)S(1)} %pack.1.own_ref), channel_id=1, source_target_pairs={{0,1},{1,0},{2,3},{3,2},{4,5},{5,4},{6,7},{7,6},{8,9},{9,8},{10,11... | collective-permute-start | bytes 737288 | tf_op jit(solution)/shard_map/ppermute | solution.py:28
  25.9 3.0 %collective-permute-start.7 = (bf16[128,8,128]{2,1,0:T(8,128)(2,1)S(1)}, bf16[128,8,128]{2,1,0:T(8,128)(2,1)S(1)}, u32[]{:S(2)}, u32[]{:S(2)}) collective-permute-start(bf16[128,8,128]{2,1,0:T(8,128)(2,1)S(1)} %get-tuple-element.27), channel_id=1, source_target_pairs={{0,1},{1,0},{2,3},{3,2},{4,5},{5,4},{6,7},{7,6},{8,9},{9,8},{10,11... | collective-permute-start | bytes 786440 | tf_op jit(solution)/shard_map/ppermute | solution.py:28
  29.6 27.2 %all-to-all-start = ((bf16[128,8,128]{2,1,0:T(8,128)(2,1)}), bf16[128,8,128]{2,1,0:T(8,128)(2,1)S(1)}, u32[]{:S(2)}, u32[]{:S(2)}) async-start(bf16[128,8,128]{2,1,0:T(8,128)(2,1)} %join.1), calls=%async_computation | async-start | bytes 524288 | tf_op jit(solution)/shard_map/all_to_all | solution.py:301

commit v5 on v4

--- a/solution.py
+++ b/solution.py
@@ -135,8 +135,8 @@
     cols = pl.ds(0, width)
     early = [
         pltpu.make_async_copy(g_own_ref, g_hbm.at[0], sems.at[0]),
-        pltpu.make_async_copy(own_ref.at[:, cols], g_hbm.at[2, :, cols], sems.at[1]),
-        pltpu.make_async_copy(other_ref.at[:, cols], g_hbm.at[3, :, cols], sems.at[2]),
+        pltpu.make_async_copy(own_ref.at[:, cols], g_hbm.at[1, :, cols], sems.at[1]),
+        pltpu.make_async_copy(other_ref.at[:, cols], g_hbm.at[2, :, cols], sems.at[2]),
     ]
     for copy in early:
         copy.start()
@@ -146,11 +146,8 @@
         copy.wait()
 
 
-def own_dx_kernel(g_ref, w_ref, g_other_ref, _, mine_ref, g_hbm, dx_scr, sem):
-    copy = pltpu.make_async_copy(g_other_ref, g_hbm.at[1], sem)
-    copy.start()
+def own_dx_kernel(g_ref, w_ref, mine_ref, dx_scr):
     half_dx(g_ref, w_ref, dx_scr, mine_ref)
-    copy.wait()
 
 
 def join_kernel(mine_ref, received_ref, out_ref):
@@ -160,22 +157,23 @@
 def total_kernel(parts_ref, out_ref):
     total = jnp.sum(parts_ref[...].astype(F32), axis=0)
     per, cols = out_ref.shape
-    out_ref[0:per // 2] = total[0:per // 2, 0:cols].astype(BF)
-    out_ref[per // 2:per] = total[0:per // 2, cols:2 * cols].astype(BF)
-
-
-def weight_kernel(g_hbm, wg_hbm, bg_hbm, g_scr, f_scr, out_scr, bias_scr, g_sems, out_sems, f_sems, bias_sem):
+    total = total[0:per // 2]
+    out_ref[...] = jnp.concatenate([total[:, 0:cols], total[:, cols:2 * cols]], axis=0).astype(BF)
+
+
+def weight_kernel(g_hbm, g_other_hbm, wg_hbm, bg_hbm, g_scr, f_scr, out_scr, bias_scr, g_sems, out_sems, f_sems, bias_sem):
     labels, width = wg_hbm.shape
     chunks = cuts(labels, CHUNK)
     half = g_hbm.shape[1]
     halves = [pl.ds(0, half), pl.ds(half, half)]
     f_copies = [
-        pltpu.make_async_copy(g_hbm.at[2 + h, :, pl.ds(0, width)], f_scr.at[at], f_sems.at[h])
+        pltpu.make_async_copy(g_hbm.at[1 + h, :, pl.ds(0, width)], f_scr.at[at], f_sems.at[h])
         for h, at in enumerate(halves)
     ]
     g_copies = [
-        pltpu.make_async_copy(g_hbm.at[h, :, pl.ds(a, n)], g_scr.at[at, pl.ds(a, n)], g_sems.at[2 * i + h])
-        for i, (a, n) in enumerate(chunks) for h, at in enumerate(halves)
+        pltpu.make_async_copy(from_ref.at[:, pl.ds(a, n)], g_scr.at[at, pl.ds(a, n)], g_sems.at[2 * i + h])
+        for i, (a, n) in enumerate(chunks)
+        for h, (at, from_ref) in enumerate(zip(halves, (g_hbm.at[0], g_other_hbm)))
     ]
     out_copies = [
         pltpu.make_async_copy(out_scr.at[pl.ds(a, n)], wg_hbm.at[pl.ds(a, n)], out_sems.at[i])
@@ -278,17 +276,16 @@
         name="other_label_grad",
     )(own, other, g_own, staged, label_bias)
     received = xor_permute(theirs, "c", 2, 1)
-    mine, g = pl.pallas_call(
+    mine = pl.pallas_call(
         own_dx_kernel,
-        out_shape=(blocks_of(F32), jax.ShapeDtypeStruct(g.shape, BF)),
-        in_specs=[vmem] * 3 + [hbm],
-        out_specs=(vmem, hbm),
-        input_output_aliases={3: 1},
-        scratch_shapes=[dx_scratch, pltpu.SemaphoreType.DMA],
+        out_shape=blocks_of(F32),
+        in_specs=[vmem] * 2,
+        out_specs=vmem,
+        scratch_shapes=[dx_scratch],
         compiler_params=pltpu.CompilerParams(vmem_limit_bytes=OTHER_VMEM),
         cost_estimate=pl.CostEstimate(flops=product, bytes_accessed=2 * labels * width, transcendentals=0),
         name="own_dx",
-    )(g_own, staged, g_other, g)
+    )(g_own, staged)
     send = pl.pallas_call(
         join_kernel,
         out_shape=blocks_of(BF),
@@ -297,13 +294,13 @@
         compiler_params=pltpu.CompilerParams(vmem_limit_bytes=16 * MIB),
         name="join",
     )(mine, received)
-    send, g = lax.optimization_barrier((send, g))
+    send, g, g_other = lax.optimization_barrier((send, g, g_other))
     parts = lax.all_to_all(send, ("zh", "x", "zl", "y"), 0, 0)
 
     weight_grad, bias_grad = pl.pallas_call(
         weight_kernel,
         out_shape=(jax.ShapeDtypeStruct((labels, width), BF), jax.ShapeDtypeStruct((labels,), F32)),
-        in_specs=[hbm],
+        in_specs=[hbm, hbm],
         out_specs=(hbm, hbm),
         scratch_shapes=[
             pltpu.VMEM((rows, labels), BF),
@@ -319,7 +316,7 @@
         cost_estimate=pl.CostEstimate(
             flops=2 * rows * labels * width, bytes_accessed=2 * labels * (width + rows), transcendentals=0),
         name="weight_grad",
-    )(g)
+    )(g, g_other)
     feature_grad = pl.pallas_call(
         total_kernel,
         out_shape=jax.ShapeDtypeStruct((per, 64), BF),

time: 58.7 us -> 56.3 us (0.959)
  Pallas kernels: 20.4 us -> 18.1 us
  starting transfers between devices: 21.5 us -> 22.6 us
  waiting for transfers between devices: 14.1 us -> 13 us
    ppermute x8, waiting for transfers between devices: 7.01 us -> 5.24 us  [xor_permute(): return lax.ppermute(x, axis, [(i, i ^ bit) for i in range(size)])]
    pallas_call x1, Pallas kernels: 7.65 us -> 6.58 us  [local(): pl.pallas_call(weight_kernel, out_shape=(jax.ShapeDtypeStruct((labels, wi...]
    pallas_call x1, Pallas kernels: 2.54 us -> 1.47 us  [local(): pl.pallas_call(own_dx_kernel, out_shape=blocks_of(F32), in_specs=[vmem] *...]
    all_to_all x1, waiting for transfers between devices: 7.05 us -> 7.73 us  [local(): parts = lax.all_to_all(send, ('zh', 'x', 'zl', 'y'), 0, 0)]
    all_to_all x1, starting transfers between devices: 12.5 us -> 13.1 us  [local(): parts = lax.all_to_all(send, ('zh', 'x', 'zl', 'y'), 0, 0)]
  transfers between devices with their start and end apart: 9 -> 9, of which waited for: 5 -> 4; matrix products, arithmetic and copies ran while one was open for 0% -> 0% of each run, Pallas kernels for 26% -> 23%
where the time goes in v5:
time: 56.3 us; the launch traced here: 55.4 us
  starting transfers between devices  22.6 us (40%)
  Pallas kernels  18.1 us (32%)
  waiting for transfers between devices  13 us (23%)
  other arithmetic  0.93 us (2%)
  between operations  0.75 us (1%)
    all_to_all x1, starting transfers between devices, local(): parts = lax.all_to_all(send, ('zh', 'x', 'zl', 'y'), 0, 0)  13.1 us
    ppermute x8, starting transfers between devices, xor_permute(): return lax.ppermute(x, axis, [(i, i ^ bit) for i in range(size)])  9.5 us
    all_to_all x1, waiting for transfers between devices, local(): parts = lax.all_to_all(send, ('zh', 'x', 'zl', 'y'), 0, 0)  7.73 us
    pallas_call x1, Pallas kernels, local(): pl.pallas_call(weight_kernel, out_shape=(jax.ShapeDtypeStruct((labels, wi...  6.58 us
    ppermute x8, waiting for transfers between devices, xor_permute(): return lax.ppermute(x, axis, [(i, i ^ bit) for i in range(size)])  5.24 us
    pallas_call x1, Pallas kernels, local(): pl.pallas_call(other_kernel, out_shape=(jax.ShapeDtypeStruct((8, half, la...  3.72 us
    pallas_call x1, Pallas kernels, local(): pl.pallas_call(stage_kernel, out_shape=jax.ShapeDtypeStruct((labels, widt...  2.72 us
    pallas_call x1, Pallas kernels, local(): pl.pallas_call(own_kernel, out_shape=jax.ShapeDtypeStruct((half, labels),...  2.07 us
  transfers between devices with their start and end apart: 9, of which 4 were waited for; matrix products, arithmetic and copies ran while one was open for 0% of the time, Pallas kernels for 23%

profile of v5, /device:TPU:8, one launch (start us, length us, event | category | flops | bytes accessed | tf_op | source)
XLA Modules:
  0.0 55.4 jit_solution(16327865899341853802)
XLA Ops:
  0.6 0.9 %fusion = bf16[12,640]{1,0:T(8,128)(2,1)S(1)} fusion(s32[12,32]{1,0:T(8,128)} %param.11, s32[640]{0:T(1024)} %constant.30, s32[640]{0:T(1024)} %constant.29, bf16[12,512]{1,0:T(8,128)(2,1)} %param.8, s32[12]{0:T(128)} %param.12, pred[640]{0:T(1024)(128)(4,1)} %constant.28), kind=kLoop, calls=%fused_computation.2 | loop fusion | flops 61440 | bytes 34992 | tf_op jit(solution)/shard_map/jit(_where)/select_n | solution.py:217
  1.5 1.7 %collective-permute-start = (bf16[12,640]{1,0:T(8,128)(2,1)S(1)}, bf16[12,640]{1,0:T(8,128)(2,1)S(1)}, u32[]{:S(2)}, u32[]{:S(2)}) collective-permute-start(bf16[12,640]{1,0:T(8,128)(2,1)S(1)} %fusion), channel_id=1, source_target_pairs={{0,6},{2,4},{4,2},{6,0},{1,7},{3,5},{5,3},{7,1},{8,14},{10,12},{12... | collective-permute-start | bytes 46088 | tf_op jit(solution)/shard_map/ppermute | solution.py:28
  3.2 2.7 %collective-permute-start.1 = (bf16[12,640]{1,0:T(8,128)(2,1)S(1)}, bf16[12,640]{1,0:T(8,128)(2,1)S(1)}, u32[]{:S(2)}, u32[]{:S(2)}) collective-permute-start(bf16[12,640]{1,0:T(8,128)(2,1)S(1)} %fusion), channel_id=1, source_target_pairs={{0,4},{2,6},{4,0},{6,2},{1,5},{3,7},{5,1},{7,3},{8,12},{10,14},{12... | collective-permute-start | bytes 46088 | tf_op jit(solution)/shard_map/ppermute | solution.py:28
  5.9 0.0 collective-permute-start.2
  5.9 0.0 collective-permute-done
  5.9 2.6 %collective-permute-done.1 = bf16[12,640]{1,0:T(8,128)(2,1)S(1)} collective-permute-done((bf16[12,640]{1,0:T(8,128)(2,1)S(1)}, bf16[12,640]{1,0:T(8,128)(2,1)S(1)}, u32[]{:S(2)}, u32[]{:S(2)}) %collective-permute-start.1) | collective-permute-done | bytes 15392 | tf_op jit(solution)/shard_map/ppermute | solution.py:28
  8.5 1.2 %collective-permute-done.2 = bf16[12,640]{1,0:T(8,128)(2,1)S(1)} collective-permute-done((bf16[12,640]{1,0:T(8,128)(2,1)S(1)}, bf16[12,640]{1,0:T(8,128)(2,1)S(1)}, u32[]{:S(2)}, u32[]{:S(2)}) %collective-permute-start.2) | collective-permute-done | bytes 15392 | tf_op jit(solution)/shard_map/ppermute | solution.py:28
  9.7 0.0 copy-start
  9.7 3.5 %collective-permute-start.3 = (bf16[48,640]{1,0:T(8,128)(2,1)S(1)}, bf16[48,640]{1,0:T(8,128)(2,1)S(1)}, u32[]{:S(2)}, u32[]{:S(2)}) collective-permute-start(bf16[48,640]{1,0:T(8,128)(2,1)S(1)} %pad_maximum_fusion.refs_0_), channel_id=1, source_target_pairs={{0,24},{8,16},{16,8},{24,0},{1,25},{9,17},{17,9},{25,1},{2,26},{10... | collective-permute-start | bytes 184328 | tf_op jit(solution)/shard_map/ppermute | solution.py:28
  13.3 0.9 %collective-permute-start.5 = (bf16[48,640]{1,0:T(8,128)(2,1)S(1)}, bf16[48,640]{1,0:T(8,128)(2,1)S(1)}, u32[]{:S(2)}, u32[]{:S(2)}) collective-permute-start(bf16[48,640]{1,0:T(8,128)(2,1)S(1)} %pad_maximum_fusion.refs_0_), channel_id=1, source_target_pairs={{0,8},{8,0},{16,24},{24,16},{1,9},{9,1},{17,25},{25,17},{2,10},{10... | collective-permute-start | bytes 184328 | tf_op jit(solution)/shard_map/ppermute | solution.py:28
  14.2 2.7 %stage_weights.1.w_ref = bf16[5888,512]{1,0:T(8,128)(2,1)S(1)} custom-call(bf16[5888,512]{1,0:T(8,128)(2,1)} %w_hbm), custom_call_target="tpu_custom_call" | custom-call | bytes 12058624 | tf_op jit(solution)/shard_map/stage_weights/pallas_call | solution.py:221
  16.9 1.5 %collective-permute-done.4.refs_2_ = bf16[48,640]{1,0:T(8,128)(2,1)S(1)} collective-permute-done((bf16[48,640]{1,0:T(8,128)(2,1)S(1)}, bf16[48,640]{1,0:T(8,128)(2,1)S(1)}, u32[]{:S(2)}, u32[]{:S(2)}) %collective-permute-start.4) | collective-permute-done | bytes 61472 | tf_op jit(solution)/shard_map/ppermute | solution.py:28
  18.4 0.0 collective-permute-done.5.refs_3_
  18.4 0.1 collective-permute-start.6
  18.5 2.1 %own_label_grad.1.g_ref.g_own_ref = bf16[192,5888]{1,0:T(8,128)(2,1)S(1)} custom-call(bf16[192,640]{1,0:T(8,128)(2,1)S(1)} %pack.1.own_ref, bf16[5888,512]{1,0:T(8,128)(2,1)S(1)} %stage_weights.1.w_ref, f32[5888]{0:T(1024)S(1)} %copy-done), custom_call_target="tpu_custom_call" | custom-call | flops 1157627904 | bytes 6029312 | tf_op jit(solution)/shard_map/own_label_grad/pallas_call | solution.py:252
  20.6 0.0 collective-permute-done.6.other_ref
  20.6 3.7 %other_label_grad.1 = (bf16[8,192,5888]{2,1,0:T(8,128)(2,1)}, bf16[192,5888]{1,0:T(8,128)(2,1)S(1)}, bf16[128,8,128]{2,1,0:T(8,128)(2,1)S(1)}) custom-call(bf16[192,640]{1,0:T(8,128)(2,1)S(1)} %pack.1.own_ref, bf16[192,640]{1,0:T(8,128)(2,1)S(1)} %collective-permute-done.6.other_ref, bf16[192,5888]{1,0:T(8,128)(2,1)S(1)} %own_label_grad.1.g_ref.g_own_ref, ...), custom_call_target="tpu_custom_call" | custom-call | flops 2315255808 | bytes 6029312 | tf_op jit(solution)/shard_map/other_label_grad/pallas_call | solution.py:263
  24.3 0.6 %collective-permute-start.7 = (bf16[128,8,128]{2,1,0:T(8,128)(2,1)S(1)}, bf16[128,8,128]{2,1,0:T(8,128)(2,1)S(1)}, u32[]{:S(2)}, u32[]{:S(2)}) collective-permute-start(bf16[128,8,128]{2,1,0:T(8,128)(2,1)S(1)} %get-tuple-element.23), channel_id=1, source_target_pairs={{0,1},{1,0},{2,3},{3,2},{4,5},{5,4},{6,7},{7,6},{8,9},{9,8},{10,11... | collective-permute-start | bytes 786440 | tf_op jit(solution)/shard_map/ppermute | solution.py:28
  24.9 1.5 %own_dx.1.mine_ref = f32[128,8,128]{2,1,0:T(8,128)S(1)} custom-call(bf16[192,5888]{1,0:T(8,128)(2,1)S(1)} %own_label_grad.1.g_ref.g_own_ref, bf16[5888,512]{1,0:T(8,128)(2,1)S(1)} %stage_weights.1.w_ref), custom_call_target="tpu_custom_call" | custom-call | flops 1157627904 | bytes 6029312 | tf_op jit(solution)/shard_map/own_dx/pallas_call | solution.py:279
  26.4 0.8 %join.1 = bf16[128,8,128]{2,1,0:T(8,128)(2,1)} custom-call(f32[128,8,128]{2,1,0:T(8,128)S(1)} %own_dx.1.mine_ref, bf16[128,8,128]{2,1,0:T(8,128)(2,1)S(1)} %collective-permute-done.7.received_ref), custom_call_target="tpu_custom_call" | custom-call | tf_op jit(solution)/shard_map/join/pallas_call | solution.py:289
  27.2 13.1 %all-to-all-start = ((bf16[128,8,128]{2,1,0:T(8,128)(2,1)}), bf16[128,8,128]{2,1,0:T(8,128)(2,1)S(1)}, u32[]{:S(2)}, u32[]{:S(2)}) async-start(bf16[128,8,128]{2,1,0:T(8,128)(2,1)} %join.1), calls=%async_computation | async-start | bytes 524288 | tf_op jit(solution)/shard_map/all_to_all | solution.py:298
  40.3 6.6 %weight_grad.1 = (bf16[5888,512]{1,0:T(8,128)(2,1)}, f32[5888]{0:T(1024)}) custom-call(bf16[8,192,5888]{2,1,0:T(8,128)(2,1)} %get-tuple-element.26.g_hbm, bf16[192,5888]{1,0:T(8,128)(2,1)S(1)} %get-tuple-element.27.g_other_hbm), custom_call_target="tpu_custom_call" | custom-call | flops 2315255808 | bytes 10551296 | tf_op jit(solution)/shard_map/weight_grad/pallas_call | solution.py:300
  46.9 7.7 %all-to-all-done.parts_ref = bf16[128,8,128]{2,1,0:T(8,128)(2,1)S(1)} async-done(((bf16[128,8,128]{2,1,0:T(8,128)(2,1)}), bf16[128,8,128]{2,1,0:T(8,128)(2,1)S(1)}, u32[]{:S(2)}, u32[]{:S(2)}) %all-to-all-start) | async-done | bytes 262176 | tf_op jit(solution)/shard_map/all_to_all | solution.py:298
  54.6 0.8 %total.1 = bf16[12,64]{1,0:T(8,128)(2,1)} custom-call(bf16[128,8,128]{2,1,0:T(8,128)(2,1)S(1)} %all-to-all-done.parts_ref), custom_call_target="tpu_custom_call" | custom-call | tf_op jit(solution)/shard_map/total/pallas_call | solution.py:320
  (6 shorter events, 0.1 us)
Async XLA Ops:
  1.5 4.3 %collective-permute-start = (bf16[12,640]{1,0:T(8,128)(2,1)S(1)}, bf16[12,640]{1,0:T(8,128)(2,1)S(1)}, u32[]{:S(2)}, u32[]{:S(2)}) collective-permute-start(bf16[12,640]{1,0:T(8,128)(2,1)S(1)} %fusion), channel_id=1, source_target_pairs={{0,6},{2,4},{4,2},{6,0},{1,7},{3,5},{5,3},{7,1},{8,14},{10,12},{12... | collective-permute-start | bytes 46088 | tf_op jit(solution)/shard_map/ppermute | solution.py:28
  3.2 5.3 %collective-permute-start.1 = (bf16[12,640]{1,0:T(8,128)(2,1)S(1)}, bf16[12,640]{1,0:T(8,128)(2,1)S(1)}, u32[]{:S(2)}, u32[]{:S(2)}) collective-permute-start(bf16[12,640]{1,0:T(8,128)(2,1)S(1)} %fusion), channel_id=1, source_target_pairs={{0,4},{2,6},{4,0},{6,2},{1,5},{3,7},{5,1},{7,3},{8,12},{10,14},{12... | collective-permute-start | bytes 46088 | tf_op jit(solution)/shard_map/ppermute | solution.py:28
  5.9 3.8 %collective-permute-start.2 = (bf16[12,640]{1,0:T(8,128)(2,1)S(1)}, bf16[12,640]{1,0:T(8,128)(2,1)S(1)}, u32[]{:S(2)}, u32[]{:S(2)}) collective-permute-start(bf16[12,640]{1,0:T(8,128)(2,1)S(1)} %fusion), channel_id=1, source_target_pairs={{0,2},{2,0},{4,6},{6,4},{1,3},{3,1},{5,7},{7,5},{8,10},{10,8},{12,... | collective-permute-start | bytes 46088 | tf_op jit(solution)/shard_map/ppermute | solution.py:28
  9.7 8.8 %copy-start = (f32[5888]{0:T(1024)S(1)}, f32[5888]{0:T(1024)}, u32[]{:S(2)}) copy-start(f32[5888]{0:T(1024)} %bias_ref.3) | copy-start | bytes 70660
  9.7 7.2 %collective-permute-start.3 = (bf16[48,640]{1,0:T(8,128)(2,1)S(1)}, bf16[48,640]{1,0:T(8,128)(2,1)S(1)}, u32[]{:S(2)}, u32[]{:S(2)}) collective-permute-start(bf16[48,640]{1,0:T(8,128)(2,1)S(1)} %pad_maximum_fusion.refs_0_), channel_id=1, source_target_pairs={{0,24},{8,16},{16,8},{24,0},{1,25},{9,17},{17,9},{25,1},{2,26},{10... | collective-permute-start | bytes 184328 | tf_op jit(solution)/shard_map/ppermute | solution.py:28
  13.2 5.1 %collective-permute-start.4 = (bf16[48,640]{1,0:T(8,128)(2,1)S(1)}, bf16[48,640]{1,0:T(8,128)(2,1)S(1)}, u32[]{:S(2)}, u32[]{:S(2)}) collective-permute-start(bf16[48,640]{1,0:T(8,128)(2,1)S(1)} %pad_maximum_fusion.refs_0_), channel_id=1, source_target_pairs={{0,16},{8,24},{16,0},{24,8},{1,17},{9,25},{17,1},{25,9},{2,18},{10... | collective-permute-start | bytes 184328 | tf_op jit(solution)/shard_map/ppermute | solution.py:28
  13.3 5.1 %collective-permute-start.5 = (bf16[48,640]{1,0:T(8,128)(2,1)S(1)}, bf16[48,640]{1,0:T(8,128)(2,1)S(1)}, u32[]{:S(2)}, u32[]{:S(2)}) collective-permute-start(bf16[48,640]{1,0:T(8,128)(2,1)S(1)} %pad_maximum_fusion.refs_0_), channel_id=1, source_target_pairs={{0,8},{8,0},{16,24},{24,16},{1,9},{9,1},{17,25},{25,17},{2,10},{10... | collective-permute-start | bytes 184328 | tf_op jit(solution)/shard_map/ppermute | solution.py:28
  18.4 2.2 %collective-permute-start.6 = (bf16[192,640]{1,0:T(8,128)(2,1)S(1)}, bf16[192,640]{1,0:T(8,128)(2,1)S(1)}, u32[]{:S(2)}, u32[]{:S(2)}) collective-permute-start(bf16[192,640]{1,0:T(8,128)(2,1)S(1)} %pack.1.own_ref), channel_id=1, source_target_pairs={{0,1},{1,0},{2,3},{3,2},{4,5},{5,4},{6,7},{7,6},{8,9},{9,8},{10,11... | collective-permute-start | bytes 737288 | tf_op jit(solution)/shard_map/ppermute | solution.py:28
  24.3 2.1 %collective-permute-start.7 = (bf16[128,8,128]{2,1,0:T(8,128)(2,1)S(1)}, bf16[128,8,128]{2,1,0:T(8,128)(2,1)S(1)}, u32[]{:S(2)}, u32[]{:S(2)}) collective-permute-start(bf16[128,8,128]{2,1,0:T(8,128)(2,1)S(1)} %get-tuple-element.23), channel_id=1, source_target_pairs={{0,1},{1,0},{2,3},{3,2},{4,5},{5,4},{6,7},{7,6},{8,9},{9,8},{10,11... | collective-permute-start | bytes 786440 | tf_op jit(solution)/shard_map/ppermute | solution.py:28
  27.2 27.5 %all-to-all-start = ((bf16[128,8,128]{2,1,0:T(8,128)(2,1)}), bf16[128,8,128]{2,1,0:T(8,128)(2,1)S(1)}, u32[]{:S(2)}, u32[]{:S(2)}) async-start(bf16[128,8,128]{2,1,0:T(8,128)(2,1)} %join.1), calls=%async_computation | async-start | bytes 524288 | tf_op jit(solution)/shard_map/all_to_all | solution.py:298

commit v6 on v5

--- a/solution.py
+++ b/solution.py
@@ -41,7 +41,7 @@
     copy.wait()
 
 
-def half_grad(rows_ref, w_ref, bias_ref, g_ref, first_scr, key_scr, even_scr, odd_scr):
+def half_grad(rows_ref, w_ref, bias_ref, g_ref, first_scr, key_scr, even_scr, odd_scr, dx_scr=None):
     labels, width = w_ref.shape
     half = rows_ref.shape[0]
     chunks = cuts(labels, CHUNK)
@@ -69,10 +69,20 @@
         buffers[i % 2][:, 0:n] = lax.dot_general(
             rows_ref[:, 0:width], w_ref[a:a + n], (((1,), (1,)), ((), ())), preferred_element_type=F32)
 
+    def add_dx(i):
+        a, n = chunks[i]
+        term = jnp.dot(g_ref[:, a:a + n], w_ref[a:a + n], preferred_element_type=F32)
+        if i == 0:
+            dx_scr[0:half] = term
+        else:
+            dx_scr[0:half] += term
+
     logits(0)
     for i, (a, n) in enumerate(chunks):
         if i + 1 < len(chunks):
             logits(i + 1)
+        if dx_scr is not None and i > 0:
+            add_dx(i - 1)
         for k in range(0, n, 128):
             bias = bias_ref[a + k:a + k + 128].reshape(1, 128)
             for r in range(0, half, ROWS_AT_ONCE):
@@ -80,6 +90,9 @@
                 s = pltpu.reciprocal(1.0 + jnp.exp(-x), approx=True)
                 hit = (first_scr[r:r + ROWS_AT_ONCE] - float(a + k)) == lanes
                 g_ref[r:r + ROWS_AT_ONCE, a + k:a + k + 128] = jnp.where(hit, s - 1.0, s).astype(BF)
+
+    if dx_scr is not None:
+        add_dx(len(chunks) - 1)
 
     def one_hit(top):
         key = top.astype(jnp.int32)
@@ -91,6 +104,11 @@
         c = lax.broadcasted_iota(jnp.int32, (16, 128), 1)
         old = g_ref[b16, l128].astype(F32)
         g_ref[b16, l128] = jnp.where((r == b % 16) & (c == l % 128), old - 1.0, old).astype(BF)
+        if dx_scr is not None:
+            l16 = pl.ds(pl.multiple_of((l // 16) * 16, 16), 16)
+            r = lax.broadcasted_iota(jnp.int32, (16, width), 0)
+            w_row = jnp.sum(jnp.where(r == l % 16, w_ref[l16].astype(F32), 0.0), axis=0, keepdims=True)
+            dx_scr[b16] -= jnp.where(r == b % 16, w_row, 0.0)
         keys = key_scr[...]
         keys = jnp.where(keys == top, -1.0, keys)
         key_scr[...] = keys
@@ -99,10 +117,10 @@
     lax.while_loop(lambda top: top >= 0.0, one_hit, jnp.max(key_scr[...]))
 
 
-def half_dx(g_ref, w_ref, dx_scr, out_ref):
+def half_dx(g_ref, w_ref, dx_scr, out_ref, with_product=True):
     labels, width = w_ref.shape
     half = g_ref.shape[0]
-    for j, (a, n) in enumerate(cuts(labels, DX_CHUNK)):
+    for j, (a, n) in enumerate(cuts(labels, DX_CHUNK) if with_product else []):
         term = jnp.dot(g_ref[:, a:a + n], w_ref[a:a + n], preferred_element_type=F32)
         if j == 0:
             dx_scr[0:half] = term
@@ -140,8 +158,8 @@
     ]
     for copy in early:
         copy.start()
-    half_grad(other_ref, w_ref, bias_ref, g_ref, first_scr, key_scr, even_scr, odd_scr)
-    half_dx(g_ref, w_ref, dx_scr, theirs_ref)
+    half_grad(other_ref, w_ref, bias_ref, g_ref, first_scr, key_scr, even_scr, odd_scr, dx_scr)
+    half_dx(g_ref, w_ref, dx_scr, theirs_ref, with_product=False)
     for copy in early:
         copy.wait()
 

time: 56.3 us -> 56.7 us (level)
  no operation moved by 1% of the time
where the time goes in v6:
time: 56.7 us; the launch traced here: 55.8 us
  starting transfers between devices  22.8 us (40%)
  Pallas kernels  17.9 us (32%)
  waiting for transfers between devices  13.4 us (24%)
  other arithmetic  0.93 us (2%)
  between operations  0.75 us (1%)
    all_to_all x1, starting transfers between devices, local(): parts = lax.all_to_all(send, ('zh', 'x', 'zl', 'y'), 0, 0)  13 us
    ppermute x8, starting transfers between devices, xor_permute(): return lax.ppermute(x, axis, [(i, i ^ bit) for i in range(size)])  9.77 us
    all_to_all x1, waiting for transfers between devices, local(): parts = lax.all_to_all(send, ('zh', 'x', 'zl', 'y'), 0, 0)  8.12 us
    pallas_call x1, Pallas kernels, local(): pl.pallas_call(weight_kernel, out_shape=(jax.ShapeDtypeStruct((labels, wi...  6.57 us
    ppermute x8, waiting for transfers between devices, xor_permute(): return lax.ppermute(x, axis, [(i, i ^ bit) for i in range(size)])  5.24 us
    pallas_call x1, Pallas kernels, local(): pl.pallas_call(other_kernel, out_shape=(jax.ShapeDtypeStruct((8, half, la...  3.54 us
    pallas_call x1, Pallas kernels, local(): pl.pallas_call(stage_kernel, out_shape=jax.ShapeDtypeStruct((labels, widt...  2.72 us
    pallas_call x1, Pallas kernels, local(): pl.pallas_call(own_kernel, out_shape=jax.ShapeDtypeStruct((half, labels),...  2.07 us
  transfers between devices with their start and end apart: 9, of which 4 were waited for; matrix products, arithmetic and copies ran while one was open for 0% of the time, Pallas kernels for 23%

profile of v6, /device:TPU:8, one launch (start us, length us, event | category | flops | bytes accessed | tf_op | source)
XLA Modules:
  0.0 55.8 jit_solution(17415809039115892857)
XLA Ops:
  0.6 0.9 %fusion = bf16[12,640]{1,0:T(8,128)(2,1)S(1)} fusion(s32[12,32]{1,0:T(8,128)} %param.11, s32[640]{0:T(1024)} %constant.30, s32[640]{0:T(1024)} %constant.29, bf16[12,512]{1,0:T(8,128)(2,1)} %param.8, s32[12]{0:T(128)} %param.12, pred[640]{0:T(1024)(128)(4,1)} %constant.28), kind=kLoop, calls=%fused_computation.2 | loop fusion | flops 61440 | bytes 34992 | tf_op jit(solution)/shard_map/jit(_where)/select_n | solution.py:235
  1.5 1.7 %collective-permute-start = (bf16[12,640]{1,0:T(8,128)(2,1)S(1)}, bf16[12,640]{1,0:T(8,128)(2,1)S(1)}, u32[]{:S(2)}, u32[]{:S(2)}) collective-permute-start(bf16[12,640]{1,0:T(8,128)(2,1)S(1)} %fusion), channel_id=1, source_target_pairs={{0,6},{2,4},{4,2},{6,0},{1,7},{3,5},{5,3},{7,1},{8,14},{10,12},{12... | collective-permute-start | bytes 46088 | tf_op jit(solution)/shard_map/ppermute | solution.py:28
  3.2 2.7 %collective-permute-start.1 = (bf16[12,640]{1,0:T(8,128)(2,1)S(1)}, bf16[12,640]{1,0:T(8,128)(2,1)S(1)}, u32[]{:S(2)}, u32[]{:S(2)}) collective-permute-start(bf16[12,640]{1,0:T(8,128)(2,1)S(1)} %fusion), channel_id=1, source_target_pairs={{0,4},{2,6},{4,0},{6,2},{1,5},{3,7},{5,1},{7,3},{8,12},{10,14},{12... | collective-permute-start | bytes 46088 | tf_op jit(solution)/shard_map/ppermute | solution.py:28
  5.9 0.0 collective-permute-start.2
  5.9 0.0 collective-permute-done
  5.9 2.6 %collective-permute-done.1 = bf16[12,640]{1,0:T(8,128)(2,1)S(1)} collective-permute-done((bf16[12,640]{1,0:T(8,128)(2,1)S(1)}, bf16[12,640]{1,0:T(8,128)(2,1)S(1)}, u32[]{:S(2)}, u32[]{:S(2)}) %collective-permute-start.1) | collective-permute-done | bytes 15392 | tf_op jit(solution)/shard_map/ppermute | solution.py:28
  8.5 1.2 %collective-permute-done.2 = bf16[12,640]{1,0:T(8,128)(2,1)S(1)} collective-permute-done((bf16[12,640]{1,0:T(8,128)(2,1)S(1)}, bf16[12,640]{1,0:T(8,128)(2,1)S(1)}, u32[]{:S(2)}, u32[]{:S(2)}) %collective-permute-start.2) | collective-permute-done | bytes 15392 | tf_op jit(solution)/shard_map/ppermute | solution.py:28
  9.7 0.0 copy-start
  9.7 3.5 %collective-permute-start.3 = (bf16[48,640]{1,0:T(8,128)(2,1)S(1)}, bf16[48,640]{1,0:T(8,128)(2,1)S(1)}, u32[]{:S(2)}, u32[]{:S(2)}) collective-permute-start(bf16[48,640]{1,0:T(8,128)(2,1)S(1)} %pad_maximum_fusion.refs_0_), channel_id=1, source_target_pairs={{0,24},{8,16},{16,8},{24,0},{1,25},{9,17},{17,9},{25,1},{2,26},{10... | collective-permute-start | bytes 184328 | tf_op jit(solution)/shard_map/ppermute | solution.py:28
  13.3 0.9 %collective-permute-start.5 = (bf16[48,640]{1,0:T(8,128)(2,1)S(1)}, bf16[48,640]{1,0:T(8,128)(2,1)S(1)}, u32[]{:S(2)}, u32[]{:S(2)}) collective-permute-start(bf16[48,640]{1,0:T(8,128)(2,1)S(1)} %pad_maximum_fusion.refs_0_), channel_id=1, source_target_pairs={{0,8},{8,0},{16,24},{24,16},{1,9},{9,1},{17,25},{25,17},{2,10},{10... | collective-permute-start | bytes 184328 | tf_op jit(solution)/shard_map/ppermute | solution.py:28
  14.2 2.7 %stage_weights.1.w_ref = bf16[5888,512]{1,0:T(8,128)(2,1)S(1)} custom-call(bf16[5888,512]{1,0:T(8,128)(2,1)} %w_hbm), custom_call_target="tpu_custom_call" | custom-call | bytes 12058624 | tf_op jit(solution)/shard_map/stage_weights/pallas_call | solution.py:239
  16.9 1.5 %collective-permute-done.4.refs_2_ = bf16[48,640]{1,0:T(8,128)(2,1)S(1)} collective-permute-done((bf16[48,640]{1,0:T(8,128)(2,1)S(1)}, bf16[48,640]{1,0:T(8,128)(2,1)S(1)}, u32[]{:S(2)}, u32[]{:S(2)}) %collective-permute-start.4) | collective-permute-done | bytes 61472 | tf_op jit(solution)/shard_map/ppermute | solution.py:28
  18.4 0.0 collective-permute-done.5.refs_3_
  18.4 0.1 collective-permute-start.6
  18.5 2.1 %own_label_grad.1.g_ref.g_own_ref = bf16[192,5888]{1,0:T(8,128)(2,1)S(1)} custom-call(bf16[192,640]{1,0:T(8,128)(2,1)S(1)} %pack.1.own_ref, bf16[5888,512]{1,0:T(8,128)(2,1)S(1)} %stage_weights.1.w_ref, f32[5888]{0:T(1024)S(1)} %copy-done), custom_call_target="tpu_custom_call" | custom-call | flops 1157627904 | bytes 6029312 | tf_op jit(solution)/shard_map/own_label_grad/pallas_call | solution.py:270
  20.6 0.0 collective-permute-done.6.other_ref
  20.6 3.5 %other_label_grad.1 = (bf16[8,192,5888]{2,1,0:T(8,128)(2,1)}, bf16[192,5888]{1,0:T(8,128)(2,1)S(1)}, bf16[128,8,128]{2,1,0:T(8,128)(2,1)S(1)}) custom-call(bf16[192,640]{1,0:T(8,128)(2,1)S(1)} %pack.1.own_ref, bf16[192,640]{1,0:T(8,128)(2,1)S(1)} %collective-permute-done.6.other_ref, bf16[192,5888]{1,0:T(8,128)(2,1)S(1)} %own_label_grad.1.g_ref.g_own_ref, ...), custom_call_target="tpu_custom_call" | custom-call | flops 2315255808 | bytes 6029312 | tf_op jit(solution)/shard_map/other_label_grad/pallas_call | solution.py:281
  24.1 0.9 %collective-permute-start.7 = (bf16[128,8,128]{2,1,0:T(8,128)(2,1)S(1)}, bf16[128,8,128]{2,1,0:T(8,128)(2,1)S(1)}, u32[]{:S(2)}, u32[]{:S(2)}) collective-permute-start(bf16[128,8,128]{2,1,0:T(8,128)(2,1)S(1)} %get-tuple-element.23), channel_id=1, source_target_pairs={{0,1},{1,0},{2,3},{3,2},{4,5},{5,4},{6,7},{7,6},{8,9},{9,8},{10,11... | collective-permute-start | bytes 786440 | tf_op jit(solution)/shard_map/ppermute | solution.py:28
  25.0 1.5 %own_dx.1.mine_ref = f32[128,8,128]{2,1,0:T(8,128)S(1)} custom-call(bf16[192,5888]{1,0:T(8,128)(2,1)S(1)} %own_label_grad.1.g_ref.g_own_ref, bf16[5888,512]{1,0:T(8,128)(2,1)S(1)} %stage_weights.1.w_ref), custom_call_target="tpu_custom_call" | custom-call | flops 1157627904 | bytes 6029312 | tf_op jit(solution)/shard_map/own_dx/pallas_call | solution.py:297
  26.5 0.8 %join.1 = bf16[128,8,128]{2,1,0:T(8,128)(2,1)} custom-call(f32[128,8,128]{2,1,0:T(8,128)S(1)} %own_dx.1.mine_ref, bf16[128,8,128]{2,1,0:T(8,128)(2,1)S(1)} %collective-permute-done.7.received_ref), custom_call_target="tpu_custom_call" | custom-call | tf_op jit(solution)/shard_map/join/pallas_call | solution.py:307
  27.2 13.0 %all-to-all-start = ((bf16[128,8,128]{2,1,0:T(8,128)(2,1)}), bf16[128,8,128]{2,1,0:T(8,128)(2,1)S(1)}, u32[]{:S(2)}, u32[]{:S(2)}) async-start(bf16[128,8,128]{2,1,0:T(8,128)(2,1)} %join.1), calls=%async_computation | async-start | bytes 524288 | tf_op jit(solution)/shard_map/all_to_all | solution.py:316
  40.2 6.6 %weight_grad.1 = (bf16[5888,512]{1,0:T(8,128)(2,1)}, f32[5888]{0:T(1024)}) custom-call(bf16[8,192,5888]{2,1,0:T(8,128)(2,1)} %get-tuple-element.26.g_hbm, bf16[192,5888]{1,0:T(8,128)(2,1)S(1)} %get-tuple-element.27.g_other_hbm), custom_call_target="tpu_custom_call" | custom-call | flops 2315255808 | bytes 10551296 | tf_op jit(solution)/shard_map/weight_grad/pallas_call | solution.py:318
  46.8 8.1 %all-to-all-done.parts_ref = bf16[128,8,128]{2,1,0:T(8,128)(2,1)S(1)} async-done(((bf16[128,8,128]{2,1,0:T(8,128)(2,1)}), bf16[128,8,128]{2,1,0:T(8,128)(2,1)S(1)}, u32[]{:S(2)}, u32[]{:S(2)}) %all-to-all-start) | async-done | bytes 262176 | tf_op jit(solution)/shard_map/all_to_all | solution.py:316
  55.0 0.8 %total.1 = bf16[12,64]{1,0:T(8,128)(2,1)} custom-call(bf16[128,8,128]{2,1,0:T(8,128)(2,1)S(1)} %all-to-all-done.parts_ref), custom_call_target="tpu_custom_call" | custom-call | tf_op jit(solution)/shard_map/total/pallas_call | solution.py:338
  (6 shorter events, 0.1 us)
Async XLA Ops:
  1.5 4.3 %collective-permute-start = (bf16[12,640]{1,0:T(8,128)(2,1)S(1)}, bf16[12,640]{1,0:T(8,128)(2,1)S(1)}, u32[]{:S(2)}, u32[]{:S(2)}) collective-permute-start(bf16[12,640]{1,0:T(8,128)(2,1)S(1)} %fusion), channel_id=1, source_target_pairs={{0,6},{2,4},{4,2},{6,0},{1,7},{3,5},{5,3},{7,1},{8,14},{10,12},{12... | collective-permute-start | bytes 46088 | tf_op jit(solution)/shard_map/ppermute | solution.py:28
  3.2 5.3 %collective-permute-start.1 = (bf16[12,640]{1,0:T(8,128)(2,1)S(1)}, bf16[12,640]{1,0:T(8,128)(2,1)S(1)}, u32[]{:S(2)}, u32[]{:S(2)}) collective-permute-start(bf16[12,640]{1,0:T(8,128)(2,1)S(1)} %fusion), channel_id=1, source_target_pairs={{0,4},{2,6},{4,0},{6,2},{1,5},{3,7},{5,1},{7,3},{8,12},{10,14},{12... | collective-permute-start | bytes 46088 | tf_op jit(solution)/shard_map/ppermute | solution.py:28
  5.9 3.8 %collective-permute-start.2 = (bf16[12,640]{1,0:T(8,128)(2,1)S(1)}, bf16[12,640]{1,0:T(8,128)(2,1)S(1)}, u32[]{:S(2)}, u32[]{:S(2)}) collective-permute-start(bf16[12,640]{1,0:T(8,128)(2,1)S(1)} %fusion), channel_id=1, source_target_pairs={{0,2},{2,0},{4,6},{6,4},{1,3},{3,1},{5,7},{7,5},{8,10},{10,8},{12,... | collective-permute-start | bytes 46088 | tf_op jit(solution)/shard_map/ppermute | solution.py:28
  9.7 8.8 %copy-start = (f32[5888]{0:T(1024)S(1)}, f32[5888]{0:T(1024)}, u32[]{:S(2)}) copy-start(f32[5888]{0:T(1024)} %bias_ref.3) | copy-start | bytes 70660
  9.7 7.2 %collective-permute-start.3 = (bf16[48,640]{1,0:T(8,128)(2,1)S(1)}, bf16[48,640]{1,0:T(8,128)(2,1)S(1)}, u32[]{:S(2)}, u32[]{:S(2)}) collective-permute-start(bf16[48,640]{1,0:T(8,128)(2,1)S(1)} %pad_maximum_fusion.refs_0_), channel_id=1, source_target_pairs={{0,24},{8,16},{16,8},{24,0},{1,25},{9,17},{17,9},{25,1},{2,26},{10... | collective-permute-start | bytes 184328 | tf_op jit(solution)/shard_map/ppermute | solution.py:28
  13.2 5.1 %collective-permute-start.4 = (bf16[48,640]{1,0:T(8,128)(2,1)S(1)}, bf16[48,640]{1,0:T(8,128)(2,1)S(1)}, u32[]{:S(2)}, u32[]{:S(2)}) collective-permute-start(bf16[48,640]{1,0:T(8,128)(2,1)S(1)} %pad_maximum_fusion.refs_0_), channel_id=1, source_target_pairs={{0,16},{8,24},{16,0},{24,8},{1,17},{9,25},{17,1},{25,9},{2,18},{10... | collective-permute-start | bytes 184328 | tf_op jit(solution)/shard_map/ppermute | solution.py:28
  13.3 5.1 %collective-permute-start.5 = (bf16[48,640]{1,0:T(8,128)(2,1)S(1)}, bf16[48,640]{1,0:T(8,128)(2,1)S(1)}, u32[]{:S(2)}, u32[]{:S(2)}) collective-permute-start(bf16[48,640]{1,0:T(8,128)(2,1)S(1)} %pad_maximum_fusion.refs_0_), channel_id=1, source_target_pairs={{0,8},{8,0},{16,24},{24,16},{1,9},{9,1},{17,25},{25,17},{2,10},{10... | collective-permute-start | bytes 184328 | tf_op jit(solution)/shard_map/ppermute | solution.py:28
  18.4 2.2 %collective-permute-start.6 = (bf16[192,640]{1,0:T(8,128)(2,1)S(1)}, bf16[192,640]{1,0:T(8,128)(2,1)S(1)}, u32[]{:S(2)}, u32[]{:S(2)}) collective-permute-start(bf16[192,640]{1,0:T(8,128)(2,1)S(1)} %pack.1.own_ref), channel_id=1, source_target_pairs={{0,1},{1,0},{2,3},{3,2},{4,5},{5,4},{6,7},{7,6},{8,9},{9,8},{10,11... | collective-permute-start | bytes 737288 | tf_op jit(solution)/shard_map/ppermute | solution.py:28
  24.1 2.3 %collective-permute-start.7 = (bf16[128,8,128]{2,1,0:T(8,128)(2,1)S(1)}, bf16[128,8,128]{2,1,0:T(8,128)(2,1)S(1)}, u32[]{:S(2)}, u32[]{:S(2)}) collective-permute-start(bf16[128,8,128]{2,1,0:T(8,128)(2,1)S(1)} %get-tuple-element.23), channel_id=1, source_target_pairs={{0,1},{1,0},{2,3},{3,2},{4,5},{5,4},{6,7},{7,6},{8,9},{9,8},{10,11... | collective-permute-start | bytes 786440 | tf_op jit(solution)/shard_map/ppermute | solution.py:28
  27.2 27.7 %all-to-all-start = ((bf16[128,8,128]{2,1,0:T(8,128)(2,1)}), bf16[128,8,128]{2,1,0:T(8,128)(2,1)S(1)}, u32[]{:S(2)}, u32[]{:S(2)}) async-start(bf16[128,8,128]{2,1,0:T(8,128)(2,1)} %join.1), calls=%async_computation | async-start | bytes 524288 | tf_op jit(solution)/shard_map/all_to_all | solution.py:316
